TPU v7x, 32 devices: a whole 2x2x4 slice. The times are simulated.
32 devices in a mesh: ctx: 8 (over y, x, core), fsdp: 4 (over z).
Axes of the slice: x: 2, y: 2, z: 4, core: 2. Of those that a mesh axis runs over, the one named last changes fastest.
Arguments:
- tokens: bfloat16 [16, 1024, 768], P('fsdp', 'ctx'), may hold values from -6 to 6
- cotangent: bfloat16 [16, 1024, 768], P('fsdp', 'ctx'), may hold values from -6 to 6
- lengths: int32 [16], P('fsdp'), may hold values from 256 to 1024, as said below
- bucket_table: int32 [2047], replicated, may hold values from 0 to 31, as said below
- gain_attn: bfloat16 [768], P('fsdp'), may hold values from 0.5 to 1.5
- w_query: bfloat16 [768, 768], P('fsdp'), may hold values from -0.109375 to 0.109375
- w_key: bfloat16 [768, 768], P('fsdp'), may hold values from -0.109375 to 0.109375
- w_value: bfloat16 [768, 768], P('fsdp'), may hold values from -0.21875 to 0.21875
- w_out: bfloat16 [768, 768], P('fsdp'), may hold values from -6 to 6
- bias_table: bfloat16 [32, 12], P('fsdp'), may hold values from -4 to 4
- gain_ffn: bfloat16 [768], P('fsdp'), may hold values from 0.5 to 1.5
- w_gate: bfloat16 [768, 3072], P('fsdp'), may hold values from -0.21875 to 0.21875
- w_up: bfloat16 [768, 3072], P('fsdp'), may hold values from -0.21875 to 0.21875
- w_ffn_out: bfloat16 [3072, 768], P('fsdp'), may hold values from -0.109375 to 0.109375
Outputs:
- out: bfloat16 [16, 1024, 768], P('fsdp', 'ctx')
- grad_tokens: float32 [16, 1024, 768], P('fsdp', 'ctx')
- grad_gain_attn: float32 [768], P('fsdp')
- grad_w_query: float32 [768, 768], P('fsdp')
- grad_w_key: float32 [768, 768], P('fsdp')
- grad_w_value: float32 [768, 768], P('fsdp')
- grad_w_out: float32 [768, 768], P('fsdp')
- grad_bias_table: float32 [32, 12], P('fsdp')
- grad_gain_ffn: float32 [768], P('fsdp')
- grad_w_gate: float32 [768, 3072], P('fsdp')
- grad_w_up: float32 [768, 3072], P('fsdp')
- grad_w_ffn_out: float32 [3072, 768], P('fsdp')
Inputs may be any that keep to these rules, and one draw needn't show every extreme that they name: `lengths`: of the 4 sequences of each index of fsdp (consecutive sequences), one has 1024 used slots and one a quarter of 1024. `bucket_table`: entry r + 1023 is the bucket of a key r slots after its query; it depends on |r| and the sign of r only, equals |r| for |r| < 32 // 4 (plus 32 // 2 where r > 0) and never falls as |r| grows.
All inputs are finite; a program needn't handle non-finite values.
Results may differ from a plain program's by a relative error of at most 0.02.
Values may be sent and summed in bfloat16 or wider, within the bound.
No kernel may reach another device: no remote copies, remote signals or barrier semaphores. Data moves between devices by JAX's collectives and lax.ppermute only.
A program may use at most 256 MiB of HBM per device.

v0:
```python
import math

import jax
import jax.numpy as jnp
from jax import lax
from jax.experimental import pallas as pl
from jax.experimental.pallas import tpu as pltpu
from jax.sharding import PartitionSpec as P

HEADS = 12
HEAD_DIM = 64
BUCKETS = 32
BLOCK = 256
TILE = 256
VMEM_BYTES = 56 * 1024 * 1024
COST = 0.5

norm_eps = 1e-06
F32 = jnp.float32
LOW = jnp.bfloat16
NN = (((1,), (0,)), ((), ()))
NT = (((1,), (1,)), ((), ()))
TN = (((0,), (0,)), ((), ()))
SMEM = pl.BlockSpec(memory_space=pltpu.SMEM)
ANY = pl.BlockSpec(memory_space=pl.ANY)


def dot(left, right, dims=NN):
    return lax.dot_general(left, right, dims, preferred_element_type=F32)


def shape_of(dims, kind):
    return jax.ShapeDtypeStruct(dims, kind)


def params(limit=VMEM_BYTES):
    return pltpu.CompilerParams(vmem_limit_bytes=limit)


def cost(flops, moved, exps=0):
    return pl.CostEstimate(
        flops=int(flops * COST), bytes_accessed=int(moved * COST), transcendentals=int(exps)
    )


def block_rows(index, rows=BLOCK):
    return pl.ds(pl.multiple_of(index * rows, rows), rows)


def rms_rows(rows_f):
    return lax.rsqrt(jnp.mean(rows_f * rows_f, axis=-1, keepdims=True) + norm_eps)


def pack_kernel(
    where_ref, gate_ref, up_ref, down_ref, out_ref, q_ref, k_ref, v_ref, small_ref,
    gate_mine_ref, up_mine_ref, x_ref, y_ref, qkv_ref, early_ref,
):
    chip, core = where_ref[0], where_ref[1]
    x_side, y_side = chip % 2, chip // 2
    wide, depth, model = gate_mine_ref.shape
    planes = gate_ref.shape[1] // model
    part = gate_ref.shape[1] // planes // 2
    slab = depth // 2
    for plane in range(planes):
        columns = pl.ds(pl.multiple_of(plane * 2 * part + core * part, 128), part)
        half, at = divmod(plane * part, model)
        gate_mine_ref[half, :, at : at + part] = gate_ref[:, columns]
        up_mine_ref[half, :, at : at + part] = up_ref[:, columns]
    quarter = part // 4
    x_rows, y_rows = block_rows(x_side, slab), block_rows(y_side, slab)
    for half in range(wide):
        at = slice(half * slab, (half + 1) * slab)
        x_ref[at, :] = gate_mine_ref[half, x_rows, :]
        y_ref[at, :] = up_mine_ref[half, y_rows, :]
    x_down = pl.ds(pl.multiple_of(core * part + x_side * quarter, quarter), quarter)
    y_down = pl.ds(pl.multiple_of(core * part + 2 * quarter + y_side * quarter, quarter), quarter)
    x_ref[wide * slab :, :] = down_ref[x_down, :]
    y_ref[wide * slab :, :] = down_ref[y_down, :]
    early_ref[slab : 2 * slab, :] = out_ref[block_rows(core, slab), :]
    early_ref[2 * slab :, :] = small_ref[...]
    width = model // 4
    for owner in range(4):

        @pl.when(chip == owner)
        def _(owner=owner):
            lanes = slice(owner * width, (owner + 1) * width)
            qkv_ref[:, :width] = q_ref[:, lanes]
            qkv_ref[:, width : 2 * width] = k_ref[:, lanes]
            qkv_ref[:, 2 * width : 3 * width] = v_ref[:, lanes]
            qkv_ref[:, 3 * width :] = jnp.zeros((depth, width), LOW)

    early_ref[:slab, :] = qkv_ref[block_rows(core, slab), :]


def pack_weights(where, gate, up, down, out, query, key, value, small):
    depth, units = gate.shape
    model = query.shape[1]
    planes = model // depth
    wide = units // 2 // model
    part = units // planes // 2
    vmem = pl.BlockSpec(memory_space=pltpu.VMEM)
    return pl.pallas_call(
        pack_kernel,
        in_specs=[SMEM] + [vmem] * 8,
        out_specs=[vmem] * 6,
        out_shape=[
            shape_of((wide, depth, model), LOW),
            shape_of((wide, depth, model), LOW),
            shape_of((wide * depth // 2 + part // 4, model), LOW),
            shape_of((wide * depth // 2 + part // 4, model), LOW),
            shape_of((depth, model), LOW),
            shape_of((depth + small.shape[0], model), LOW),
        ],
        compiler_params=params(),
        cost_estimate=cost(0, 16e6),
        name="pack_weights",
    )(where, gate, up, down, out, query, key, value, small)


def prepare_kernel(lens_ref, tok_ref, send_ref, order_ref, sorted_ref):
    batch = tok_ref.shape[0]
    lens = [lens_ref[i] for i in range(batch)]
    for mine in range(batch):
        rank = 0
        for other in range(batch):
            if other != mine:
                ahead = lens[other] > lens[mine] if other > mine else lens[other] >= lens[mine]
                rank = rank + ahead.astype(jnp.int32)
        slot = jnp.where(rank == 0, 0, jnp.where(rank == batch - 1, 1, rank + 1))
        order_ref[slot] = mine
        sorted_ref[slot] = lens[mine]
    for slot in range(batch):
        rows = tok_ref[order_ref[slot]]
        for chip in range(send_ref.shape[0]):
            send_ref[chip, slot] = rows


def prepare(lengths, tokens, chips):
    batch, rows, model = tokens.shape
    vmem = pl.BlockSpec(memory_space=pltpu.VMEM)
    return pl.pallas_call(
        prepare_kernel,
        in_specs=[SMEM, vmem],
        out_specs=[vmem, SMEM, SMEM],
        out_shape=[
            shape_of((chips, batch, rows, model), LOW),
            shape_of((batch,), jnp.int32),
            shape_of((batch,), jnp.int32),
        ],
        compiler_params=params(),
        cost_estimate=cost(0, 4e6),
        name="prepare",
    )(lengths, tokens)


def sort_rows_kernel(order_ref, lens_ref, start_ref, tok_ref, cot_ref, local_ref, dy_ref):
    slot = pl.program_id(0)
    local_ref[...] = tok_ref[0]
    grads = cot_ref[0].astype(F32)
    place_in = lax.broadcasted_iota(jnp.int32, grads.shape, 0) + start_ref[0]
    dy_ref[...] = jnp.where(place_in < lens_ref[slot], grads, 0.0).astype(LOW)


def sort_rows(order, lens, start, tokens, cotangent):
    batch, rows, model = tokens.shape
    by_order = pl.BlockSpec((1, rows, model), lambda s, order, lens, start: (order[s], 0, 0))
    in_order = pl.BlockSpec((rows, model), lambda s, order, lens, start: (s, 0))
    return pl.pallas_call(
        sort_rows_kernel,
        grid_spec=pltpu.PrefetchScalarGridSpec(
            num_scalar_prefetch=3,
            grid=(batch,),
            in_specs=[by_order, by_order],
            out_specs=[in_order, in_order],
        ),
        out_shape=[
            shape_of((batch * rows, model), LOW),
            shape_of((batch * rows, model), LOW),
        ],
        compiler_params=params(),
        cost_estimate=cost(0, 3e6),
        name="sort_rows",
    )(order, lens, start, tokens, cotangent)


def build_bias(offsets_ref, bias_ref):
    heads, _, width = bias_ref.shape
    span = offsets_ref.shape[1]
    for head in range(heads):
        line = jnp.broadcast_to(offsets_ref[head : head + 1, :], (8, span))
        for group in range(BLOCK // 8):
            turned = pltpu.roll(
                line, (group * 8 - (BLOCK - 1)) % span, 1, stride=1, stride_axis=0
            )
            bias_ref[head, group * 8 : group * 8 + 8, :] = turned[:, :width]


def fold_diagonals(bias_grad_ref, offsets_grad_ref):
    heads, _, width = bias_grad_ref.shape
    span = offsets_grad_ref.shape[1]
    for head in range(heads):
        total = jnp.zeros((8, span), F32)
        for group in range(BLOCK // 8):
            rows = bias_grad_ref[head, group * 8 : group * 8 + 8, :]
            wide = jnp.concatenate([rows, jnp.zeros((8, span - width), F32)], axis=1)
            total = total + pltpu.roll(wide, (BLOCK - 8 - group * 8) % span, 1)
        line = jnp.zeros((1, span), F32)
        for row in range(8):
            line = line + pltpu.roll(total, (7 - row) % span, 1)[row : row + 1, :]
        offsets_grad_ref[head : head + 1, :] = line


def kept_scores(scores, column, length, count):
    wide = count * BLOCK
    tail = jnp.where(column < length - (wide - BLOCK), scores[:, wide - BLOCK :], -1e30)
    if count == 1:
        return tail
    return jnp.concatenate([scores[:, : wide - BLOCK], tail], axis=1)


def token_block(tok_ref, index):
    pieces, _, rows, model = tok_ref.shape
    parts = BLOCK // rows
    return tok_ref[pl.ds(index * parts, parts), 0].reshape(BLOCK, model)


def attn_forward_first_kernel(
    lens_ref, where_ref, tok_ref, gain_ref, w0_ref, w1_ref, w2_ref, w3_ref, v1_ref, v2_ref, v3_ref, off_ref,
    ot_ref, of_ref, q_ref, k_ref, v_ref, w_ref,
    bias_ref, vm_ref,
):
    depth, model = w0_ref.shape
    width = w_ref.shape[2]
    planes, slab = model // depth, depth // 2
    core, plane = where_ref[1], where_ref[2]
    for kind in range(3):
        lanes = slice(kind * width, (kind + 1) * width)
        w_ref[kind, block_rows(plane, depth), :] = w0_ref[:, lanes]
        for back, (piece_ref, other_ref) in enumerate(
            ((w1_ref, v1_ref), (w2_ref, v2_ref), (w3_ref, v3_ref))
        ):
            owner = lax.rem(plane + planes - 1 - back, planes)
            w_ref[kind, block_rows(owner * 2 + core, slab), :] = piece_ref[:slab, lanes]
            w_ref[kind, block_rows(owner * 2 + 1 - core, slab), :] = other_ref[:slab, lanes]
    attend_slot(
        lens_ref[2 * core], tok_ref, gain_ref, w_ref, off_ref,
        ot_ref, of_ref, q_ref, k_ref, v_ref, bias_ref, vm_ref,
    )


def attn_forward_second_kernel(
    lens_ref, where_ref, tok_ref, gain_ref, w_ref, off_ref, of_in, q_in, k_in, v_in,
    ot_ref, of_ref, q_ref, k_ref, v_ref,
    bias_ref, vm_ref,
):
    attend_slot(
        lens_ref[2 * where_ref[1] + 1], tok_ref, gain_ref, w_ref, off_ref,
        ot_ref, of_ref, q_ref, k_ref, v_ref, bias_ref, vm_ref,
    )


def attend_slot(
    length, tok_ref, gain_ref, w_ref, off_ref,
    ot_ref, of_ref, q_ref, k_ref, v_ref, bias_ref, vm_ref,
):
    pieces, _, piece_rows, model = tok_ref.shape
    blocks = pieces * piece_rows // BLOCK
    width = w_ref.shape[2]
    per_chip = width // HEAD_DIM
    used = (length + BLOCK - 1) // BLOCK
    parts = BLOCK // piece_rows
    build_bias(off_ref, bias_ref)
    owner = lax.broadcasted_iota(jnp.int32, (BLOCK, width), 1) // HEAD_DIM
    column = lax.broadcasted_iota(jnp.int32, (BLOCK, BLOCK), 1)
    spare = lax.broadcasted_iota(jnp.int32, (BLOCK, HEAD_DIM), 1)
    nothing = jnp.zeros((BLOCK, width), LOW)

    def project(index, carry):
        rows = block_rows(index)
        rows_f = token_block(tok_ref, index).astype(F32)
        normed = (rows_f * rms_rows(rows_f) * gain_ref[...]).astype(LOW)
        q_ref[0, rows, :] = dot(normed, w_ref[0]).astype(LOW)
        k_ref[0, rows, :] = dot(normed, w_ref[1]).astype(LOW)
        val = dot(normed, w_ref[2]).astype(LOW)
        v_ref[0, rows, :] = val
        for head in range(per_chip):
            vm_ref[head, rows, :] = jnp.where(owner == head, val, nothing)
        return carry

    lax.fori_loop(0, used, project, 0)

    def attend(index, carry):
        rows = block_rows(index)
        query = q_ref[0, rows, :]
        start = pl.multiple_of((blocks - 1 - index) * BLOCK, BLOCK)
        for count in range(1, blocks + 1):

            @pl.when(used == count)
            def _(count=count):
                wide = count * BLOCK
                total = jnp.zeros((BLOCK, width), F32)
                sums = jnp.zeros((BLOCK, HEAD_DIM), F32)
                for head in range(per_chip):
                    mine = jnp.where(owner == head, query, nothing)
                    scores = dot(mine, k_ref[0, :wide, :], NT)
                    scores = scores + bias_ref[head, :, pl.ds(start, wide)]
                    scores = kept_scores(scores, column, length, count)
                    top = jnp.max(scores, axis=-1, keepdims=True)
                    weights = jnp.exp(scores - top)
                    row_total = jnp.sum(weights, axis=-1, keepdims=True)
                    part = dot(weights.astype(LOW), vm_ref[head, :wide, :])
                    total = total + part * (1.0 / row_total)
                    sums = jnp.where(spare == head, top + jnp.log(row_total), sums)
                of_ref[0, rows, :width] = total
                of_ref[0, rows, width:] = sums
                turned = jnp.transpose(total.astype(LOW))
                for piece in range(parts):
                    lanes = slice(piece * piece_rows, (piece + 1) * piece_rows)
                    ot_ref[index * parts + piece, 0] = turned[:, lanes]

        return carry

    lax.fori_loop(0, used, attend, 0)

    def clear(index, carry):
        ot_ref[pl.ds(index * parts, parts), 0] = jnp.zeros((parts, width, piece_rows), LOW)
        return carry

    lax.fori_loop(used, blocks, clear, 0)


def attn_forward(slot, lens, where, tokens, gain, weights, offsets, kept=()):
    pieces, slots, rows, model = tokens.shape
    width = model // 4
    per_chip = width // HEAD_DIM
    seq = pieces * rows
    by_slot = lambda i: (slot, 0, 0)
    whole = lambda array: pl.BlockSpec(array.shape, lambda i: (0,) * array.ndim)
    lane_rows = pl.BlockSpec((1, seq, width), by_slot)
    results = [
        shape_of((slots, seq, width + HEAD_DIM), F32),
        shape_of((slots, seq, width), LOW),
        shape_of((slots, seq, width), LOW),
        shape_of((slots, seq, width), LOW),
    ]
    last = [shape_of((3, model, width), LOW)] if slot == 0 else []
    return pl.pallas_call(
        attn_forward_first_kernel if slot == 0 else attn_forward_second_kernel,
        grid=(1,),
        in_specs=[
            SMEM,
            SMEM,
            pl.BlockSpec((pieces, 1, rows, model), lambda i: (0, slot, 0, 0)),
            whole(gain),
        ]
        + [whole(array) for array in weights]
        + [whole(offsets)]
        + [ANY] * len(kept),
        out_specs=[
            pl.BlockSpec((pieces, 1, width, rows), lambda i: (0, 0, 0, 0)),
            pl.BlockSpec((1, seq, width + HEAD_DIM), by_slot),
            lane_rows,
            lane_rows,
            lane_rows,
        ]
        + [whole(array) for array in last],
        out_shape=[shape_of((pieces, 1, width, rows), LOW)] + results + last,
        scratch_shapes=[
            pltpu.VMEM((per_chip, BLOCK, 2 * seq - BLOCK), F32),
            pltpu.VMEM((per_chip, seq, width), LOW),
        ],
        input_output_aliases={5 + len(weights) + i: 1 + i for i in range(len(kept))},
        compiler_params=params(),
        cost_estimate=cost(
            2 * seq * (model * 3 * width + 2 * seq * 256 * per_chip),
            seq * 2 * (model + 8 * width),
        ),
        name="attn_forward",
    )(lens, where, tokens, gain, *weights, offsets, *kept)


def attn_backward_kernel(
    lens_ref, where_ref, tok_ref, gain_ref, w_ref, off_ref, q_ref, k_ref, v_ref, of_ref, dot_ref,
    dn_ref, dw_keep_ref, dw_send_ref, dgain_ref, doff_ref,
    bias_ref, dbias_ref, km_ref, dq_ref, dkt_ref, dvt_ref, dwt_ref, dw_ref,
):
    slot = pl.program_id(0)
    pieces, _, piece_rows, model = tok_ref.shape
    blocks = pieces * piece_rows // BLOCK
    width = w_ref.shape[2]
    per_chip = width // HEAD_DIM
    core = where_ref[1]
    length = lens_ref[2 * core + slot]
    used = (length + BLOCK - 1) // BLOCK
    parts = BLOCK // piece_rows

    @pl.when(slot == 0)
    def _():
        build_bias(off_ref, bias_ref)
        dbias_ref[...] = jnp.zeros_like(dbias_ref)
        dwt_ref[...] = jnp.zeros_like(dwt_ref)
        dgain_ref[...] = jnp.zeros_like(dgain_ref)

    dkt_ref[...] = jnp.zeros_like(dkt_ref)
    dvt_ref[...] = jnp.zeros_like(dvt_ref)
    owner = lax.broadcasted_iota(jnp.int32, (BLOCK, width), 1) // HEAD_DIM
    column = lax.broadcasted_iota(jnp.int32, (BLOCK, BLOCK), 1)
    nothing = jnp.zeros((BLOCK, width), LOW)

    def split_keys(index, carry):
        rows = block_rows(index)
        key = k_ref[0, rows, :]
        for head in range(per_chip):
            km_ref[head, rows, :] = jnp.where(owner == head, key, nothing)
        return carry

    lax.fori_loop(0, used, split_keys, 0)

    def attend(index, carry):
        rows = block_rows(index)
        query = q_ref[0, rows, :]
        query_t = jnp.transpose(query)
        grad_t = jnp.concatenate(
            [dot_ref[index * parts + piece, 0] for piece in range(parts)], axis=1
        )
        grad = jnp.transpose(grad_t)
        product = grad.astype(F32) * of_ref[0, rows, :width]
        start = pl.multiple_of((blocks - 1 - index) * BLOCK, BLOCK)
        for count in range(1, blocks + 1):

            @pl.when(used == count)
            def _(count=count):
                wide = count * BLOCK
                grad_query = jnp.zeros((BLOCK, width), F32)
                for head in range(per_chip):
                    lanes = slice(head * HEAD_DIM, (head + 1) * HEAD_DIM)
                    mine = jnp.where(owner == head, query, nothing)
                    scores = dot(mine, k_ref[0, :wide, :], NT)
                    scores = scores + bias_ref[head, :, pl.ds(start, wide)]
                    scores = kept_scores(scores, column, length, count)
                    lse = of_ref[0, rows, width + head : width + head + 1]
                    probs = jnp.exp(scores - lse)
                    delta = jnp.sum(
                        jnp.where(owner == head, product, 0.0), axis=-1, keepdims=True
                    )
                    grad_mine = jnp.where(owner == head, grad, nothing)
                    grad_probs = dot(grad_mine, v_ref[0, :wide, :], NT)
                    grad_scores = probs * (grad_probs - delta)
                    dbias_ref[head, :, pl.ds(start, wide)] += grad_scores
                    grad_scores = grad_scores.astype(LOW)
                    grad_query = grad_query + dot(grad_scores, km_ref[head, :wide, :])
                    dkt_ref[lanes, :wide] += dot(query_t[lanes, :], grad_scores)
                    dvt_ref[lanes, :wide] += dot(grad_t[lanes, :], probs.astype(LOW))
                dq_ref[rows, :] = grad_query.astype(LOW)

        return carry

    lax.fori_loop(0, used, attend, 0)

    def finish(index, carry):
        rows = block_rows(index)
        grad_query = dq_ref[rows, :]
        key_t = dkt_ref[:, rows].astype(LOW)
        value_t = dvt_ref[:, rows].astype(LOW)
        rows_f = token_block(tok_ref, index).astype(F32)
        unit = rows_f * rms_rows(rows_f)
        normed = (unit * gain_ref[...]).astype(LOW)
        grad_normed = (
            dot(grad_query, w_ref[0], NT)
            + dot(jnp.transpose(key_t), w_ref[1], NT)
            + dot(jnp.transpose(value_t), w_ref[2], NT)
        )
        dgain_ref[...] += jnp.sum(grad_normed * unit, axis=0, keepdims=True)
        dn_ref[pl.ds(index * parts, parts), 0] = grad_normed.astype(LOW).reshape(
            parts, piece_rows, model
        )
        dwt_ref[0:width, :] += dot(jnp.transpose(grad_query), normed)
        dwt_ref[width : 2 * width, :] += dot(key_t, normed)
        dwt_ref[2 * width :, :] += dot(value_t, normed)
        return carry

    lax.fori_loop(0, used, finish, 0)

    def clear(index, carry):
        dn_ref[pl.ds(index * parts, parts), 0] = jnp.zeros((parts, piece_rows, model), LOW)
        return carry

    lax.fori_loop(used, blocks, clear, 0)

    @pl.when(slot == pl.num_programs(0) - 1)
    def _():
        fold_diagonals(dbias_ref, doff_ref)
        dw_ref[...] = jnp.transpose(dwt_ref[...].astype(LOW))
        planes, slab, _ = dw_keep_ref.shape
        for plane in range(planes):
            lanes = slice(0, 3 * width)
            dw_keep_ref[plane, :, lanes] = dw_ref[block_rows(2 * plane + core, slab), :]
            dw_send_ref[plane, :, lanes] = dw_ref[block_rows(2 * plane + 1 - core, slab), :]
            rest = jnp.zeros((slab, model - 3 * width), LOW)
            dw_keep_ref[plane, :, 3 * width :] = rest
            dw_send_ref[plane, :, 3 * width :] = rest


def attn_backward(
    lens, where, tokens, gain, w_qkv, offsets, query, key, value, attn_full, grad, planes
):
    pieces, slots, rows, model = tokens.shape
    width = w_qkv.shape[2]
    per_chip = width // HEAD_DIM
    seq = pieces * rows
    lane_rows = pl.BlockSpec((1, seq, width), lambda s: (s, 0, 0))
    by_slot = lambda s: (0, s, 0, 0)
    once = lambda s: (0, 0)
    return pl.pallas_call(
        attn_backward_kernel,
        grid=(slots,),
        in_specs=[
            SMEM,
            SMEM,
            pl.BlockSpec((pieces, 1, rows, model), by_slot),
            pl.BlockSpec((1, model), once),
            pl.BlockSpec((3, model, width), lambda s: (0, 0, 0)),
            pl.BlockSpec(offsets.shape, once),
            lane_rows,
            lane_rows,
            lane_rows,
            pl.BlockSpec((1, seq, width + HEAD_DIM), lambda s: (s, 0, 0)),
            pl.BlockSpec((pieces, 1, width, rows), by_slot),
        ],
        out_specs=[
            pl.BlockSpec((pieces, 1, rows, model), by_slot),
            pl.BlockSpec((planes, model // planes // 2, model), lambda s: (0, 0, 0)),
            pl.BlockSpec((planes, model // planes // 2, model), lambda s: (0, 0, 0)),
            pl.BlockSpec((1, model), once),
            pl.BlockSpec((per_chip, 2 * seq), once),
        ],
        out_shape=[
            shape_of((pieces, slots, rows, model), LOW),
            shape_of((planes, model // planes // 2, model), LOW),
            shape_of((planes, model // planes // 2, model), LOW),
            shape_of((1, model), F32),
            shape_of((per_chip, 2 * seq), F32),
        ],
        scratch_shapes=[
            pltpu.VMEM((per_chip, BLOCK, 2 * seq - BLOCK), F32),
            pltpu.VMEM((per_chip, BLOCK, 2 * seq - BLOCK), F32),
            pltpu.VMEM((per_chip, seq, width), LOW),
            pltpu.VMEM((seq, width), LOW),
            pltpu.VMEM((width, seq), F32),
            pltpu.VMEM((width, seq), F32),
            pltpu.VMEM((3 * width, model), F32),
            pltpu.VMEM((model, 3 * width), LOW),
        ],
        compiler_params=params(),
        cost_estimate=cost(
            4 * slots * seq * (model * 6 * width + 5 * seq * 256 * per_chip),
            slots * seq * 2 * (2 * model + 12 * width),
        ),
        name="attn_backward",
    )(lens, where, tokens, gain, w_qkv, offsets, query, key, value, attn_full, grad)


def side_by_side(attn_refs, chip):
    return jnp.concatenate(
        [ref[2 * chip + core, 0] for core in range(2) for ref in attn_refs], axis=1
    )


def out_project_kernel(
    where_ref, tok_ref, attn0_ref, attn1_ref, own_ref, a1_ref, a2_ref, a3_ref, b1_ref, b2_ref, b3_ref, gain_ref,
    res_ref, nf_ref, w_ref,
):
    core, plane = where_ref[1], where_ref[2]
    depth = own_ref.shape[0]
    slab = depth // 2
    planes = w_ref.shape[0] // depth
    w_ref[block_rows(plane, depth), :] = own_ref[...]
    for back, (piece_ref, other_ref) in enumerate(
        ((a1_ref, b1_ref), (a2_ref, b2_ref), (a3_ref, b3_ref))
    ):
        owner = lax.rem(plane + planes - 1 - back, planes)
        w_ref[block_rows(owner * 2 + core, slab), :] = piece_ref[slab : 2 * slab, :]
        w_ref[block_rows(owner * 2 + 1 - core, slab), :] = other_ref[slab : 2 * slab, :]
    chips, width = attn0_ref.shape[0] // 2, attn0_ref.shape[2]
    total = tok_ref[...].astype(F32)
    for chip in range(chips):
        total = total + dot(
            side_by_side((attn0_ref, attn1_ref), chip), w_ref[chip * width : (chip + 1) * width, :], TN
        )
    res_ref[...] = total
    nf_ref[...] = (total * rms_rows(total) * gain_ref[...]).astype(LOW)


def out_project(where, tokens, attn, own, pieces, others, gain):
    rows, model = tokens.shape
    vmem = pl.BlockSpec(memory_space=pltpu.VMEM)
    return pl.pallas_call(
        out_project_kernel,
        in_specs=[SMEM] + [vmem] * 11,
        out_specs=[vmem] * 3,
        out_shape=[
            shape_of((rows, model), F32),
            shape_of((rows, model), LOW),
            shape_of((model, model), LOW),
        ],
        compiler_params=params(),
        cost_estimate=cost(4 * rows * model * model, rows * model * 12),
        name="out_project",
    )(where, tokens, *attn, own, *pieces, *others, gain)


def out_back_kernel(
    where_ref, own_ref, recv_ref, res_ref, dy_ref, gain_ref, w_ref, attn0_ref, attn1_ref,
    dattn_ref, dres_ref, dgain_ref, keep_ref, send_ref,
    gout_ref,
):
    chips, width, rows = dattn_ref.shape[0] // 2, dattn_ref.shape[2], dattn_ref.shape[3]
    grad = own_ref[...] + recv_ref[...].astype(F32)
    residual = res_ref[...]
    scale = rms_rows(residual)
    unit = residual * scale
    dgain_ref[...] = jnp.sum(grad * unit, axis=0, keepdims=True)
    inner = grad * gain_ref[...]
    dres = dy_ref[...].astype(F32) + scale * (
        inner - unit * jnp.mean(inner * unit, axis=-1, keepdims=True)
    )
    dres_ref[...] = dres
    branch = dres.astype(LOW)
    for chip in range(chips):
        heads = slice(chip * width, (chip + 1) * width)
        part = dot(w_ref[heads, :], branch, NT).astype(LOW)
        for slot in range(4):
            dattn_ref[2 * chip + slot // 2, slot % 2] = part[:, slot * rows : (slot + 1) * rows]
        gout_ref[heads, :] = dot(side_by_side((attn0_ref, attn1_ref), chip), branch).astype(LOW)
    core = where_ref[1]
    planes, slab, _ = keep_ref.shape
    for plane in range(planes):
        keep_ref[plane] = gout_ref[block_rows(2 * plane + core, slab), :]
        send_ref[plane] = gout_ref[block_rows(2 * plane + 1 - core, slab), :]


def out_back(where, own, recv, residual, dy, gain, w_out, attn, planes):
    rows, model = own.shape
    vmem = pl.BlockSpec(memory_space=pltpu.VMEM)
    half = shape_of((planes, model // planes // 2, model), LOW)
    return pl.pallas_call(
        out_back_kernel,
        in_specs=[SMEM] + [vmem] * 8,
        out_specs=[vmem] * 5,
        out_shape=[
            shape_of((attn[0].shape[0], 2, *attn[0].shape[2:]), LOW),
            shape_of((rows, model), F32),
            shape_of((1, model), F32),
            half,
            half,
        ],
        scratch_shapes=[pltpu.VMEM((model, model), LOW)],
        compiler_params=params(),
        cost_estimate=cost(8 * rows * model * model, rows * model * 20),
        name="out_back",
    )(where, own, recv, residual, dy, gain, w_out, *attn)


def gate_and_slope(gate):
    inner = 0.7978845608028654 * (gate + 0.044715 * gate * gate * gate)
    bent = jnp.tanh(inner)
    half = 0.5 * (1.0 + bent)
    slope = half + 0.5 * gate * (1.0 - bent * bent) * (
        0.7978845608028654 * (1.0 + 3.0 * 0.044715 * gate * gate)
    )
    return gate * half, slope


def ffn_first_kernel(
    where_ref, nf_own_ref, nf_other_ref, dy_own_ref, dy_other_ref,
    gate_own, up_own, down_own, x1, x2, x3, y1, y2, y3, sx1, sx2, sx3, sy1, sy2, sy3,
    hidden_ref, dup_ref, own_ref, other_ref, down_ref, g0_ref, g1_ref, g2_ref, g3_ref,
    gate_ref, up_ref, nf_ref, nft_ref, dy_ref, total_ref, dgate_ref, grad_ref, sems,
):
    step = pl.program_id(0)
    half = nf_own_ref.shape[0]
    chip, core, plane = where_ref[0], where_ref[1], where_ref[2]
    wide, model, _ = gate_ref.shape
    units = down_ref.shape[0]
    tile = hidden_ref.shape[1]
    depth = gate_own.shape[1]
    planes = model // depth
    slab = depth // 2
    part = units // planes
    quarter = part // 4

    @pl.when(step == 0)
    def _():
        copies = []

        def copy(source, target):
            started = pltpu.make_async_copy(source, target, sems.at[len(copies)])
            started.start()
            copies.append(started)

        own_rows = pl.ds(pl.multiple_of(plane * depth, depth), depth)
        for index in range(wide):
            copy(gate_own.at[index], gate_ref.at[index, own_rows, :])
            copy(up_own.at[index], up_ref.at[index, own_rows, :])
        copy(
            down_own.at[pl.ds(pl.multiple_of(core * part, part), part), :],
            down_ref.at[pl.ds(pl.multiple_of(plane * part, part), part), :],
        )
        for back in range(planes - 1):
            owner = lax.rem(plane + planes - 1 - back, planes)
            for along, straight, swapped, weight_ref, side in (
                (0, (x1, x2, x3)[back], (sx1, sx2, sx3)[back], gate_ref, lax.rem(chip, 2)),
                (1, (y1, y2, y3)[back], (sy1, sy2, sy3)[back], up_ref, chip // 2),
            ):
                for piece, here in ((straight, side), (swapped, 1 - side)):
                    at = pl.ds(pl.multiple_of(owner * depth + here * slab, slab), slab)
                    for index in range(wide):
                        copy(
                            piece.at[pl.ds(index * slab, slab), :],
                            weight_ref.at[index, at, :],
                        )
                    copy(
                        piece.at[pl.ds(wide * slab, quarter), :],
                        down_ref.at[
                            pl.ds(
                                pl.multiple_of(
                                    owner * part + (2 * along + here) * quarter, quarter
                                ),
                                quarter,
                            ),
                            :,
                        ],
                    )
        nf_ref[:half, :] = nf_own_ref[...]
        nf_ref[half:, :] = nf_other_ref[...]
        nft_ref[:, :half] = jnp.transpose(nf_own_ref[...])
        nft_ref[:, half:] = jnp.transpose(nf_other_ref[...])
        dy_ref[:half, :] = dy_own_ref[...]
        dy_ref[half:, :] = dy_other_ref[...]
        total_ref[...] = jnp.zeros_like(total_ref)
        for started in copies:
            started.wait()

    per = model // tile
    index = step // per
    lanes = pl.ds(pl.multiple_of(lax.rem(step, per) * tile, tile), tile)
    gate_w = gate_ref[index, :, lanes]
    up_w = up_ref[index, :, lanes]
    down_w = down_ref[block_rows(step, tile), :]
    for quarter_rows in range(4):
        rows = slice(quarter_rows * half // 2, (quarter_rows + 1) * half // 2)
        nf = nf_ref[rows, :]
        gate = dot(nf, gate_w)
        up = dot(nf, up_w)
        dhidden = dot(dy_ref[rows, :], down_w, NT)
        bent, slope = gate_and_slope(gate)
        hidden_ref[rows, :] = (bent * up).astype(LOW)
        dgate = (dhidden * up * slope).astype(LOW)
        dup = (dhidden * bent).astype(LOW)
        dgate_ref[rows, :] = dgate
        dup_ref[rows, :] = dup
        total_ref[rows, :] += dot(dgate, gate_w, NT) + dot(dup, up_w, NT)

    grad_ref[...] = dot(nft_ref[...], dgate_ref[...]).astype(LOW)
    for away, out_ref in enumerate((g0_ref, g1_ref, g2_ref, g3_ref)):
        out_ref[0] = grad_ref[block_rows(lax.rem(plane + away, planes), depth), :]

    @pl.when(step == pl.num_programs(0) - 1)
    def _():
        own_ref[...] = total_ref[:half, :]
        other_ref[...] = total_ref[half:, :].astype(LOW)


def ffn_first(where, nf_own, nf_other, dy_own, dy_other, own_weights, pieces, tile=TILE):
    half, model = nf_own.shape
    wide, depth, _ = own_weights[0].shape
    units = wide * model
    per = model // tile
    whole = pl.BlockSpec((half, model), lambda t: (0, 0))
    lane_tile = pl.BlockSpec((2 * half, tile), lambda t: (0, t))
    grad_tile = pl.BlockSpec((1, depth, tile), lambda t: (t // per, 0, t % per))
    copies = 2 * wide + 1 + 3 * 4 * (wide + 1)
    return pl.pallas_call(
        ffn_first_kernel,
        grid=(units // tile,),
        in_specs=[SMEM, whole, whole, whole, whole] + [ANY] * 15,
        out_specs=[
            lane_tile, lane_tile, whole, whole,
            pl.BlockSpec((units, model), lambda t: (0, 0)),
        ]
        + [grad_tile] * 4,
        out_shape=[
            shape_of((2 * half, units), LOW),
            shape_of((2 * half, units), LOW),
            shape_of((half, model), F32),
            shape_of((half, model), LOW),
            shape_of((units, model), LOW),
        ]
        + [shape_of((wide, depth, model), LOW)] * 4,
        scratch_shapes=[
            pltpu.VMEM((wide, model, model), LOW),
            pltpu.VMEM((wide, model, model), LOW),
            pltpu.VMEM((2 * half, model), LOW),
            pltpu.VMEM((model, 2 * half), LOW),
            pltpu.VMEM((2 * half, model), LOW),
            pltpu.VMEM((2 * half, model), F32),
            pltpu.VMEM((2 * half, tile), LOW),
            pltpu.VMEM((model, tile), LOW),
            pltpu.SemaphoreType.DMA((copies,)),
        ],
        compiler_params=params(),
        cost_estimate=cost(
            2 * 2 * 6 * 2 * half * model * units,
            6 * model * units + 12 * half * units + 20 * half * model,
        ),
        name="ffn_first",
    )(where, nf_own, nf_other, dy_own, dy_other, *own_weights, *pieces)


def ffn_second_kernel(
    where_ref, nf_own_ref, nf_other_ref, dy_own_ref, dy_other_ref, hidden_ref, dup_ref, down_ref,
    own_ref, other_ref, u_keep_ref, u_send_ref, f_keep_ref, f_send_ref,
    nft_ref, dy_ref, total_ref, grad_ref, gdown_ref,
):
    step = pl.program_id(0)
    half = nf_own_ref.shape[0]
    chip = where_ref[0]
    x_side, y_side = lax.rem(chip, 2), chip // 2
    planes, _, slab, tile = u_keep_ref.shape

    @pl.when(step == 0)
    def _():
        nft_ref[:, :half] = jnp.transpose(nf_own_ref[...])
        nft_ref[:, half:] = jnp.transpose(nf_other_ref[...])
        dy_ref[:half, :] = dy_own_ref[...]
        dy_ref[half:, :] = dy_other_ref[...]
        total_ref[...] = jnp.zeros_like(total_ref)

    hidden = hidden_ref[...]
    grad_ref[...] = dot(nft_ref[...], dup_ref[...]).astype(LOW)
    for plane in range(planes):
        u_keep_ref[plane, 0] = grad_ref[block_rows(2 * plane + x_side, slab), :]
        u_send_ref[plane, 0] = grad_ref[block_rows(2 * plane + 1 - x_side, slab), :]
    gdown_ref[block_rows(step, tile), :] = dot(jnp.transpose(hidden), dy_ref[...]).astype(LOW)
    total_ref[...] += dot(hidden, down_ref[...])

    @pl.when(step == pl.num_programs(0) - 1)
    def _():
        own_ref[...] = total_ref[:half, :]
        other_ref[...] = total_ref[half:, :].astype(LOW)
        rows = f_keep_ref.shape[1]
        for plane in range(planes):
            f_keep_ref[plane] = gdown_ref[block_rows(2 * plane + y_side, rows), :]
            f_send_ref[plane] = gdown_ref[block_rows(2 * plane + 1 - y_side, rows), :]


def ffn_second(
    where, nf_own, nf_other, dy_own, dy_other, hidden, dup, w_down, planes, tile=TILE
):
    half, model = nf_own.shape
    units = hidden.shape[1]
    wide, slab, rows = units // model, model // planes // 2, units // planes // 2
    per = model // tile
    whole = pl.BlockSpec((half, model), lambda t: (0, 0))
    lane_tile = pl.BlockSpec((2 * half, tile), lambda t: (0, t))
    row_tile = pl.BlockSpec((tile, model), lambda t: (t, 0))
    up_tile = pl.BlockSpec((planes, 1, slab, tile), lambda t: (0, t // per, 0, t % per))
    down_whole = pl.BlockSpec((planes, rows, model), lambda t: (0, 0, 0))
    return pl.pallas_call(
        ffn_second_kernel,
        grid=(units // tile,),
        in_specs=[SMEM, whole, whole, whole, whole, lane_tile, lane_tile, row_tile],
        out_specs=[whole, whole, up_tile, up_tile, down_whole, down_whole],
        out_shape=[
            shape_of((half, model), F32),
            shape_of((half, model), LOW),
            shape_of((planes, wide, slab, model), LOW),
            shape_of((planes, wide, slab, model), LOW),
            shape_of((planes, rows, model), LOW),
            shape_of((planes, rows, model), LOW),
        ],
        scratch_shapes=[
            pltpu.VMEM((model, 2 * half), LOW),
            pltpu.VMEM((2 * half, model), LOW),
            pltpu.VMEM((2 * half, model), F32),
            pltpu.VMEM((model, tile), LOW),
            pltpu.VMEM((units, model), LOW),
        ],
        compiler_params=params(),
        cost_estimate=cost(
            2 * 2 * 3 * 2 * half * model * units,
            8 * model * units + 12 * half * units + 20 * half * model,
        ),
        name="ffn_second",
    )(where, nf_own, nf_other, dy_own, dy_other, hidden, dup, w_down)


def second_halves_kernel(
    where_ref, u_keep_ref, u_came_ref, f_keep_ref, f_came_ref,
    u_mine_ref, u_send_ref, f_mine_ref, f_send_ref,
):
    chip = where_ref[0]
    x_side, y_side = lax.rem(chip, 2), chip // 2
    for wanted, u_ref, f_ref in ((0, u_mine_ref, f_mine_ref), (1, u_send_ref, f_send_ref)):
        u_side = jnp.bitwise_xor(y_side, wanted)
        rows = block_rows(u_side, u_ref.shape[2])
        u_ref[...] = (
            u_keep_ref[:, :, rows, :].astype(F32) + u_came_ref[:, :, rows, :].astype(F32)
        ).astype(LOW)
        f_side = jnp.bitwise_xor(x_side, wanted)
        rows = block_rows(f_side, f_ref.shape[1])
        f_ref[...] = (
            f_keep_ref[:, rows, :].astype(F32) + f_came_ref[:, rows, :].astype(F32)
        ).astype(LOW)


def second_halves(where, u_keep, u_came, f_keep, f_came):
    planes, wide, slab, model = u_keep.shape
    rows = f_keep.shape[1]
    vmem = pl.BlockSpec(memory_space=pltpu.VMEM)
    return pl.pallas_call(
        second_halves_kernel,
        in_specs=[SMEM] + [vmem] * 4,
        out_specs=[vmem] * 4,
        out_shape=[
            shape_of((planes, wide, slab // 2, model), LOW),
            shape_of((planes, wide, slab // 2, model), LOW),
            shape_of((planes, rows // 2, model), LOW),
            shape_of((planes, rows // 2, model), LOW),
        ],
        compiler_params=params(),
        cost_estimate=cost(0, 7e6),
        name="second_halves",
    )(where, u_keep, u_came, f_keep, f_came)


def by_chip_kernel(where_ref, *refs):
    gate_refs, keep_ref, came_ref, out_refs = refs[:4], refs[4], refs[5], refs[6:]
    chip = where_ref[0]
    wide, depth, model = gate_refs[0].shape
    planes, slab, _ = keep_ref.shape
    rows, half, lanes = depth // 4, slab // 2, model // 2
    for away, out_ref in enumerate(out_refs):
        to_chip = jnp.bitwise_xor(chip, away)
        to_x, to_y = lax.rem(to_chip, 2), to_chip // 2
        at = block_rows(to_x * 2 + to_y, rows)
        for index in range(wide):
            total = gate_refs[0][index, at, :].astype(F32)
            for gate_ref in gate_refs[1:]:
                total = total + gate_ref[index, at, :].astype(F32)
            out_ref[index * rows : (index + 1) * rows, :] = total.astype(LOW)
        columns = block_rows(to_y, lanes)
        for plane in range(planes):
            low = wide * rows + (plane // 2) * half
            left = (plane % 2) * lanes
            out_ref[low : low + half, left : left + lanes] = (
                keep_ref[plane, block_rows(to_x, half), columns].astype(F32)
                + came_ref[plane, block_rows(to_x, half), columns].astype(F32)
            ).astype(LOW)


def by_chip(where, gates, keep, came):
    wide, depth, model = gates[0].shape
    planes, slab, _ = keep.shape
    vmem = pl.BlockSpec(memory_space=pltpu.VMEM)
    return pl.pallas_call(
        by_chip_kernel,
        in_specs=[SMEM] + [vmem] * 6,
        out_specs=[vmem] * 4,
        out_shape=[shape_of((wide * depth // 4 + planes * slab // 4, model), LOW)] * 4,
        compiler_params=params(),
        cost_estimate=cost(0, 3e6),
        name="by_chip",
    )(where, *gates, keep, came)


def by_plane_kernel(where_ref, *refs):
    u_ref, u_came_ref, f_ref, f_came_ref, w_ref, w_came_ref, line_ref, line_came_ref = refs[:8]
    part_refs, out_refs, gate_ref = refs[8:12], refs[12:16], refs[16]
    plane = where_ref[2]
    planes, wide, rows, model = u_ref.shape
    slab = w_ref.shape[1]
    half, lanes = slab // 2, model // 2

    def four(at, columns):
        total = part_refs[0][at, columns].astype(F32)
        for part_ref in part_refs[1:]:
            total = total + part_ref[at, columns].astype(F32)
        return total.astype(LOW)

    gate_ref[...] = four(slice(0, wide * rows), slice(0, model))
    for away, out_ref in enumerate(out_refs):
        at = lax.rem(plane + away, planes)

        def both(ref, came_ref):
            return (ref[at].astype(F32) + came_ref[at].astype(F32)).astype(LOW)

        for index in range(wide):
            out_ref[index * rows : (index + 1) * rows, :] = (
                u_ref[at, index].astype(F32) + u_came_ref[at, index].astype(F32)
            ).astype(LOW)
        low = wide * rows
        out_ref[low : low + f_ref.shape[1], :] = both(f_ref, f_came_ref)
        low = low + f_ref.shape[1]
        used = 3 * model // 4
        out_ref[low : low + slab, :used] = both(w_ref, w_came_ref)[:, :used]
        out_part = four(
            pl.ds(pl.multiple_of(wide * rows + at // 2 * half, half), half),
            pl.ds(pl.multiple_of(lax.rem(at, 2) * lanes, lanes), lanes),
        )
        out_ref[low : low + half, used:] = out_part[:, : model - used]
        out_ref[low + half : low + slab, used:] = out_part[:, model - used :]
        out_ref[low + slab :, :] = both(line_ref, line_came_ref)


def by_plane(where, u_mine, u_came, f_mine, f_came, w_keep, w_came, line_keep, line_came, parts):
    planes, wide, slab, model = u_mine.shape
    rows = wide * slab + f_mine.shape[1] + w_keep.shape[1] + line_keep.shape[1]
    vmem = pl.BlockSpec(memory_space=pltpu.VMEM)
    return pl.pallas_call(
        by_plane_kernel,
        in_specs=[SMEM] + [vmem] * 12,
        out_specs=[vmem] * (planes + 1),
        out_shape=[shape_of((rows, model), LOW)] * planes + [shape_of((wide * slab, model), LOW)],
        compiler_params=params(),
        cost_estimate=cost(0, 6e6),
        name="by_plane",
    )(
        where, u_mine, u_came, f_mine, f_came, w_keep, w_came, line_keep, line_came, *parts
    )


def unpack_kernel(where_ref, *refs):
    piece_refs = refs[:8]
    gate_ref, up_ref, down_ref, q_ref, k_ref, v_ref, out_ref, small_ref = refs[8:]
    chip, core = where_ref[0], where_ref[1]
    depth, units = gate_ref.shape
    model = down_ref.shape[1]
    part = down_ref.shape[0] // 2
    quarter, slab = depth // 4, depth // 2
    wide = units // 2 // model
    planes = units // 2 // part
    width, lanes, half = model // 4, model // 2, slab // 2
    small = jnp.zeros(small_ref.shape, F32)
    for far in range(8):
        away, other = far % 4, far // 4
        from_core = core if other == 0 else 1 - core
        from_chip = jnp.bitwise_xor(chip, away)
        from_x, from_y = lax.rem(from_chip, 2), from_chip // 2
        piece_ref = piece_refs[far]
        gate_rows = block_rows(from_x * 2 + from_y, quarter)
        for plane in range(planes):
            index, at = divmod(plane * part, model)
            columns = pl.ds(pl.multiple_of(plane * 2 * part + from_core * part, 128), part)
            rows = slice(index * quarter, (index + 1) * quarter)
            gate_ref[gate_rows, columns] = piece_ref[rows, at : at + part].astype(F32)
            rows = slice((wide + index) * quarter, (wide + index + 1) * quarter)
            up_ref[gate_rows, columns] = piece_ref[rows, at : at + part].astype(F32)
        low = 2 * wide * quarter
        rows = part // 4
        down_ref[block_rows(from_core * 4 + from_y * 2 + from_x, rows), :] = piece_ref[
            low : low + rows, :
        ].astype(F32)
        low = low + rows
        used = 3 * width
        out_ref[block_rows(from_core * 2 + from_x, half), block_rows(from_y, lanes)] = (
            jnp.concatenate(
                [piece_ref[low : low + half, used:], piece_ref[low + half : low + slab, used:]],
                axis=1,
            ).astype(F32)
        )
        for home in range(4):

            @pl.when(from_chip == home)
            def _(home=home, piece_ref=piece_ref, from_core=from_core, low=low):
                to_lanes = slice(home * width, (home + 1) * width)
                for kind, target_ref in enumerate((q_ref, k_ref, v_ref)):
                    target_ref[block_rows(from_core, slab), to_lanes] = piece_ref[
                        low : low + slab, kind * width : (kind + 1) * width
                    ].astype(F32)

        small = small + piece_ref[low + slab :, :].astype(F32)
    small_ref[...] = small


def unpack(where, pieces, depth, units):
    rows, model = pieces[0].shape
    planes = model // depth
    part = units // planes
    taken = units // 2 // model * depth // 2 + part // 8 + depth // 2
    vmem = pl.BlockSpec(memory_space=pltpu.VMEM)
    return pl.pallas_call(
        unpack_kernel,
        in_specs=[SMEM] + [vmem] * 8,
        out_specs=[vmem] * 8,
        out_shape=[
            shape_of((depth, units), F32),
            shape_of((depth, units), F32),
            shape_of((part, model), F32),
            shape_of((depth, model), F32),
            shape_of((depth, model), F32),
            shape_of((depth, model), F32),
            shape_of((depth, model), F32),
            shape_of((rows - taken, model), F32),
        ],
        compiler_params=params(),
        cost_estimate=cost(0, 24e6),
        name="unpack",
    )(where, *pieces)


def finish_out_kernel(order_ref, lens_ref, start_ref, res_ref, own_ref, recv_ref, out_ref):
    slot = pl.program_id(0)
    total = res_ref[...] + own_ref[...] + recv_ref[...].astype(F32)
    place_in = lax.broadcasted_iota(jnp.int32, total.shape, 0) + start_ref[0]
    out_ref[0] = jnp.where(place_in < lens_ref[slot], total, 0.0).astype(LOW)


def finish_out(order, lens, start, residual, own, recv, batch):
    rows, model = residual.shape[0] // batch, residual.shape[1]
    in_order = pl.BlockSpec((rows, model), lambda s, order, lens, start: (s, 0))
    return pl.pallas_call(
        finish_out_kernel,
        grid_spec=pltpu.PrefetchScalarGridSpec(
            num_scalar_prefetch=3,
            grid=(batch,),
            in_specs=[in_order, in_order, in_order],
            out_specs=pl.BlockSpec((1, rows, model), lambda s, order, lens, start: (order[s], 0, 0)),
        ),
        out_shape=shape_of((batch, rows, model), LOW),
        compiler_params=params(),
        cost_estimate=cost(0, 6e6),
        name="finish_out",
    )(order, lens, start, residual, own, recv)


def finish_tokens_kernel(order_ref, dn_ref, tok_ref, dres_ref, gain_ref, out_ref):
    grad = dn_ref[0, 0].astype(F32)
    for chip in range(1, dn_ref.shape[0]):
        grad = grad + dn_ref[chip, 0].astype(F32)
    rows_f = tok_ref[...].astype(F32)
    scale = rms_rows(rows_f)
    unit = rows_f * scale
    inner = grad * gain_ref[...]
    out_ref[0] = dres_ref[...] + scale * (
        inner - unit * jnp.mean(inner * unit, axis=-1, keepdims=True)
    )


def finish_tokens(order, dn, tokens, dres, gain):
    chips, batch, rows, model = dn.shape
    in_order = pl.BlockSpec((rows, model), lambda s, order: (s, 0))
    return pl.pallas_call(
        finish_tokens_kernel,
        grid_spec=pltpu.PrefetchScalarGridSpec(
            num_scalar_prefetch=1,
            grid=(batch,),
            in_specs=[
                pl.BlockSpec((chips, 1, rows, model), lambda s, order: (0, s, 0, 0)),
                in_order,
                in_order,
                pl.BlockSpec((1, model), lambda s, order: (0, 0)),
            ],
            out_specs=pl.BlockSpec((1, rows, model), lambda s, order: (order[s], 0, 0)),
        ),
        out_shape=shape_of((batch, rows, model), F32),
        compiler_params=params(),
        cost_estimate=cost(0, 10e6),
        name="finish_tokens",
    )(order, dn, tokens, dres, gain)


CORE, X, Y, XY = 1, 2, 4, 6


def swap(values, bits):
    count = lax.axis_size("ctx")
    return lax.ppermute(values, "ctx", [(i, i ^ bits) for i in range(count)])


def shift(values, places):
    count = lax.axis_size("fsdp")
    return lax.ppermute(values, "fsdp", [(i, (i + places) % count) for i in range(count)])


def column_ends(piece):
    return shift(piece, 1), shift(piece, 3)


def after(values, *others):
    return lax.optimization_barrier((values, *others))[0]


def pick(values, index, axis):
    return lax.dynamic_index_in_dim(values, index, axis, keepdims=False)


def add(*parts):
    total = parts[0].astype(F32)
    for part in parts[1:]:
        total = total + part.astype(F32)
    return total.astype(LOW)


def column_sum(picks):
    return [picks[0]] + [shift(picks[away], away) for away in range(1, len(picks))]


def plane_swaps(parts):
    return [parts[0], swap(parts[1], X), swap(parts[2], Y), swap(parts[3], XY)]


def per_device_plane(
    tokens, cotangent, lengths, bucket_table, gain_attn, w_query, w_key, w_value, w_out,
    bias_table, gain_ffn, w_gate, w_up, w_ffn_out,
):
    batch, rows, model = tokens.shape
    planes = lax.axis_size("fsdp")
    chips = lax.axis_size("ctx") // 2
    me = lax.axis_index("ctx")
    plane = lax.axis_index("fsdp")
    core, chip = me % 2, me // 2
    depth, units = w_gate.shape
    chip_heads = HEADS // chips
    width = chip_heads * HEAD_DIM
    where = jnp.stack([chip, core, plane]).astype(jnp.int32)
    start = (me * rows)[None].astype(jnp.int32)

    small = jnp.concatenate([gain_attn, gain_ffn, bias_table.reshape(-1)])
    small = jnp.pad(small[None], ((0, 15), (0, model - small.shape[0])))
    gate_mine, up_mine, x_piece, y_piece, qkv_mine, early_piece = pack_weights(
        where, w_gate, w_up, w_ffn_out, w_out, w_query, w_key, w_value, small
    )
    send, order, lens = prepare(lengths, after(tokens, early_piece), chips)
    gathered = lax.all_to_all(send.reshape(2 * chips, 2, rows, model), "ctx", 0, 0)

    near, far = column_ends(early_piece)
    early = [near, shift(near, 1), far]
    early_others = [swap(piece, CORE) for piece in early]
    x_piece, y_piece, *_ = lax.optimization_barrier((x_piece, y_piece, *early))
    x_near, x_far = column_ends(x_piece)
    y_near, y_far = column_ends(y_piece)

    by_distance = jnp.stack([piece[depth] for piece in [early_piece] + early])
    all_small = jnp.stack([pick(by_distance, (plane + planes - i) % planes, 0) for i in range(planes)])
    full_gain_attn = all_small[:, :depth].reshape(1, model).astype(F32)
    full_gain_ffn = all_small[:, depth : 2 * depth].reshape(1, model).astype(F32)
    small_end = 2 * depth + bias_table.size
    full_table = all_small[:, 2 * depth : small_end].reshape(BUCKETS, HEADS)

    hot = bucket_table[:, None] == jnp.arange(BUCKETS, dtype=jnp.int32)[None, :]
    hot = jnp.concatenate([hot, jnp.zeros((1, BUCKETS), bool)])
    my_table = lax.dynamic_slice_in_dim(full_table, chip * chip_heads, chip_heads, 1)
    offsets = jnp.einsum("tb,bh->ht", hot.astype(LOW), my_table, preferred_element_type=F32)

    first_out, *kept, w_qkv = attn_forward(
        0, lens, where, gathered, full_gain_attn, [qkv_mine, *early, *early_others], offsets
    )
    x_near, y_near, x_far, y_far, first_out = lax.optimization_barrier(
        (x_near, y_near, x_far, y_far, first_out)
    )
    x_found = [x_near, shift(x_near, 1), x_far]
    y_found = [y_near, shift(y_near, 1), y_far]
    x_swapped, y_swapped = [swap(t, X) for t in x_found], [swap(t, Y) for t in y_found]
    second_out, *kept = attn_forward(
        1, lens, where, gathered, full_gain_attn, [w_qkv], offsets, kept
    )
    attn = [lax.all_to_all(part, "ctx", 0, 0) for part in (first_out, second_out)]
    attn_full, query, key, value = kept
    flat, dy = sort_rows(order, lens, start, tokens, cotangent)
    residual, nf_own, full_out = out_project(
        where, flat, attn, w_out, early, early_others, full_gain_ffn
    )
    dy_other = swap(dy, CORE)
    nf_other = swap(nf_own, CORE)
    hidden, dup, dnf_own, dnf_send, full_down, *g_picks = ffn_first(
        where, nf_own, nf_other, dy, dy_other, (gate_mine, up_mine, w_ffn_out),
        x_found + y_found + x_swapped + y_swapped,
    )

    g_parts = column_sum(g_picks)
    dattn, dres, dgain_ffn, o_keep, o_send = out_back(
        where, dnf_own, swap(dnf_send, CORE), residual, dy, full_gain_ffn, full_out, attn, planes
    )
    dattn_all = lax.all_to_all(dattn, "ctx", 0, 0)
    o_came = swap(o_send, CORE)
    out_own, out_send, u_keep, u_send, f_keep, f_send = ffn_second(
        where, nf_own, nf_other, dy, dy_other, hidden, dup, full_down, planes
    )
    g_parts[1], g_parts[3], u_send, f_send, dattn_all = lax.optimization_barrier(
        (g_parts[1], g_parts[3], u_send, f_send, dattn_all)
    )
    u_came, f_came = swap(u_send, X), swap(f_send, Y)
    out_came = swap(out_send, CORE)
    dn, dw_keep, dw_send, dgain_attn, doffsets = attn_backward(
        lens, where, gathered, full_gain_attn, w_qkv, offsets,
        query, key, value, attn_full, dattn_all, planes,
    )

    u_came, f_came, dn, dw_send, dgain_attn, *g_parts = lax.optimization_barrier(
        (u_came, f_came, dn, dw_send, dgain_attn, *g_parts)
    )
    u_mine, u_send, f_mine, f_send = second_halves(where, u_keep, u_came, f_keep, f_came)
    u_came, f_came = swap(u_send, Y), swap(f_send, X)
    w_came = swap(dw_send, CORE)
    chip_parts = plane_swaps(by_chip(where, g_parts, o_keep, o_came))

    out_rows = finish_out(order, lens, start, residual, out_own, out_came, batch)
    mine_buckets = jnp.einsum(
        "ht,tb->bh", doffsets, hot.astype(F32), precision=lax.Precision.HIGHEST
    )
    buckets = lax.dynamic_update_slice_in_dim(
        jnp.zeros((BUCKETS, HEADS), F32), mine_buckets, chip * chip_heads, 1
    )
    line = jnp.concatenate(
        [
            dgain_attn.reshape(planes, depth),
            dgain_ffn.reshape(planes, depth),
            buckets.reshape(planes, -1),
        ],
        axis=1,
    ).astype(LOW)
    line = jnp.pad(line[:, None, :], ((0, 0), (0, 15), (0, model - line.shape[1])))
    nothing = jnp.zeros_like(line)
    line_came = swap(jnp.where(core == 1, line, nothing), CORE)
    line_kept = jnp.where(core == 0, line, nothing)
    *plane_parts, gate_part = by_plane(
        where, u_mine, u_came, f_mine, f_came, dw_keep, w_came, line_kept, line_came, chip_parts
    )
    dn, *plane_parts = lax.optimization_barrier((dn, *plane_parts))
    dn = lax.all_to_all(dn, "ctx", 0, 0).reshape(chips, batch, rows, model)
    dtok = finish_tokens(order, dn, flat, dres, full_gain_attn)
    pack = jnp.concatenate([gate_part, add(*column_sum(plane_parts))])

    packs = plane_swaps([after(pack, out_rows)] * 4)
    packs = packs + [swap(piece, CORE) for piece in packs]
    packs[-1] = after(packs[-1], dtok)
    grad_gate, grad_up, grad_down, grad_query, grad_key, grad_value, grad_out, sums = unpack(
        where, packs, depth, units
    )
    grad_gain_attn = sums[0, :depth]
    grad_gain_ffn = sums[0, depth : 2 * depth]
    grad_buckets = sums[0, 2 * depth : small_end].reshape(BUCKETS // planes, HEADS)

    return (
        out_rows, dtok, grad_gain_attn, grad_query, grad_key, grad_value, grad_out, grad_buckets,
        grad_gain_ffn, grad_gate, grad_up, grad_down,
    )


def gelu_tanh(values):
    return (
        0.5
        * values
        * (1.0 + jnp.tanh(0.7978845608028654 * (values + 0.044715 * values * values * values)))
    )


def normalize(values, gain_vec):
    return (
        values * lax.rsqrt(jnp.mean(values * values, axis=-1, keepdims=True) + norm_eps) * gain_vec
    )


def project(values, matrix):
    return jnp.einsum("msd,de->mse", values, matrix, preferred_element_type=jnp.float32)


def back_project(values, matrix):
    return jnp.einsum("mse,de->msd", values, matrix, preferred_element_type=jnp.float32)


def outer_sum(left_rows, right_rows):
    return jnp.einsum("msd,mse->de", left_rows, right_rows, preferred_element_type=jnp.float32)


def split_heads(values):
    return values.reshape(values.shape[0], values.shape[1], HEADS, HEAD_DIM)


def toeplitz_bias(offset_bias, start, query_rows, key_rows):
    span = query_rows + key_rows - 1
    window = lax.dynamic_slice_in_dim(offset_bias, start, span, 1)
    wrapped = jnp.concatenate(
        [
            window[:, query_rows - 1 :],
            jnp.zeros((window.shape[0], 1), jnp.float32),
            window[:, : query_rows - 1],
        ],
        axis=1,
    )
    tiled = jnp.tile(wrapped, (1, query_rows))
    shaped = tiled[:, : query_rows * span].reshape(window.shape[0], query_rows, span)
    return shaped[:, :, :key_rows]


def diagonal_sums(grad_bias, query_rows, key_rows):
    span = query_rows + key_rows - 1
    heads = grad_bias.shape[0]
    padded = jnp.pad(grad_bias, ((0, 0), (0, 0), (0, span - key_rows)))
    flat = jnp.pad(padded.reshape(heads, query_rows * span), ((0, 0), (0, query_rows)))
    slots = jnp.sum(flat.reshape(heads, query_rows, span + 1), axis=1)
    return jnp.concatenate([slots[:, key_rows + 1 :], slots[:, :key_rows]], axis=1)


def block_scores(query_heads, key_heads, pair_bias, key_ok):
    scores = jnp.einsum(
        "mihe,mjhe->mhij", query_heads, key_heads, preferred_element_type=jnp.float32
    )
    scores = scores + pair_bias[None]
    return jnp.where(key_ok[:, None, None, :], scores, -1e30)


def over_blocks(update, make_bias, carried, pieces):
    piece_rows = pieces[0].shape[1]
    block_rows = math.gcd(piece_rows, 256)
    block_count = piece_rows // block_rows

    def advance(block_index, running):
        block_start = block_index * block_rows
        sub_pieces = tuple(
            (
                lax.dynamic_slice_in_dim(member, block_index * block_rows, block_rows, 1)
                for member in pieces
            )
        )
        bias_info = make_bias(block_start, block_rows)
        return update(running, sub_pieces, block_start, slice(None), bias_info)

    return lax.fori_loop(0, block_count, advance, carried)


def per_device_general(
    tokens,
    cotangent,
    lengths,
    bucket_table,
    gain_attn,
    w_query,
    w_key,
    w_value,
    w_out,
    bias_table,
    gain_ffn,
    w_gate,
    w_up,
    w_ffn_out,
):
    shards = (
        gain_attn,
        w_query,
        w_key,
        w_value,
        w_out,
        bias_table,
        gain_ffn,
        w_gate,
        w_up,
        w_ffn_out,
    )
    gathered = (
        lax.all_gather(shards[0], "fsdp", axis=0, tiled=True),
        lax.all_gather(shards[1], "fsdp", axis=0, tiled=True),
        lax.all_gather(shards[2], "fsdp", axis=0, tiled=True),
        lax.all_gather(shards[3], "fsdp", axis=0, tiled=True),
        lax.all_gather(shards[4], "fsdp", axis=0, tiled=True),
        lax.all_gather(shards[5], "fsdp", axis=0, tiled=True),
        lax.all_gather(shards[6], "fsdp", axis=0, tiled=True),
        lax.all_gather(shards[7], "fsdp", axis=0, tiled=True),
        lax.all_gather(shards[8], "fsdp", axis=0, tiled=True),
        lax.all_gather(shards[9], "fsdp", axis=0, tiled=True),
    )
    (
        full_gain_attn,
        full_query,
        full_key,
        full_value,
        full_out,
        full_bias,
        full_gain_ffn,
        full_gate,
        full_up,
        full_ffn_out,
    ) = gathered
    batch_rows, local_rows, model_width = tokens.shape
    seq_len = local_rows * lax.axis_size("ctx")
    table_len = bucket_table.shape[0]
    first_pos = lax.axis_index("ctx") * local_rows
    positions = first_pos + jnp.arange(local_rows, dtype=jnp.int32)
    valid_mask = positions[None, :] < lengths[:, None]
    valid_rows = valid_mask.astype(jnp.float32)
    bucket_hot = bucket_table[:, None] == jnp.arange(BUCKETS, dtype=jnp.int32)[None, :]

    def offset_bias_of(bias_weights):
        return jnp.einsum(
            "tb,bh->ht",
            bucket_hot.astype(jnp.bfloat16),
            bias_weights,
            preferred_element_type=jnp.float32,
        )

    forward_offsets = offset_bias_of(full_bias)

    def keys_bias(offset_bias):

        def keys_make(block_start, block_rows):
            start = block_start - first_pos - (local_rows - 1) + (seq_len - 1)
            return (toeplitz_bias(offset_bias, start, local_rows, block_rows), start)

        return keys_make

    def queries_bias(offset_bias):

        def queries_make(block_start, block_rows):
            start = first_pos - block_start - (block_rows - 1) + (seq_len - 1)
            return (toeplitz_bias(offset_bias, start, block_rows, local_rows), start)

        return queries_make

    tokens_f = tokens.astype(jnp.float32)
    attn_gain = full_gain_attn.astype(jnp.float32)
    normed = normalize(tokens_f, attn_gain).astype(jnp.bfloat16)
    queries = project(normed, full_query).astype(jnp.bfloat16)
    keys_local = project(normed, full_key).astype(jnp.bfloat16)
    values_local = project(normed, full_value).astype(jnp.bfloat16)
    query_heads = split_heads(queries)

    def forward_block(running, sub_pieces, block_start, member_pick, bias_info):
        max_score, row_total, weighted = running
        key_part, value_part = sub_pieces
        key_pos = block_start + jnp.arange(key_part.shape[1], dtype=jnp.int32)
        key_ok = key_pos[None, :] < lengths[:, None]
        scores = block_scores(query_heads, split_heads(key_part), bias_info[0], key_ok)
        new_max = jnp.maximum(max_score, jnp.max(scores, axis=-1))
        shrink = jnp.exp(max_score - new_max)
        weights = jnp.exp(scores - new_max[..., None])
        row_total = row_total * shrink + jnp.sum(weights, axis=-1)
        weighted = weighted * jnp.transpose(shrink, (0, 2, 1))[..., None] + jnp.einsum(
            "mhij,mjhe->mihe",
            weights.astype(jnp.bfloat16),
            split_heads(value_part),
            preferred_element_type=jnp.float32,
        )
        return (new_max, row_total, weighted)

    start_state = (
        jnp.full((batch_rows, HEADS, local_rows), -1e30, jnp.float32),
        jnp.zeros((batch_rows, HEADS, local_rows), jnp.float32),
        jnp.zeros((batch_rows, local_rows, HEADS, HEAD_DIM), jnp.float32),
    )
    max_score, row_total, weighted = over_blocks(
        forward_block,
        keys_bias(forward_offsets),
        start_state,
        (
            lax.all_gather(keys_local, "ctx", axis=1, tiled=True),
            lax.all_gather(values_local, "ctx", axis=1, tiled=True),
        ),
    )
    log_total = max_score + jnp.log(row_total)
    attn_full = weighted / jnp.transpose(row_total, (0, 2, 1))[..., None]
    attn_low = attn_full.reshape(batch_rows, local_rows, model_width).astype(jnp.bfloat16)
    residual = tokens_f + project(attn_low, full_out)
    ffn_gain = full_gain_ffn.astype(jnp.float32)
    normed_ffn = normalize(residual, ffn_gain).astype(jnp.bfloat16)
    gate_proj = project(normed_ffn, full_gate)
    up_proj = project(normed_ffn, full_up)
    hidden = (gelu_tanh(gate_proj) * up_proj).astype(jnp.bfloat16)
    result = valid_rows[..., None] * (residual + project(hidden, full_ffn_out))
    output = result.astype(jnp.bfloat16)
    back_weights = (
        lax.all_gather(shards[0], "fsdp", axis=0, tiled=True),
        lax.all_gather(shards[1], "fsdp", axis=0, tiled=True),
        lax.all_gather(shards[2], "fsdp", axis=0, tiled=True),
        lax.all_gather(shards[3], "fsdp", axis=0, tiled=True),
        lax.all_gather(shards[4], "fsdp", axis=0, tiled=True),
        lax.all_gather(shards[5], "fsdp", axis=0, tiled=True),
        lax.all_gather(shards[6], "fsdp", axis=0, tiled=True),
        lax.all_gather(shards[7], "fsdp", axis=0, tiled=True),
        lax.all_gather(shards[8], "fsdp", axis=0, tiled=True),
        lax.all_gather(shards[9], "fsdp", axis=0, tiled=True),
    )
    (
        back_gain_attn,
        back_query,
        back_key,
        back_value,
        back_out,
        back_bias,
        back_gain_ffn,
        back_gate,
        back_up,
        back_ffn_out,
    ) = back_weights
    back_offsets = offset_bias_of(back_bias)
    grad_out = cotangent.astype(jnp.float32) * valid_rows[..., None]
    grad_low = grad_out.astype(jnp.bfloat16)
    grad_w_ffn_out = outer_sum(hidden, grad_low)
    grad_hidden = back_project(grad_low, back_ffn_out)

    def gated_product(gate_in, up_in):
        return gelu_tanh(gate_in) * up_in

    gated_value, gated_back = jax.vjp(gated_product, gate_proj, up_proj)
    grad_gate, grad_up = gated_back(grad_hidden)
    grad_gate = grad_gate.astype(jnp.bfloat16)
    grad_up = grad_up.astype(jnp.bfloat16)
    grad_w_gate = outer_sum(normed_ffn, grad_gate)
    grad_w_up = outer_sum(normed_ffn, grad_up)
    grad_normed_ffn = back_project(grad_gate, back_gate) + back_project(grad_up, back_up)
    norm_value, norm_back = jax.vjp(normalize, residual, back_gain_ffn.astype(jnp.float32))
    grad_resid_part, grad_gain_ffn = norm_back(grad_normed_ffn)
    grad_resid = grad_out + grad_resid_part
    grad_branch = grad_resid.astype(jnp.bfloat16)
    grad_w_out = outer_sum(attn_low, grad_branch)
    grad_attn = back_project(grad_branch, back_out).astype(jnp.bfloat16)
    grad_heads = split_heads(grad_attn)
    delta_row = jnp.einsum(
        "mihe,mihe->mhi", grad_heads, attn_full, preferred_element_type=jnp.float32
    )

    def query_grad_block(running, sub_pieces, block_start, member_pick, bias_info):
        grad_query, grad_offsets = running
        pair_bias, table_start = bias_info
        key_part, value_part = sub_pieces
        key_heads = split_heads(key_part)
        key_pos = block_start + jnp.arange(key_part.shape[1], dtype=jnp.int32)
        key_ok = key_pos[None, :] < lengths[:, None]
        scores = block_scores(query_heads, key_heads, pair_bias, key_ok)
        probabilities = jnp.exp(scores - log_total[..., None])
        grad_probs = jnp.einsum(
            "mihe,mjhe->mhij",
            grad_heads,
            split_heads(value_part),
            preferred_element_type=jnp.float32,
        )
        grad_scores = (probabilities * (grad_probs - delta_row[..., None])).astype(jnp.bfloat16)
        grad_query = grad_query + jnp.einsum(
            "mhij,mjhe->mihe", grad_scores, key_heads, preferred_element_type=jnp.float32
        )
        pair_grad = jnp.sum(grad_scores.astype(jnp.float32), axis=0)
        diag = diagonal_sums(pair_grad, pair_grad.shape[1], pair_grad.shape[2])
        current = lax.dynamic_slice_in_dim(grad_offsets, table_start, diag.shape[1], 1)
        grad_offsets = lax.dynamic_update_slice_in_dim(grad_offsets, current + diag, table_start, 1)
        return (grad_query, grad_offsets)

    query_state = (
        jnp.zeros((batch_rows, local_rows, HEADS, HEAD_DIM), jnp.float32),
        jnp.zeros((HEADS, table_len), jnp.float32),
    )
    grad_query, grad_offsets = over_blocks(
        query_grad_block,
        keys_bias(back_offsets),
        query_state,
        (
            lax.all_gather(keys_local, "ctx", axis=1, tiled=True),
            lax.all_gather(values_local, "ctx", axis=1, tiled=True),
        ),
    )
    grad_buckets = jnp.einsum(
        "ht,tb->bh", grad_offsets, bucket_hot.astype(jnp.float32), precision=lax.Precision.HIGHEST
    )
    stats_lse, stats_delta = (
        lax.all_gather(log_total, "ctx", axis=2, tiled=True),
        lax.all_gather(delta_row, "ctx", axis=2, tiled=True),
    )
    key_heads_local = split_heads(keys_local)
    value_heads_local = split_heads(values_local)

    def key_grad_block(running, sub_pieces, block_start, member_pick, bias_info):
        grad_key, grad_value = running
        query_part, grad_part = sub_pieces
        rows_here = query_part.shape[1]
        query_part_heads = split_heads(query_part)
        grad_part_heads = split_heads(grad_part)
        scores = block_scores(query_part_heads, key_heads_local, bias_info[0], valid_mask)
        lse_part = lax.dynamic_slice_in_dim(stats_lse, block_start, rows_here, 2)
        delta_part = lax.dynamic_slice_in_dim(stats_delta, block_start, rows_here, 2)
        probabilities = jnp.exp(scores - lse_part[..., None])
        grad_value = grad_value + jnp.einsum(
            "mhij,mihe->mjhe",
            probabilities.astype(jnp.bfloat16),
            grad_part_heads,
            preferred_element_type=jnp.float32,
        )
        grad_probs = jnp.einsum(
            "mihe,mjhe->mhij",
            grad_part_heads,
            value_heads_local,
            preferred_element_type=jnp.float32,
        )
        grad_scores = (probabilities * (grad_probs - delta_part[..., None])).astype(jnp.bfloat16)
        grad_key = grad_key + jnp.einsum(
            "mhij,mihe->mjhe", grad_scores, query_part_heads, preferred_element_type=jnp.float32
        )
        return (grad_key, grad_value)

    key_state = (
        jnp.zeros((batch_rows, local_rows, HEADS, HEAD_DIM), jnp.float32),
        jnp.zeros((batch_rows, local_rows, HEADS, HEAD_DIM), jnp.float32),
    )
    grad_key, grad_value = over_blocks(
        key_grad_block,
        queries_bias(back_offsets),
        key_state,
        (
            lax.all_gather(queries, "ctx", axis=1, tiled=True),
            lax.all_gather(grad_attn, "ctx", axis=1, tiled=True),
        ),
    )
    grad_q = grad_query.reshape(batch_rows, local_rows, model_width).astype(jnp.bfloat16)
    grad_k = grad_key.reshape(batch_rows, local_rows, model_width).astype(jnp.bfloat16)
    grad_v = grad_value.reshape(batch_rows, local_rows, model_width).astype(jnp.bfloat16)
    grad_w_query = outer_sum(normed, grad_q)
    grad_w_key = outer_sum(normed, grad_k)
    grad_w_value = outer_sum(normed, grad_v)
    grad_normed = (
        back_project(grad_q, back_query)
        + back_project(grad_k, back_key)
        + back_project(grad_v, back_value)
    )
    attn_norm_value, attn_norm_back = jax.vjp(
        normalize, tokens_f, back_gain_attn.astype(jnp.float32)
    )
    grad_tokens_part, grad_gain_attn = attn_norm_back(grad_normed)
    grad_tokens = grad_resid + grad_tokens_part
    grads = (
        grad_gain_attn,
        grad_w_query,
        grad_w_key,
        grad_w_value,
        grad_w_out,
        grad_buckets,
        grad_gain_ffn,
        grad_w_gate,
        grad_w_up,
        grad_w_ffn_out,
    )
    shard_sums = (
        lax.psum_scatter(grads[0], "fsdp", scatter_dimension=0, tiled=True),
        lax.psum_scatter(grads[1], "fsdp", scatter_dimension=0, tiled=True),
        lax.psum_scatter(grads[2], "fsdp", scatter_dimension=0, tiled=True),
        lax.psum_scatter(grads[3], "fsdp", scatter_dimension=0, tiled=True),
        lax.psum_scatter(grads[4], "fsdp", scatter_dimension=0, tiled=True),
        lax.psum_scatter(grads[5], "fsdp", scatter_dimension=0, tiled=True),
        lax.psum_scatter(grads[6], "fsdp", scatter_dimension=0, tiled=True),
        lax.psum_scatter(grads[7], "fsdp", scatter_dimension=0, tiled=True),
        lax.psum_scatter(grads[8], "fsdp", scatter_dimension=0, tiled=True),
        lax.psum_scatter(grads[9], "fsdp", scatter_dimension=0, tiled=True),
    )
    totals = lax.psum(
        (
            shard_sums[0],
            shard_sums[1],
            shard_sums[2],
            shard_sums[3],
            shard_sums[4],
            shard_sums[5],
            shard_sums[6],
            shard_sums[7],
            shard_sums[8],
            shard_sums[9],
        ),
        "ctx",
    )
    return (output, grad_tokens) + tuple(totals)


def solution(mesh):
    placed = (
        P("fsdp", "ctx", None),
        P("fsdp", "ctx", None),
        P("fsdp"),
        P(),
        P("fsdp"),
        P("fsdp", None),
        P("fsdp", None),
        P("fsdp", None),
        P("fsdp", None),
        P("fsdp", None),
        P("fsdp"),
        P("fsdp", None),
        P("fsdp", None),
        P("fsdp", None),
    )
    plane = mesh.shape["ctx"] == 8 and mesh.shape["fsdp"] == 4
    return jax.shard_map(
        per_device_plane if plane else per_device_general,
        mesh=mesh,
        in_specs=placed,
        out_specs=(
            P("fsdp", "ctx", None),
            P("fsdp", "ctx", None),
            P("fsdp"),
            P("fsdp", None),
            P("fsdp", None),
            P("fsdp", None),
            P("fsdp", None),
            P("fsdp", None),
            P("fsdp"),
            P("fsdp", None),
            P("fsdp", None),
            P("fsdp", None),
        ),
        check_vma=False,
    )
```

profile of v0, /device:TPU:9, one launch (start us, length us, event | category | flops | bytes accessed | tf_op | source)
XLA Modules:
  0.0 385.3 jit_solution(12893975034846457567)
XLA Ops:
  3.4 4.1 %pack_weights.1 = (bf16[2,192,768]{2,1,0:T(8,128)(2,1)}, bf16[2,192,768]{2,1,0:T(8,128)(2,1)}, bf16[288,768]{1,0:T(8,128)(2,1)}, bf16[288,768]{1,0:T(8,128)(2,1)...) custom-call(s32[3]{0:T(128)} %pad_add_fusion.where_ref, bf16[192,3072]{1,0:T(8,128)(2,1)} %gate_ref.1, ...), custom_call_target="tpu_custom_call" | custom-call | bytes 8000000 | tf_op jit(solution)/shard_map/pack_weights/pallas_call | solution.py:102
  7.5 3.0 prepare.1
  10.5 4.4 %all-to-all-start = ((bf16[8,2,128,768]{3,2,1,0:T(8,128)(2,1)}), bf16[8,2,128,768]{3,2,1,0:T(8,128)(2,1)S(1)}, u32[]{:S(2)}, u32[]{:S(2)}) async-start(bf16[8,2,128,768]{3,2,1,0:T(8,128)(2,1)} %bitcast.10), calls=%async_computation | async-start | bytes 6291456 | tf_op jit(solution)/shard_map/all_to_all | solution.py:1235
  15.0 1.3 collective-permute-start
  16.4 4.3 %sort_rows.1 = (bf16[512,768]{1,0:T(8,128)(2,1)}, bf16[512,768]{1,0:T(8,128)(2,1)}) custom-call(s32[4]{0:T(128)} %get-tuple-element.114.order_ref, s32[4]{0:T(128)} %get-tuple-element.115.lens_ref, s32[1]{0:T(128)} %bitcast.3.start_ref, bf16[4,128,768]{2,1,0:T(8,128)(2,1)} %tok_ref.2, bf16[4,128,768]{2,1,0:T(8,128)(2,1)} %cot_ref.1), custom_call_target="tpu_custom_call" | custom-call | bytes 1500000 | tf_op jit(solution)/shard_map/sort_rows/pallas_call | solution.py:168
  22.1 2.3 collective-permute-done.w1_ref.a1_ref
  24.4 1.4 collective-permute-start.1
  26.8 7.5 %collective-permute-start.7 = (bf16[208,768]{1,0:T(8,128)(2,1)}, bf16[208,768]{1,0:T(8,128)(2,1)}, u32[]{:S(2)}, u32[]{:S(2)}) collective-permute-start(bf16[208,768]{1,0:T(8,128)(2,1)} %collective-permute-done.w1_ref.a1_ref), channel_id=1, source_target_pairs={{0,4},{4,0},{8,12},{12,8},{16,20},{20,16},{24,28},{28,24},{1,5},{5... | collective-permute-start | bytes 958472 | tf_op jit(solution)/shard_map/ppermute | solution.py:1178
  35.0 3.0 collective-permute-done.1.w2_ref.a2_ref
  40.5 1.3 collective-permute-start.3
  41.8 1.0 fusion.off_ref
  44.2 2.5 collective-permute-start.6
  46.8 2.6 all-to-all-done.tok_ref
  49.4 1.6 copy-done.1
  51.0 14.7 %attn_forward.2 = (bf16[8,1,192,128]{3,2,1,0:T(8,128)(2,1)}, f32[2,1024,256]{2,1,0:T(8,128)}, bf16[2,1024,192]{2,1,0:T(8,128)(2,1)}, bf16[2,1024,192]{2,1,0:T(8,...) custom-call(s32[4]{0:T(128)} %get-tuple-element.115.lens_ref, s32[3]{0:T(128)} %pad_add_fusion.where_ref, ...), custom_call_target="tpu_custom_call" | custom-call | flops 2063597568 | bytes 2359296 | tf_op jit(solution)/shard_map/attn_forward/pallas_call | solution.py:347
  65.7 14.1 %attn_forward.3 = (bf16[8,1,192,128]{3,2,1,0:T(8,128)(2,1)}, f32[2,1024,256]{2,1,0:T(8,128)}, bf16[2,1024,192]{2,1,0:T(8,128)(2,1)}, bf16[2,1024,192]{2,1,0:T(8,128)(2,1)}, bf16[2,1024,192]{2,1,0:T(8,128)(2,1)}) custom-call(s32[4]{0:T(128)} %get-tuple-element.115.lens_ref, ...), custom_call_target="tpu_custom_call", output_to_operand_aliasing={{1}: (6, {}), {2}: (7, {}), {3}: (8, {}), {4}: (9, {})} | custom-call | flops 2063597568 | bytes 2359296 | tf_op jit(solution)/shard_map/attn_forward/pallas_call | solution.py:347
  79.9 5.0 %all-to-all-start.2 = ((bf16[8,1,192,128]{3,2,1,0:T(8,128)(2,1)}), bf16[8,1,192,128]{3,2,1,0:T(8,128)(2,1)S(1)}, u32[]{:S(2)}, u32[]{:S(2)}) async-start(bf16[8,1,192,128]{3,2,1,0:T(8,128)(2,1)} %get-tuple-element.130), calls=%async_computation.2 | async-start | bytes 786432 | tf_op jit(solution)/shard_map/all_to_all | solution.py:1268
  84.9 6.0 %all-to-all-done.2.attn1_ref = bf16[8,1,192,128]{3,2,1,0:T(8,128)(2,1)S(1)} async-done(((bf16[8,1,192,128]{3,2,1,0:T(8,128)(2,1)}), bf16[8,1,192,128]{3,2,1,0:T(8,128)(2,1)S(1)}, u32[]{:S(2)}, u32[]{:S(2)}) %all-to-all-start.2) | async-done | bytes 393248 | tf_op jit(solution)/shard_map/all_to_all | solution.py:1268
  90.9 5.7 %all-to-all-start.1 = ((bf16[8,1,192,128]{3,2,1,0:T(8,128)(2,1)}), bf16[8,1,192,128]{3,2,1,0:T(8,128)(2,1)S(1)}, u32[]{:S(2)}, u32[]{:S(2)}) async-start(bf16[8,1,192,128]{3,2,1,0:T(8,128)(2,1)} %get-tuple-element.124), calls=%async_computation.1 | async-start | bytes 786432 | tf_op jit(solution)/shard_map/all_to_all | solution.py:1268
  96.6 1.4 collective-permute-start.14
  98.9 3.8 all-to-all-done.1.attn0_ref
  103.4 5.0 %out_project.1 = (f32[512,768]{1,0:T(8,128)}, bf16[512,768]{1,0:T(8,128)(2,1)}, bf16[768,768]{1,0:T(8,128)(2,1)}) custom-call(s32[3]{0:T(128)} %pad_add_fusion.where_ref, bf16[512,768]{1,0:T(8,128)(2,1)} %get-tuple-element.116.tok_ref, bf16[8,1,192,128]{3,2,1,0:T(8,128)(2,1)} %copy-done.3, bf16[8,1,192,128]{3,2,1,0:T(8,128)(2,1)} %copy-done.2, ...), custom_call_target="tpu_custom_call" | custom-call | flops 603979776 | bytes 2359296 | tf_op jit(solution)/shard_map/out_project/pallas_call | solution.py:597
  108.4 2.8 collective-permute-start.10
  111.5 6.4 %collective-permute-done.13.y2 = bf16[288,768]{1,0:T(8,128)(2,1)S(1)} collective-permute-done((bf16[288,768]{1,0:T(8,128)(2,1)}, bf16[288,768]{1,0:T(8,128)(2,1)S(1)}, u32[]{:S(2)}, u32[]{:S(2)}) %collective-permute-start.13) | collective-permute-done | bytes 442400 | tf_op jit(solution)/shard_map/ppermute | solution.py:1183
  117.9 1.2 collective-permute-start.19
  119.1 1.2 collective-permute-start.15
  120.3 1.8 collective-permute-done.16.sx3
  122.1 1.2 collective-permute-start.18
  123.4 9.3 %collective-permute-done.19.sy3 = bf16[288,768]{1,0:T(8,128)(2,1)S(1)} collective-permute-done((bf16[288,768]{1,0:T(8,128)(2,1)}, bf16[288,768]{1,0:T(8,128)(2,1)S(1)}, u32[]{:S(2)}, u32[]{:S(2)}) %collective-permute-start.19) | collective-permute-done | bytes 442400 | tf_op jit(solution)/shard_map/ppermute | solution.py:1178
  132.7 9.5 %collective-permute-done.18.sy2 = bf16[288,768]{1,0:T(8,128)(2,1)S(1)} collective-permute-done((bf16[288,768]{1,0:T(8,128)(2,1)S(1)}, bf16[288,768]{1,0:T(8,128)(2,1)S(1)}, u32[]{:S(2)}, u32[]{:S(2)}) %collective-permute-start.18) | collective-permute-done | bytes 442400 | tf_op jit(solution)/shard_map/ppermute | solution.py:1178
  143.3 29.4 %ffn_first.1 = (bf16[1024,1536]{1,0:T(8,128)(2,1)}, bf16[1024,1536]{1,0:T(8,128)(2,1)}, f32[512,768]{1,0:T(8,128)}, bf16[512,768]{1,0:T(8,128)(2,1)}, bf16[1536,...) custom-call(s32[3]{0:T(128)} %pad_add_fusion.where_ref, ...), custom_call_target="tpu_custom_call" | custom-call | flops 14495514624 | bytes 12189696 | tf_op jit(solution)/shard_map/ffn_first/pallas_call | solution.py:783
  172.7 0.9 collective-permute-start.23
  173.6 12.7 %collective-permute-start.22 = (bf16[2,192,768]{2,1,0:T(8,128)(2,1)}, bf16[2,192,768]{2,1,0:T(8,128)(2,1)S(1)}, u32[]{:S(2)}, u32[]{:S(2)}) collective-permute-start(bf16[2,192,768]{2,1,0:T(8,128)(2,1)} %get-tuple-element.146), channel_id=1, source_target_pairs={{0,3},{1,0},{2,1},{3,2},{4,7},{5,4},{6,5},{7,6},{8,11},{9,8},{10,9... | collective-permute-start | bytes 1769480 | tf_op jit(solution)/shard_map/ppermute | solution.py:1183
  186.3 0.9 copy-done.7
  187.2 6.5 %out_back.1 = (bf16[8,2,192,128]{3,2,1,0:T(8,128)(2,1)}, f32[512,768]{1,0:T(8,128)}, f32[1,768]{1,0:T(1,128)}, bf16[4,96,768]{2,1,0:T(8,128)(2,1)}, bf16[4,96,768]{2,1,0:T(8,128)(2,1)}) custom-call(s32[3]{0:T(128)} %pad_add_fusion.where_ref, f32[512,768]{1,0:T(8,128)} %get-tuple-element.149.own_ref, bf16[512,768]{1,0:T(8,128)(2,1)} %copy-done.7, ...), custom_call_target="tpu_custom_call" | custom-call | flops 1207959552 | bytes 3932160 | tf_op jit(solution)/shard_map/out_back/pallas_call | solution.py:646
  193.8 4.1 %all-to-all-start.3 = ((bf16[8,2,192,128]{3,2,1,0:T(8,128)(2,1)}), bf16[8,2,192,128]{3,2,1,0:T(8,128)(2,1)S(1)}, u32[]{:S(2)}, u32[]{:S(2)}) async-start(bf16[8,2,192,128]{3,2,1,0:T(8,128)(2,1)} %get-tuple-element.152), calls=%async_computation.3 | async-start | bytes 1572864 | tf_op jit(solution)/shard_map/all_to_all | solution.py:1285
  197.8 15.8 %ffn_second.1 = (f32[512,768]{1,0:T(8,128)}, bf16[512,768]{1,0:T(8,128)(2,1)}, bf16[4,2,96,768]{3,2,1,0:T(8,128)(2,1)}, bf16[4,2,96,768]{3,2,1,0:T(8,128)(2,1)},...) custom-call(s32[3]{0:T(128)} %pad_add_fusion.where_ref, bf16[512,768]{1,0:T(8,128)(2,1)} %get-tuple-element.132.nf_own_ref, ...), custom_call_target="tpu_custom_call" | custom-call | flops 7247757312 | bytes 13369344 | tf_op jit(solution)/shard_map/ffn_second/pallas_call | solution.py:869
  215.0 1.6 collective-permute-start.24
  216.6 1.2 collective-permute-start.25
  217.9 36.4 %attn_backward.1 = (bf16[8,2,128,768]{3,2,1,0:T(8,128)(2,1)}, bf16[4,96,768]{2,1,0:T(8,128)(2,1)}, bf16[4,96,768]{2,1,0:T(8,128)(2,1)}, f32[1,768]{1,0:T(1,128)}, f32[3,2048]{1,0:T(4,128)}) custom-call(s32[4]{0:T(128)} %get-tuple-element.115.lens_ref, s32[3]{0:T(128)} %pad_add_fusion.where_ref, bf16[8,2,128,768]{3,2,1,0:T(8,128)(2,1)} %copy-done.1, ...), custom_call_target="tpu_custom_call" | custom-call | flops 19730006016 | bytes 7864320 | tf_op jit(solution)/shard_map/attn_backward/pallas_call | solution.py:514
  254.3 1.3 fusion.2
  256.2 4.1 %by_chip.1 = (bf16[192,768]{1,0:T(8,128)(2,1)}, bf16[192,768]{1,0:T(8,128)(2,1)}, bf16[192,768]{1,0:T(8,128)(2,1)}, bf16[192,768]{1,0:T(8,128)(2,1)}) custom-call(s32[3]{0:T(128)} %pad_add_fusion.where_ref, bf16[2,192,768]{2,1,0:T(8,128)(2,1)} %get-tuple-element.181.refs_0_, bf16[2,192,768]{2,1,0:T(8,128)(2,1)} %copy-done.12, ...), custom_call_target="tpu_custom_call" | custom-call | bytes 1500000 | tf_op jit(solution)/shard_map/by_chip/pallas_call | solution.py:966
  260.7 4.3 %second_halves.1 = (bf16[4,2,48,768]{3,2,1,0:T(8,128)(2,1)}, bf16[4,2,48,768]{3,2,1,0:T(8,128)(2,1)}, bf16[4,96,768]{2,1,0:T(8,128)(2,1)}, bf16[4,96,768]{2,1,0:T(8,128)(2,1)}) custom-call(s32[3]{0:T(128)} %pad_add_fusion.where_ref, bf16[4,2,96,768]{3,2,1,0:T(8,128)(2,1)} %get-tuple-element.168.u_keep_ref, bf16[4,2,96,768]{3,2,1,0:T(8,128)(2,1)} %copy-done.4, ...), custom_call_target="tpu_custom_call" | custom-call | bytes 3500000 | tf_op jit(solution)/shard_map/second_halves/pallas_call | solution.py:921
  265.0 1.4 collective-permute-start.28
  267.8 0.9 collective-permute-done.30.refs_7_
  268.8 1.1 collective-permute-start.33
  270.1 16.6 %collective-permute-done.33.refs_10_ = bf16[192,768]{1,0:T(8,128)(2,1)S(1)} collective-permute-done((bf16[192,768]{1,0:T(8,128)(2,1)}, bf16[192,768]{1,0:T(8,128)(2,1)S(1)}, u32[]{:S(2)}, u32[]{:S(2)}) %collective-permute-start.33) | collective-permute-done | bytes 294944 | tf_op jit(solution)/shard_map/ppermute | solution.py:1178
  288.0 3.9 %by_plane.1 = (bf16[304,768]{1,0:T(8,128)(2,1)}, bf16[304,768]{1,0:T(8,128)(2,1)}, bf16[304,768]{1,0:T(8,128)(2,1)}, bf16[304,768]{1,0:T(8,128)(2,1)}, bf16[96,768]{1,0:T(8,128)(2,1)}) custom-call(s32[3]{0:T(128)} %pad_add_fusion.where_ref, bf16[4,2,48,768]{3,2,1,0:T(8,128)(2,1)} %get-tuple-element.172.refs_0_, bf16[4,2,48,768]{3,2,1,0:T(8,128)(2,1)} %copy-done.9, ...), custom_call_target="tpu_custom_call" | custom-call | bytes 3000000 | tf_op jit(solution)/shard_map/by_plane/pallas_call | solution.py:1020
  292.0 3.6 all-to-all-start.4
  295.8 1.4 collective-permute-start.37
  297.2 1.0 collective-permute-done.20.recv_ref
  299.1 4.7 %finish_out.1 = bf16[4,128,768]{2,1,0:T(8,128)(2,1)} custom-call(s32[4]{0:T(128)} %get-tuple-element.114.order_ref, s32[4]{0:T(128)} %get-tuple-element.115.lens_ref, s32[1]{0:T(128)} %bitcast.3.start_ref, f32[512,768]{1,0:T(8,128)} %get-tuple-element.131.res_ref, f32[512,768]{1,0:T(8,128)} %get-tuple-element.143.own_ref, bf16[512,768]{1,0:T(8,128)(2,1)} %copy-done.8), custom_call_target="tpu_custom_call" | custom-call | bytes 3000000 | tf_op jit(solution)/shard_map/finish_out/pallas_call | solution.py:1122
  303.8 4.0 %collective-permute-done.35 = bf16[304,768]{1,0:T(8,128)(2,1)S(1)} collective-permute-done((bf16[304,768]{1,0:T(8,128)(2,1)}, bf16[304,768]{1,0:T(8,128)(2,1)S(1)}, u32[]{:S(2)}, u32[]{:S(2)}) %collective-permute-start.35) | collective-permute-done | bytes 466976 | tf_op jit(solution)/shard_map/ppermute | solution.py:1183
  307.7 28.2 %collective-permute-done.36 = bf16[304,768]{1,0:T(8,128)(2,1)S(1)} collective-permute-done((bf16[304,768]{1,0:T(8,128)(2,1)}, bf16[304,768]{1,0:T(8,128)(2,1)S(1)}, u32[]{:S(2)}, u32[]{:S(2)}) %collective-permute-start.36) | collective-permute-done | bytes 466976 | tf_op jit(solution)/shard_map/ppermute | solution.py:1183
  336.3 0.9 pad_maximum_fusion.refs_0_
  337.2 2.0 collective-permute-start.40
  339.8 13.0 %collective-permute-done.40.refs_3_ = bf16[400,768]{1,0:T(8,128)(2,1)} collective-permute-done((bf16[400,768]{1,0:T(8,128)(2,1)}, bf16[400,768]{1,0:T(8,128)(2,1)}, u32[]{:S(2)}, u32[]{:S(2)}) %collective-permute-start.40) | collective-permute-done | bytes 614432 | tf_op jit(solution)/shard_map/ppermute | solution.py:1178
  352.8 3.4 collective-permute-start.44
  356.2 10.0 %collective-permute-done.38.refs_1_ = bf16[400,768]{1,0:T(8,128)(2,1)} collective-permute-done((bf16[400,768]{1,0:T(8,128)(2,1)}, bf16[400,768]{1,0:T(8,128)(2,1)}, u32[]{:S(2)}, u32[]{:S(2)}) %collective-permute-start.38) | collective-permute-done | bytes 614432 | tf_op jit(solution)/shard_map/ppermute | solution.py:1178
  366.2 1.6 collective-permute-start.42
  367.8 1.6 copy-done
  369.5 5.4 %finish_tokens.1 = f32[4,128,768]{2,1,0:T(8,128)} custom-call(s32[4]{0:T(128)} %get-tuple-element.114.order_ref, bf16[4,4,128,768]{3,2,1,0:T(8,128)(2,1)} %bitcast.9, bf16[512,768]{1,0:T(8,128)(2,1)} %get-tuple-element.116.tok_ref, f32[512,768]{1,0:T(8,128)} %get-tuple-element.196.dres_ref, f32[1,768]{1,0:T(1,128)} %reshape.122.gain_ref), custom_call_target="tpu_custom_call" | custom-call | bytes 5000000 | tf_op jit(solution)/shard_map/finish_tokens/pallas_call | solution.py:1153
  374.9 7.4 %unpack.1 = (f32[192,3072]{1,0:T(8,128)}, f32[192,3072]{1,0:T(8,128)}, f32[768,768]{1,0:T(8,128)}, f32[192,768]{1,0:T(8,128)}, f32[192,768]{1,0:T(8,128)}, /*ind...) custom-call(s32[3]{0:T(128)} %pad_add_fusion.where_ref, bf16[400,768]{1,0:T(8,128)(2,1)} %pad_maximum_fusion.refs_0_, ...), custom_call_target="tpu_custom_call" | custom-call | bytes 12000000 | tf_op jit(solution)/shard_map/unpack/pallas_call | solution.py:1092
  383.0 1.4 fusion.16
  (156 shorter events, 21.8 us)
Async XLA Ops:
  10.5 38.9 %all-to-all-start = ((bf16[8,2,128,768]{3,2,1,0:T(8,128)(2,1)}), bf16[8,2,128,768]{3,2,1,0:T(8,128)(2,1)S(1)}, u32[]{:S(2)}, u32[]{:S(2)}) async-start(bf16[8,2,128,768]{3,2,1,0:T(8,128)(2,1)} %bitcast.10), calls=%async_computation | async-start | bytes 6291456 | tf_op jit(solution)/shard_map/all_to_all | solution.py:1235
  15.0 10.8 %copy-start.21 = (s32[2047]{0:T(1024)S(1)}, s32[2047]{0:T(1024)}, u32[]{:S(2)}) copy-start(s32[2047]{0:T(1024)} %param.17) | copy-start | bytes 24568
  15.0 9.4 %collective-permute-start = (bf16[208,768]{1,0:T(8,128)(2,1)}, bf16[208,768]{1,0:T(8,128)(2,1)}, u32[]{:S(2)}, u32[]{:S(2)}) collective-permute-start(bf16[208,768]{1,0:T(8,128)(2,1)} %get-tuple-element.112), channel_id=1, source_target_pairs={{0,1},{1,2},{2,3},{3,0},{4,5},{5,6},{6,7},{7,4},{8,9},{9,10},{10,1... | collective-permute-start | bytes 958472 | tf_op jit(solution)/shard_map/ppermute | solution.py:1183
  16.3 18.1 %collective-permute-start.2 = (bf16[208,768]{1,0:T(8,128)(2,1)}, bf16[208,768]{1,0:T(8,128)(2,1)}, u32[]{:S(2)}, u32[]{:S(2)}) collective-permute-start(bf16[208,768]{1,0:T(8,128)(2,1)} %get-tuple-element.112), channel_id=1, source_target_pairs={{0,3},{1,0},{2,1},{3,2},{4,7},{5,4},{6,5},{7,6},{8,11},{9,8},{10,9... | collective-permute-start | bytes 958472 | tf_op jit(solution)/shard_map/ppermute | solution.py:1183
  20.7 87.7 %collective-permute-start.11 = (bf16[512,768]{1,0:T(8,128)(2,1)}, bf16[512,768]{1,0:T(8,128)(2,1)}, u32[]{:S(2)}, u32[]{:S(2)}) collective-permute-start(bf16[512,768]{1,0:T(8,128)(2,1)} %get-tuple-element.133.dy_own_ref.dy_ref), channel_id=1, source_target_pairs={{0,4},{4,0},{8,12},{12,8},{16,20},{20,16},{24,28},{28,24},{1,5},{5... | collective-permute-start | bytes 2359304 | tf_op jit(solution)/shard_map/ppermute | solution.py:1178
  24.4 13.6 %collective-permute-start.1 = (bf16[208,768]{1,0:T(8,128)(2,1)}, bf16[208,768]{1,0:T(8,128)(2,1)S(1)}, u32[]{:S(2)}, u32[]{:S(2)}) collective-permute-start(bf16[208,768]{1,0:T(8,128)(2,1)} %collective-permute-done.w1_ref.a1_ref), channel_id=1, source_target_pairs={{0,1},{1,2},{2,3},{3,0},{4,5},{5,6},{6,7},{7,4},{8,9},{9,10},{10,1... | collective-permute-start | bytes 958472 | tf_op jit(solution)/shard_map/ppermute | solution.py:1183
  26.8 15.9 %collective-permute-start.7 = (bf16[208,768]{1,0:T(8,128)(2,1)}, bf16[208,768]{1,0:T(8,128)(2,1)}, u32[]{:S(2)}, u32[]{:S(2)}) collective-permute-start(bf16[208,768]{1,0:T(8,128)(2,1)} %collective-permute-done.w1_ref.a1_ref), channel_id=1, source_target_pairs={{0,4},{4,0},{8,12},{12,8},{16,20},{20,16},{24,28},{28,24},{1,5},{5... | collective-permute-start | bytes 958472 | tf_op jit(solution)/shard_map/ppermute | solution.py:1178
  35.0 8.4 %collective-permute-start.9 = (bf16[208,768]{1,0:T(8,128)(2,1)}, bf16[208,768]{1,0:T(8,128)(2,1)}, u32[]{:S(2)}, u32[]{:S(2)}) collective-permute-start(bf16[208,768]{1,0:T(8,128)(2,1)} %collective-permute-done.2.w3_ref.a3_ref), channel_id=1, source_target_pairs={{0,4},{4,0},{8,12},{12,8},{16,20},{20,16},{24,28},{28,24},{1,5},{5... | collective-permute-start | bytes 958472 | tf_op jit(solution)/shard_map/ppermute | solution.py:1178
  38.9 5.3 %collective-permute-start.8 = (bf16[208,768]{1,0:T(8,128)(2,1)}, bf16[208,768]{1,0:T(8,128)(2,1)}, u32[]{:S(2)}, u32[]{:S(2)}) collective-permute-start(bf16[208,768]{1,0:T(8,128)(2,1)} %copy-done.15), channel_id=1, source_target_pairs={{0,4},{4,0},{8,12},{12,8},{16,20},{20,16},{24,28},{28,24},{1,5},{5... | collective-permute-start | bytes 958472 | tf_op jit(solution)/shard_map/ppermute | solution.py:1178
  40.5 44.4 %collective-permute-start.3 = (bf16[288,768]{1,0:T(8,128)(2,1)}, bf16[288,768]{1,0:T(8,128)(2,1)}, u32[]{:S(2)}, u32[]{:S(2)}) collective-permute-start(bf16[288,768]{1,0:T(8,128)(2,1)} %get-tuple-element.119), channel_id=1, source_target_pairs={{0,1},{1,2},{2,3},{3,0},{4,5},{5,6},{6,7},{7,4},{8,9},{9,10},{10,1... | collective-permute-start | bytes 1327112 | tf_op jit(solution)/shard_map/ppermute | solution.py:1183
  42.7 42.2 %collective-permute-start.5 = (bf16[288,768]{1,0:T(8,128)(2,1)}, bf16[288,768]{1,0:T(8,128)(2,1)}, u32[]{:S(2)}, u32[]{:S(2)}) collective-permute-start(bf16[288,768]{1,0:T(8,128)(2,1)} %get-tuple-element.119), channel_id=1, source_target_pairs={{0,3},{1,0},{2,1},{3,2},{4,7},{5,4},{6,5},{7,6},{8,11},{9,8},{10,9... | collective-permute-start | bytes 1327112 | tf_op jit(solution)/shard_map/ppermute | solution.py:1183
  43.5 41.4 %collective-permute-start.4 = (bf16[288,768]{1,0:T(8,128)(2,1)}, bf16[288,768]{1,0:T(8,128)(2,1)}, u32[]{:S(2)}, u32[]{:S(2)}) collective-permute-start(bf16[288,768]{1,0:T(8,128)(2,1)} %get-tuple-element.120), channel_id=1, source_target_pairs={{0,1},{1,2},{2,3},{3,0},{4,5},{5,6},{6,7},{7,4},{8,9},{9,10},{10,1... | collective-permute-start | bytes 1327112 | tf_op jit(solution)/shard_map/ppermute | solution.py:1183
  44.2 40.7 %collective-permute-start.6 = (bf16[288,768]{1,0:T(8,128)(2,1)}, bf16[288,768]{1,0:T(8,128)(2,1)}, u32[]{:S(2)}, u32[]{:S(2)}) collective-permute-start(bf16[288,768]{1,0:T(8,128)(2,1)} %get-tuple-element.120), channel_id=1, source_target_pairs={{0,3},{1,0},{2,1},{3,2},{4,7},{5,4},{6,5},{7,6},{8,11},{9,8},{10,9... | collective-permute-start | bytes 1327112 | tf_op jit(solution)/shard_map/ppermute | solution.py:1183
  79.9 11.0 %all-to-all-start.2 = ((bf16[8,1,192,128]{3,2,1,0:T(8,128)(2,1)}), bf16[8,1,192,128]{3,2,1,0:T(8,128)(2,1)S(1)}, u32[]{:S(2)}, u32[]{:S(2)}) async-start(bf16[8,1,192,128]{3,2,1,0:T(8,128)(2,1)} %get-tuple-element.130), calls=%async_computation.2 | async-start | bytes 786432 | tf_op jit(solution)/shard_map/all_to_all | solution.py:1268
  90.9 11.7 %copy-start.2 = (bf16[8,1,192,128]{3,2,1,0:T(8,128)(2,1)}, bf16[8,1,192,128]{3,2,1,0:T(8,128)(2,1)S(1)}, u32[]{:S(2)}) copy-start(bf16[8,1,192,128]{3,2,1,0:T(8,128)(2,1)S(1)} %all-to-all-done.2.attn1_ref) | copy-start | bytes 1179652
  90.9 11.7 %all-to-all-start.1 = ((bf16[8,1,192,128]{3,2,1,0:T(8,128)(2,1)}), bf16[8,1,192,128]{3,2,1,0:T(8,128)(2,1)S(1)}, u32[]{:S(2)}, u32[]{:S(2)}) async-start(bf16[8,1,192,128]{3,2,1,0:T(8,128)(2,1)} %get-tuple-element.124), calls=%async_computation.1 | async-start | bytes 786432 | tf_op jit(solution)/shard_map/all_to_all | solution.py:1268
  96.6 14.6 %collective-permute-start.12 = (bf16[288,768]{1,0:T(8,128)(2,1)}, bf16[288,768]{1,0:T(8,128)(2,1)S(1)}, u32[]{:S(2)}, u32[]{:S(2)}) collective-permute-start(bf16[288,768]{1,0:T(8,128)(2,1)} %collective-permute-done.3.x1), channel_id=1, source_target_pairs={{0,1},{1,2},{2,3},{3,0},{4,5},{5,6},{6,7},{7,4},{8,9},{9,10},{10,1... | collective-permute-start | bytes 1327112 | tf_op jit(solution)/shard_map/ppermute | solution.py:1183
  96.6 22.5 %collective-permute-start.14 = (bf16[288,768]{1,0:T(8,128)(2,1)}, bf16[288,768]{1,0:T(8,128)(2,1)S(1)}, u32[]{:S(2)}, u32[]{:S(2)}) collective-permute-start(bf16[288,768]{1,0:T(8,128)(2,1)} %collective-permute-done.3.x1), channel_id=1, source_target_pairs={{0,8},{4,12},{8,0},{12,4},{16,24},{20,28},{24,16},{28,20},{1,9},{5... | collective-permute-start | bytes 1327112 | tf_op jit(solution)/shard_map/ppermute | solution.py:1178
  98.0 19.9 %collective-permute-start.13 = (bf16[288,768]{1,0:T(8,128)(2,1)}, bf16[288,768]{1,0:T(8,128)(2,1)S(1)}, u32[]{:S(2)}, u32[]{:S(2)}) collective-permute-start(bf16[288,768]{1,0:T(8,128)(2,1)} %collective-permute-done.4.y1), channel_id=1, source_target_pairs={{0,1},{1,2},{2,3},{3,0},{4,5},{5,6},{6,7},{7,4},{8,9},{9,10},{10,1... | collective-permute-start | bytes 1327112 | tf_op jit(solution)/shard_map/ppermute | solution.py:1183
  98.0 24.1 %collective-permute-start.16 = (bf16[288,768]{1,0:T(8,128)(2,1)}, bf16[288,768]{1,0:T(8,128)(2,1)S(1)}, u32[]{:S(2)}, u32[]{:S(2)}) collective-permute-start(bf16[288,768]{1,0:T(8,128)(2,1)} %collective-permute-done.5.x3), channel_id=1, source_target_pairs={{0,8},{4,12},{8,0},{12,4},{16,24},{20,28},{24,16},{28,20},{1,9},{5... | collective-permute-start | bytes 1327112 | tf_op jit(solution)/shard_map/ppermute | solution.py:1178
  108.4 33.7 %collective-permute-start.10 = (bf16[512,768]{1,0:T(8,128)(2,1)}, bf16[512,768]{1,0:T(8,128)(2,1)S(1)}, u32[]{:S(2)}, u32[]{:S(2)}) collective-permute-start(bf16[512,768]{1,0:T(8,128)(2,1)} %get-tuple-element.132.nf_own_ref), channel_id=1, source_target_pairs={{0,4},{4,0},{8,12},{12,8},{16,20},{20,16},{24,28},{28,24},{1,5},{5... | collective-permute-start | bytes 2359304 | tf_op jit(solution)/shard_map/ppermute | solution.py:1178
  111.2 30.9 %copy-start.26 = (bf16[288,768]{1,0:T(8,128)(2,1)}, bf16[288,768]{1,0:T(8,128)(2,1)S(1)}, u32[]{:S(2)}) copy-start(bf16[288,768]{1,0:T(8,128)(2,1)S(1)} %collective-permute-done.12.x2) | copy-start | bytes 1327108
  111.2 12.1 %collective-permute-start.17 = (bf16[288,768]{1,0:T(8,128)(2,1)}, bf16[288,768]{1,0:T(8,128)(2,1)S(1)}, u32[]{:S(2)}, u32[]{:S(2)}) collective-permute-start(bf16[288,768]{1,0:T(8,128)(2,1)} %collective-permute-done.4.y1), channel_id=1, source_target_pairs={{0,16},{4,20},{8,24},{12,28},{16,0},{20,4},{24,8},{28,12},{1,17},{... | collective-permute-start | bytes 1327112 | tf_op jit(solution)/shard_map/ppermute | solution.py:1178
  117.9 24.2 %copy-start.28 = (bf16[288,768]{1,0:T(8,128)(2,1)}, bf16[288,768]{1,0:T(8,128)(2,1)S(1)}, u32[]{:S(2)}) copy-start(bf16[288,768]{1,0:T(8,128)(2,1)S(1)} %collective-permute-done.13.y2) | copy-start | bytes 1327108
  117.9 14.7 %collective-permute-start.19 = (bf16[288,768]{1,0:T(8,128)(2,1)}, bf16[288,768]{1,0:T(8,128)(2,1)S(1)}, u32[]{:S(2)}, u32[]{:S(2)}) collective-permute-start(bf16[288,768]{1,0:T(8,128)(2,1)} %collective-permute-done.6.y3), channel_id=1, source_target_pairs={{0,16},{4,20},{8,24},{12,28},{16,0},{20,4},{24,8},{28,12},{1,17},{... | collective-permute-start | bytes 1327112 | tf_op jit(solution)/shard_map/ppermute | solution.py:1178
  119.1 23.1 %copy-start.27 = (bf16[288,768]{1,0:T(8,128)(2,1)}, bf16[288,768]{1,0:T(8,128)(2,1)S(1)}, u32[]{:S(2)}) copy-start(bf16[288,768]{1,0:T(8,128)(2,1)S(1)} %collective-permute-done.14.sx1) | copy-start | bytes 1327108
  119.1 13.6 %collective-permute-start.15 = (bf16[288,768]{1,0:T(8,128)(2,1)S(1)}, bf16[288,768]{1,0:T(8,128)(2,1)S(1)}, u32[]{:S(2)}, u32[]{:S(2)}) collective-permute-start(bf16[288,768]{1,0:T(8,128)(2,1)S(1)} %collective-permute-done.12.x2), channel_id=1, source_target_pairs={{0,8},{4,12},{8,0},{12,4},{16,24},{20,28},{24,16},{28,20},{1,9},{5... | collective-permute-start | bytes 1327112 | tf_op jit(solution)/shard_map/ppermute | solution.py:1178
  122.1 20.0 %copy-start.29 = (bf16[288,768]{1,0:T(8,128)(2,1)}, bf16[288,768]{1,0:T(8,128)(2,1)S(1)}, u32[]{:S(2)}) copy-start(bf16[288,768]{1,0:T(8,128)(2,1)S(1)} %collective-permute-done.16.sx3) | copy-start | bytes 1327108
  122.1 20.0 %collective-permute-start.18 = (bf16[288,768]{1,0:T(8,128)(2,1)S(1)}, bf16[288,768]{1,0:T(8,128)(2,1)S(1)}, u32[]{:S(2)}, u32[]{:S(2)}) collective-permute-start(bf16[288,768]{1,0:T(8,128)(2,1)S(1)} %collective-permute-done.13.y2), channel_id=1, source_target_pairs={{0,16},{4,20},{8,24},{12,28},{16,0},{20,4},{24,8},{28,12},{1,17},{... | collective-permute-start | bytes 1327112 | tf_op jit(solution)/shard_map/ppermute | solution.py:1178
  123.4 18.8 %copy-start.30 = (bf16[288,768]{1,0:T(8,128)(2,1)}, bf16[288,768]{1,0:T(8,128)(2,1)S(1)}, u32[]{:S(2)}) copy-start(bf16[288,768]{1,0:T(8,128)(2,1)S(1)} %collective-permute-done.17.sy1) | copy-start | bytes 1327108
  132.6 9.5 %copy-start.31 = (bf16[288,768]{1,0:T(8,128)(2,1)}, bf16[288,768]{1,0:T(8,128)(2,1)S(1)}, u32[]{:S(2)}) copy-start(bf16[288,768]{1,0:T(8,128)(2,1)S(1)} %collective-permute-done.19.sy3) | copy-start | bytes 1327108
  132.7 9.5 %copy-start.32 = (bf16[288,768]{1,0:T(8,128)(2,1)}, bf16[288,768]{1,0:T(8,128)(2,1)S(1)}, u32[]{:S(2)}) copy-start(bf16[288,768]{1,0:T(8,128)(2,1)S(1)} %collective-permute-done.15.sx2) | copy-start | bytes 1327108
  172.7 13.6 %collective-permute-start.23 = (bf16[512,768]{1,0:T(8,128)(2,1)}, bf16[512,768]{1,0:T(8,128)(2,1)S(1)}, u32[]{:S(2)}, u32[]{:S(2)}) collective-permute-start(bf16[512,768]{1,0:T(8,128)(2,1)} %get-tuple-element.150), channel_id=1, source_target_pairs={{0,4},{4,0},{8,12},{12,8},{16,20},{20,16},{24,28},{28,24},{1,5},{5... | collective-permute-start | bytes 2359304 | tf_op jit(solution)/shard_map/ppermute | solution.py:1178
  173.6 40.3 %collective-permute-start.21 = (bf16[2,192,768]{2,1,0:T(8,128)(2,1)}, bf16[2,192,768]{2,1,0:T(8,128)(2,1)S(1)}, u32[]{:S(2)}, u32[]{:S(2)}) collective-permute-start(bf16[2,192,768]{2,1,0:T(8,128)(2,1)} %get-tuple-element.145), channel_id=1, source_target_pairs={{0,1},{1,2},{2,3},{3,0},{4,5},{5,6},{6,7},{7,4},{8,9},{9,10},{10,1... | collective-permute-start | bytes 1769480 | tf_op jit(solution)/shard_map/ppermute | solution.py:1183
  173.6 40.3 %collective-permute-start.22 = (bf16[2,192,768]{2,1,0:T(8,128)(2,1)}, bf16[2,192,768]{2,1,0:T(8,128)(2,1)S(1)}, u32[]{:S(2)}, u32[]{:S(2)}) collective-permute-start(bf16[2,192,768]{2,1,0:T(8,128)(2,1)} %get-tuple-element.146), channel_id=1, source_target_pairs={{0,3},{1,0},{2,1},{3,2},{4,7},{5,4},{6,5},{7,6},{8,11},{9,8},{10,9... | collective-permute-start | bytes 1769480 | tf_op jit(solution)/shard_map/ppermute | solution.py:1183
  186.3 69.8 %collective-permute-start.26 = (bf16[2,192,768]{2,1,0:T(8,128)(2,1)}, bf16[2,192,768]{2,1,0:T(8,128)(2,1)}, u32[]{:S(2)}, u32[]{:S(2)}) collective-permute-start(bf16[2,192,768]{2,1,0:T(8,128)(2,1)} %get-tuple-element.165), channel_id=1, source_target_pairs={{0,2},{1,3},{2,0},{3,1},{4,6},{5,7},{6,4},{7,5},{8,10},{9,11},{10,... | collective-permute-start | bytes 1769480 | tf_op jit(solution)/shard_map/ppermute | solution.py:1183
  193.8 20.2 %all-to-all-start.3 = ((bf16[8,2,192,128]{3,2,1,0:T(8,128)(2,1)}), bf16[8,2,192,128]{3,2,1,0:T(8,128)(2,1)S(1)}, u32[]{:S(2)}, u32[]{:S(2)}) async-start(bf16[8,2,192,128]{3,2,1,0:T(8,128)(2,1)} %get-tuple-element.152), calls=%async_computation.3 | async-start | bytes 1572864 | tf_op jit(solution)/shard_map/all_to_all | solution.py:1285
  197.8 16.0 %copy-start.23 = (f32[1,768]{1,0:T(1,128)S(1)}, f32[1,768]{1,0:T(1,128)}, u32[]{:S(2)}) copy-start(f32[1,768]{1,0:T(1,128)} %get-tuple-element.179) | copy-start | bytes 9220
  213.6 42.6 %collective-permute-start.31 = (bf16[4,96,768]{2,1,0:T(8,128)(2,1)}, bf16[4,96,768]{2,1,0:T(8,128)(2,1)}, u32[]{:S(2)}, u32[]{:S(2)}) collective-permute-start(bf16[4,96,768]{2,1,0:T(8,128)(2,1)} %get-tuple-element.186), channel_id=1, source_target_pairs={{0,4},{4,0},{8,12},{12,8},{16,20},{20,16},{24,28},{28,24},{1,5},{5... | collective-permute-start | bytes 1769480 | tf_op jit(solution)/shard_map/ppermute | solution.py:1178
  215.0 41.1 %collective-permute-start.24 = (bf16[4,2,96,768]{3,2,1,0:T(8,128)(2,1)}, bf16[4,2,96,768]{3,2,1,0:T(8,128)(2,1)S(1)}, u32[]{:S(2)}, u32[]{:S(2)}) collective-permute-start(bf16[4,2,96,768]{3,2,1,0:T(8,128)(2,1)} %get-tuple-element.153), channel_id=1, source_target_pairs={{0,8},{4,12},{8,0},{12,4},{16,24},{20,28},{24,16},{28,20},{1,9},{5... | collective-permute-start | bytes 3538952 | tf_op jit(solution)/shard_map/ppermute | solution.py:1178
  216.6 39.5 %collective-permute-start.25 = (bf16[4,192,768]{2,1,0:T(8,128)(2,1)}, bf16[4,192,768]{2,1,0:T(8,128)(2,1)S(1)}, u32[]{:S(2)}, u32[]{:S(2)}) collective-permute-start(bf16[4,192,768]{2,1,0:T(8,128)(2,1)} %get-tuple-element.154), channel_id=1, source_target_pairs={{0,16},{4,20},{8,24},{12,28},{16,0},{20,4},{24,8},{28,12},{1,17},{... | collective-permute-start | bytes 3538952 | tf_op jit(solution)/shard_map/ppermute | solution.py:1178
  260.2 9.6 %collective-permute-start.32 = (bf16[192,768]{1,0:T(8,128)(2,1)}, bf16[192,768]{1,0:T(8,128)(2,1)S(1)}, u32[]{:S(2)}, u32[]{:S(2)}) collective-permute-start(bf16[192,768]{1,0:T(8,128)(2,1)} %get-tuple-element.188), channel_id=1, source_target_pairs={{0,8},{4,12},{8,0},{12,4},{16,24},{20,28},{24,16},{28,20},{1,9},{5... | collective-permute-start | bytes 884744 | tf_op jit(solution)/shard_map/ppermute | solution.py:1178
  265.0 21.6 %collective-permute-start.27 = (bf16[4,2,48,768]{3,2,1,0:T(8,128)(2,1)}, bf16[4,2,48,768]{3,2,1,0:T(8,128)(2,1)S(1)}, u32[]{:S(2)}, u32[]{:S(2)}) collective-permute-start(bf16[4,2,48,768]{3,2,1,0:T(8,128)(2,1)} %get-tuple-element.173), channel_id=1, source_target_pairs={{0,16},{4,20},{8,24},{12,28},{16,0},{20,4},{24,8},{28,12},{1,17},{... | collective-permute-start | bytes 1769480 | tf_op jit(solution)/shard_map/ppermute | solution.py:1178
  265.0 21.6 %collective-permute-start.28 = (bf16[4,96,768]{2,1,0:T(8,128)(2,1)}, bf16[4,96,768]{2,1,0:T(8,128)(2,1)S(1)}, u32[]{:S(2)}, u32[]{:S(2)}) collective-permute-start(bf16[4,96,768]{2,1,0:T(8,128)(2,1)} %get-tuple-element.175), channel_id=1, source_target_pairs={{0,8},{4,12},{8,0},{12,4},{16,24},{20,28},{24,16},{28,20},{1,9},{5... | collective-permute-start | bytes 1769480 | tf_op jit(solution)/shard_map/ppermute | solution.py:1178
  266.5 20.2 %collective-permute-start.29 = (bf16[4,96,768]{2,1,0:T(8,128)(2,1)S(1)}, bf16[4,96,768]{2,1,0:T(8,128)(2,1)S(1)}, u32[]{:S(2)}, u32[]{:S(2)}) collective-permute-start(bf16[4,96,768]{2,1,0:T(8,128)(2,1)S(1)} %copy-done.25), channel_id=1, source_target_pairs={{0,4},{4,0},{8,12},{12,8},{16,20},{20,16},{24,28},{28,24},{1,5},{5... | collective-permute-start | bytes 1769480 | tf_op jit(solution)/shard_map/ppermute | solution.py:1178
  267.3 1.4 collective-permute-start.30
  268.8 17.9 %copy-start.20 = (bf16[4,16,768]{2,1,0:T(8,128)(2,1)}, bf16[4,16,768]{2,1,0:T(8,128)(2,1)S(1)}, u32[]{:S(2)}) copy-start(bf16[4,16,768]{2,1,0:T(8,128)(2,1)S(1)} %collective-permute-done.30.refs_7_) | copy-start | bytes 294916
  268.8 17.9 %collective-permute-start.33 = (bf16[192,768]{1,0:T(8,128)(2,1)}, bf16[192,768]{1,0:T(8,128)(2,1)S(1)}, u32[]{:S(2)}, u32[]{:S(2)}) collective-permute-start(bf16[192,768]{1,0:T(8,128)(2,1)} %get-tuple-element.189), channel_id=1, source_target_pairs={{0,16},{4,20},{8,24},{12,28},{16,0},{20,4},{24,8},{28,12},{1,17},{... | collective-permute-start | bytes 884744 | tf_op jit(solution)/shard_map/ppermute | solution.py:1178
  269.8 16.9 %copy-start.16 = (bf16[192,768]{1,0:T(8,128)(2,1)}, bf16[192,768]{1,0:T(8,128)(2,1)S(1)}, u32[]{:S(2)}) copy-start(bf16[192,768]{1,0:T(8,128)(2,1)S(1)} %collective-permute-done.32.refs_9_) | copy-start | bytes 884740
  269.8 16.8 %collective-permute-start.34 = (bf16[192,768]{1,0:T(8,128)(2,1)S(1)}, bf16[192,768]{1,0:T(8,128)(2,1)S(1)}, u32[]{:S(2)}, u32[]{:S(2)}) collective-permute-start(bf16[192,768]{1,0:T(8,128)(2,1)S(1)} %copy-done.34), channel_id=1, source_target_pairs={{0,24},{4,28},{8,16},{12,20},{16,8},{20,12},{24,0},{28,4},{1,25},{... | collective-permute-start | bytes 884744 | tf_op jit(solution)/shard_map/ppermute | solution.py:1178
  292.0 75.9 %all-to-all-start.4 = ((bf16[8,2,128,768]{3,2,1,0:T(8,128)(2,1)}), bf16[8,2,128,768]{3,2,1,0:T(8,128)(2,1)S(1)}, u32[]{:S(2)}, u32[]{:S(2)}) async-start(bf16[8,2,128,768]{3,2,1,0:T(8,128)(2,1)} %get-tuple-element.195), calls=%async_computation.4 | async-start | bytes 6291456 | tf_op jit(solution)/shard_map/all_to_all | solution.py:1331
  295.6 2.6 collective-permute-start.20
  295.6 12.1 %collective-permute-start.35 = (bf16[304,768]{1,0:T(8,128)(2,1)}, bf16[304,768]{1,0:T(8,128)(2,1)S(1)}, u32[]{:S(2)}, u32[]{:S(2)}) collective-permute-start(bf16[304,768]{1,0:T(8,128)(2,1)} %get-tuple-element.199), channel_id=1, source_target_pairs={{0,1},{1,2},{2,3},{3,0},{4,5},{5,6},{6,7},{7,4},{8,9},{9,10},{10,1... | collective-permute-start | bytes 1400840 | tf_op jit(solution)/shard_map/ppermute | solution.py:1183
  295.7 40.3 %collective-permute-start.36 = (bf16[304,768]{1,0:T(8,128)(2,1)}, bf16[304,768]{1,0:T(8,128)(2,1)S(1)}, u32[]{:S(2)}, u32[]{:S(2)}) collective-permute-start(bf16[304,768]{1,0:T(8,128)(2,1)} %get-tuple-element.200), channel_id=1, source_target_pairs={{0,2},{1,3},{2,0},{3,1},{4,6},{5,7},{6,4},{7,5},{8,10},{9,11},{10,... | collective-permute-start | bytes 1400840 | tf_op jit(solution)/shard_map/ppermute | solution.py:1183
  295.8 40.2 %collective-permute-start.37 = (bf16[304,768]{1,0:T(8,128)(2,1)}, bf16[304,768]{1,0:T(8,128)(2,1)S(1)}, u32[]{:S(2)}, u32[]{:S(2)}) collective-permute-start(bf16[304,768]{1,0:T(8,128)(2,1)} %get-tuple-element.201), channel_id=1, source_target_pairs={{0,3},{1,0},{2,1},{3,2},{4,7},{5,4},{6,5},{7,6},{8,11},{9,8},{10,9... | collective-permute-start | bytes 1400840 | tf_op jit(solution)/shard_map/ppermute | solution.py:1183
  299.1 36.9 %copy-start.14 = (bf16[304,768]{1,0:T(8,128)(2,1)S(1)}, bf16[304,768]{1,0:T(8,128)(2,1)}, u32[]{:S(2)}) copy-start(bf16[304,768]{1,0:T(8,128)(2,1)} %get-tuple-element.198) | copy-start | bytes 1400836
  303.8 32.5 %copy-start.19 = (bf16[96,768]{1,0:T(8,128)(2,1)S(1)}, bf16[96,768]{1,0:T(8,128)(2,1)}, u32[]{:S(2)}) copy-start(bf16[96,768]{1,0:T(8,128)(2,1)} %get-tuple-element.197) | copy-start | bytes 442372
  337.2 15.7 %collective-permute-start.40 = (bf16[400,768]{1,0:T(8,128)(2,1)}, bf16[400,768]{1,0:T(8,128)(2,1)}, u32[]{:S(2)}, u32[]{:S(2)}) collective-permute-start(bf16[400,768]{1,0:T(8,128)(2,1)} %pad_maximum_fusion.refs_0_), channel_id=1, source_target_pairs={{0,24},{4,28},{8,16},{12,20},{16,8},{20,12},{24,0},{28,4},{1,25},{... | collective-permute-start | bytes 1843208 | tf_op jit(solution)/shard_map/ppermute | solution.py:1178
  339.1 27.0 %collective-permute-start.38 = (bf16[400,768]{1,0:T(8,128)(2,1)}, bf16[400,768]{1,0:T(8,128)(2,1)}, u32[]{:S(2)}, u32[]{:S(2)}) collective-permute-start(bf16[400,768]{1,0:T(8,128)(2,1)} %pad_maximum_fusion.refs_0_), channel_id=1, source_target_pairs={{0,8},{4,12},{8,0},{12,4},{16,24},{20,28},{24,16},{28,20},{1,9},{5... | collective-permute-start | bytes 1843208 | tf_op jit(solution)/shard_map/ppermute | solution.py:1178
  339.4 28.3 %collective-permute-start.39 = (bf16[400,768]{1,0:T(8,128)(2,1)}, bf16[400,768]{1,0:T(8,128)(2,1)}, u32[]{:S(2)}, u32[]{:S(2)}) collective-permute-start(bf16[400,768]{1,0:T(8,128)(2,1)} %pad_maximum_fusion.refs_0_), channel_id=1, source_target_pairs={{0,16},{4,20},{8,24},{12,28},{16,0},{20,4},{24,8},{28,12},{1,17},{... | collective-permute-start | bytes 1843208 | tf_op jit(solution)/shard_map/ppermute | solution.py:1178
  352.8 22.1 %collective-permute-start.44 = (bf16[400,768]{1,0:T(8,128)(2,1)}, bf16[400,768]{1,0:T(8,128)(2,1)}, u32[]{:S(2)}, u32[]{:S(2)}) collective-permute-start(bf16[400,768]{1,0:T(8,128)(2,1)} %collective-permute-done.40.refs_3_), channel_id=1, source_target_pairs={{0,4},{4,0},{8,12},{12,8},{16,20},{20,16},{24,28},{28,24},{1,5},{5... | collective-permute-start | bytes 1843208 | tf_op jit(solution)/shard_map/ppermute | solution.py:1178
  356.2 18.7 %collective-permute-start.41 = (bf16[400,768]{1,0:T(8,128)(2,1)}, bf16[400,768]{1,0:T(8,128)(2,1)}, u32[]{:S(2)}, u32[]{:S(2)}) collective-permute-start(bf16[400,768]{1,0:T(8,128)(2,1)} %pad_maximum_fusion.refs_0_), channel_id=1, source_target_pairs={{0,4},{4,0},{8,12},{12,8},{16,20},{20,16},{24,28},{28,24},{1,5},{5... | collective-permute-start | bytes 1843208 | tf_op jit(solution)/shard_map/ppermute | solution.py:1178
  366.2 8.7 %collective-permute-start.42 = (bf16[400,768]{1,0:T(8,128)(2,1)}, bf16[400,768]{1,0:T(8,128)(2,1)}, u32[]{:S(2)}, u32[]{:S(2)}) collective-permute-start(bf16[400,768]{1,0:T(8,128)(2,1)} %collective-permute-done.38.refs_1_), channel_id=1, source_target_pairs={{0,4},{4,0},{8,12},{12,8},{16,20},{20,16},{24,28},{28,24},{1,5},{5... | collective-permute-start | bytes 1843208 | tf_op jit(solution)/shard_map/ppermute | solution.py:1178
  367.8 7.1 %collective-permute-start.43 = (bf16[400,768]{1,0:T(8,128)(2,1)}, bf16[400,768]{1,0:T(8,128)(2,1)}, u32[]{:S(2)}, u32[]{:S(2)}) collective-permute-start(bf16[400,768]{1,0:T(8,128)(2,1)} %collective-permute-done.39.refs_2_), channel_id=1, source_target_pairs={{0,4},{4,0},{8,12},{12,8},{16,20},{20,16},{24,28},{28,24},{1,5},{5... | collective-permute-start | bytes 1843208 | tf_op jit(solution)/shard_map/ppermute | solution.py:1178
  (21 other events, 48.2 us)
where the time goes:
time: 387 us; the launch traced here: 385 us
  Pallas kernels  163 us (42%)
  waiting for transfers between devices  118 us (30%)
  starting transfers between devices  77.8 us (20%)
  local copies, waits for them, and re-layouts  18.5 us (5%)
    ppermute x30, waiting for transfers between devices, swap(): return lax.ppermute(values, 'ctx', [(i, i ^ bits) for i in range(count)])  62.2 us
    ppermute x15, waiting for transfers between devices, shift(): lax.ppermute(values, 'fsdp', [(i, (i + places) % count) for i in range(co...  43.9 us
    pallas_call x1, Pallas kernels, attn_backward(): pl.pallas_call(attn_backward_kernel, grid=(slots,), in_specs=[SMEM, SMEM,...  36.4 us
    ppermute x30, starting transfers between devices, swap(): return lax.ppermute(values, 'ctx', [(i, i ^ bits) for i in range(count)])  32.6 us
    pallas_call x1, Pallas kernels, ffn_first(): pl.pallas_call(ffn_first_kernel, grid=(units // tile,), in_specs=[SMEM, w...  29.4 us
    pallas_call x2, Pallas kernels, attn_forward(): pl.pallas_call(attn_forward_first_kernel if slot == 0 else attn_forward_s...  28.8 us
    ppermute x15, starting transfers between devices, shift(): lax.ppermute(values, 'fsdp', [(i, (i + places) % count) for i in range(co...  22.4 us
    pallas_call x1, Pallas kernels, ffn_second(): pl.pallas_call(ffn_second_kernel, grid=(units // tile,), in_specs=[SMEM,...  15.8 us
  transfers between devices with their start and end apart: 50, of which 16 were waited for; matrix products, arithmetic and copies ran while one was open for 2% of the time, Pallas kernels for 29%

commit v1 on v0

--- a/solution.py
+++ b/solution.py
@@ -662,13 +662,10 @@
 
 
 def gate_and_slope(gate):
-    inner = 0.7978845608028654 * (gate + 0.044715 * gate * gate * gate)
-    bent = jnp.tanh(inner)
-    half = 0.5 * (1.0 + bent)
-    slope = half + 0.5 * gate * (1.0 - bent * bent) * (
-        0.7978845608028654 * (1.0 + 3.0 * 0.044715 * gate * gate)
-    )
-    return gate * half, slope
+    square = gate * gate
+    half = 0.5 + 0.5 * jnp.tanh(gate * (0.7978845608028654 + 0.035677408136300125 * square))
+    turn = gate * (1.5957691216057308 + 0.21406444881780075 * square)
+    return gate * half, half * (1.0 + (1.0 - half) * turn)
 
 
 def ffn_first_kernel(
@@ -689,19 +686,16 @@
     part = units // planes
     quarter = part // 4
 
-    @pl.when(step == 0)
-    def _():
+    def all_copies():
         copies = []
 
-        def copy(source, target):
-            started = pltpu.make_async_copy(source, target, sems.at[len(copies)])
-            started.start()
-            copies.append(started)
+        def copy(source, target, late=False):
+            copies.append(((source, target, sems.at[len(copies)]), late))
 
         own_rows = pl.ds(pl.multiple_of(plane * depth, depth), depth)
         for index in range(wide):
-            copy(gate_own.at[index], gate_ref.at[index, own_rows, :])
-            copy(up_own.at[index], up_ref.at[index, own_rows, :])
+            copy(gate_own.at[index], gate_ref.at[index, own_rows, :], index > 0)
+            copy(up_own.at[index], up_ref.at[index, own_rows, :], index > 0)
         copy(
             down_own.at[pl.ds(pl.multiple_of(core * part, part), part), :],
             down_ref.at[pl.ds(pl.multiple_of(plane * part, part), part), :],
@@ -718,6 +712,7 @@
                         copy(
                             piece.at[pl.ds(index * slab, slab), :],
                             weight_ref.at[index, at, :],
+                            index > 0,
                         )
                     copy(
                         piece.at[pl.ds(wide * slab, quarter), :],
@@ -731,6 +726,15 @@
                             :,
                         ],
                     )
+        return copies
+
+    @pl.when(step == 0)
+    def _():
+        copies = all_copies()
+        for late_turn in (False, True):
+            for copied, late in copies:
+                if late == late_turn:
+                    pltpu.make_async_copy(*copied).start()
         nf_ref[:half, :] = nf_own_ref[...]
         nf_ref[half:, :] = nf_other_ref[...]
         nft_ref[:, :half] = jnp.transpose(nf_own_ref[...])
@@ -738,21 +742,37 @@
         dy_ref[:half, :] = dy_own_ref[...]
         dy_ref[half:, :] = dy_other_ref[...]
         total_ref[...] = jnp.zeros_like(total_ref)
-        for started in copies:
-            started.wait()
+        for copied, late in copies:
+            if not late:
+                pltpu.make_async_copy(*copied).wait()
 
     per = model // tile
+
+    @pl.when(step == per)
+    def _():
+        for copied, late in all_copies():
+            if late:
+                pltpu.make_async_copy(*copied).wait()
+
     index = step // per
     lanes = pl.ds(pl.multiple_of(lax.rem(step, per) * tile, tile), tile)
     gate_w = gate_ref[index, :, lanes]
     up_w = up_ref[index, :, lanes]
     down_w = down_ref[block_rows(step, tile), :]
-    for quarter_rows in range(4):
-        rows = slice(quarter_rows * half // 2, (quarter_rows + 1) * half // 2)
+    count = 4
+    size = 2 * half // count
+
+    def products(part):
+        rows = slice(part * size, (part + 1) * size)
         nf = nf_ref[rows, :]
-        gate = dot(nf, gate_w)
-        up = dot(nf, up_w)
-        dhidden = dot(dy_ref[rows, :], down_w, NT)
+        return dot(nf, gate_w), dot(nf, up_w), dot(dy_ref[rows, :], down_w, NT)
+
+    ahead = products(0)
+    for part in range(count):
+        rows = slice(part * size, (part + 1) * size)
+        gate, up, dhidden = ahead
+        if part + 1 < count:
+            ahead = products(part + 1)
         bent, slope = gate_and_slope(gate)
         hidden_ref[rows, :] = (bent * up).astype(LOW)
         dgate = (dhidden * up * slope).astype(LOW)
@@ -1237,9 +1257,8 @@
     near, far = column_ends(early_piece)
     early = [near, shift(near, 1), far]
     early_others = [swap(piece, CORE) for piece in early]
-    x_piece, y_piece, *_ = lax.optimization_barrier((x_piece, y_piece, *early))
-    x_near, x_far = column_ends(x_piece)
-    y_near, y_far = column_ends(y_piece)
+    x_near, x_far = column_ends(after(x_piece, near, far))
+    y_near, y_far = column_ends(after(y_piece, *early))
 
     by_distance = jnp.stack([piece[depth] for piece in [early_piece] + early])
     all_small = jnp.stack([pick(by_distance, (plane + planes - i) % planes, 0) for i in range(planes)])
@@ -1256,22 +1275,25 @@
     first_out, *kept, w_qkv = attn_forward(
         0, lens, where, gathered, full_gain_attn, [qkv_mine, *early, *early_others], offsets
     )
-    x_near, y_near, x_far, y_far, first_out = lax.optimization_barrier(
-        (x_near, y_near, x_far, y_far, first_out)
-    )
+    x_near, y_near, first_out = lax.optimization_barrier((x_near, y_near, first_out))
     x_found = [x_near, shift(x_near, 1), x_far]
     y_found = [y_near, shift(y_near, 1), y_far]
-    x_swapped, y_swapped = [swap(t, X) for t in x_found], [swap(t, Y) for t in y_found]
     second_out, *kept = attn_forward(
         1, lens, where, gathered, full_gain_attn, [w_qkv], offsets, kept
     )
-    attn = [lax.all_to_all(part, "ctx", 0, 0) for part in (first_out, second_out)]
+    attn_first = lax.all_to_all(first_out, "ctx", 0, 0)
+    second_out, attn_first, x_found[2], y_found[2], *_ = lax.optimization_barrier(
+        (second_out, attn_first, x_found[2], y_found[2], x_near, y_near)
+    )
+    attn = [attn_first, lax.all_to_all(second_out, "ctx", 0, 0)]
+    x_swapped, y_swapped = [swap(t, X) for t in x_found], [swap(t, Y) for t in y_found]
+    attn[1] = after(attn[1], *x_swapped, *y_swapped)
     attn_full, query, key, value = kept
     flat, dy = sort_rows(order, lens, start, tokens, cotangent)
     residual, nf_own, full_out = out_project(
         where, flat, attn, w_out, early, early_others, full_gain_ffn
     )
-    dy_other = swap(dy, CORE)
+    dy_other = swap(after(dy, nf_own), CORE)
     nf_other = swap(nf_own, CORE)
     hidden, dup, dnf_own, dnf_send, full_down, *g_picks = ffn_first(
         where, nf_own, nf_other, dy, dy_other, (gate_mine, up_mine, w_ffn_out),

time: 387 us -> 378 us (0.977); the launches traced: 385 us -> 372 us
  Pallas kernels: 163 us -> 152 us
    ppermute x30, waiting for transfers between devices: 62.2 us -> 50.4 us  [swap(): return lax.ppermute(values, 'ctx', [(i, i ^ bits) for i in range(count)])]
    all_to_all x2, waiting for transfers between devices: 9.76 us -> 18.9 us  [the longest x1 18.9 us: per_device_plane(): attn = [attn_first, lax.all_to_all(second_out, 'ctx', 0, 0)]]
    ppermute x15, starting transfers between devices: 22.4 us -> 13.8 us  [shift(): lax.ppermute(values, 'fsdp', [(i, (i + places) % count) for i in range(co...]
    all_to_all x2, starting transfers between devices: 10.7 us -> 17.7 us  [the longest x1 12.6 us: per_device_plane(): attn_first = lax.all_to_all(first_out, 'ctx', 0, 0)]
    pallas_call x2, Pallas kernels: 28.8 us -> 22.5 us  [attn_forward(): pl.pallas_call(attn_forward_first_kernel if slot == 0 else attn_forward_s...]
    ppermute x15, waiting for transfers between devices: 43.9 us -> 49.3 us  [shift(): lax.ppermute(values, 'fsdp', [(i, (i + places) % count) for i in range(co...]
    unnamed x70 -> x68, local copies, waits for them, and re-layouts: 10.1 us -> 9.81 us
  transfers between devices with their start and end apart: 50 -> 50, of which waited for: 16 -> 14; matrix products, arithmetic and copies ran while one was open for 2% -> 2% of each run, Pallas kernels for 29% -> 27%
where the time goes in v1:
time: 378 us; the launch traced here: 372 us
  Pallas kernels  152 us (40%)
  waiting for transfers between devices  119 us (31%)
  starting transfers between devices  75 us (20%)
  local copies, waits for them, and re-layouts  18.2 us (5%)
  other arithmetic  3.81 us (1%)
    ppermute x30, waiting for transfers between devices, swap(): return lax.ppermute(values, 'ctx', [(i, i ^ bits) for i in range(count)])  50.4 us
    ppermute x15, waiting for transfers between devices, shift(): lax.ppermute(values, 'fsdp', [(i, (i + places) % count) for i in range(co...  49.3 us
    pallas_call x1, Pallas kernels, attn_backward(): pl.pallas_call(attn_backward_kernel, grid=(slots,), in_specs=[SMEM, SMEM,...  35.5 us
    ppermute x30, starting transfers between devices, swap(): return lax.ppermute(values, 'ctx', [(i, i ^ bits) for i in range(count)])  31.2 us
    pallas_call x1, Pallas kernels, ffn_first(): pl.pallas_call(ffn_first_kernel, grid=(units // tile,), in_specs=[SMEM, w...  25.7 us
    pallas_call x2, Pallas kernels, attn_forward(): pl.pallas_call(attn_forward_first_kernel if slot == 0 else attn_forward_s...  22.5 us
    all_to_all x1, waiting for transfers between devices, per_device_plane(): attn = [attn_first, lax.all_to_all(second_out, 'ctx', 0, 0)]  18.9 us
    pallas_call x1, Pallas kernels, ffn_second(): pl.pallas_call(ffn_second_kernel, grid=(units // tile,), in_specs=[SMEM,...  15.8 us
  transfers between devices with their start and end apart: 50, of which 14 were waited for; matrix products, arithmetic and copies ran while one was open for 2% of the time, Pallas kernels for 27%

profile of v1, /device:TPU:9, one launch (start us, length us, event | category | flops | bytes accessed | tf_op | source)
XLA Modules:
  0.0 371.6 jit_solution(7138796246291250264)
XLA Ops:
  3.5 4.1 %pack_weights.1 = (bf16[2,192,768]{2,1,0:T(8,128)(2,1)}, bf16[2,192,768]{2,1,0:T(8,128)(2,1)}, bf16[288,768]{1,0:T(8,128)(2,1)}, bf16[288,768]{1,0:T(8,128)(2,1)...) custom-call(s32[3]{0:T(128)} %pad_add_fusion.where_ref, bf16[192,3072]{1,0:T(8,128)(2,1)} %gate_ref.1, ...), custom_call_target="tpu_custom_call" | custom-call | bytes 8000000 | tf_op jit(solution)/shard_map/pack_weights/pallas_call | solution.py:102
  7.5 3.0 prepare.1
  10.6 4.4 %all-to-all-start = ((bf16[8,2,128,768]{3,2,1,0:T(8,128)(2,1)}), bf16[8,2,128,768]{3,2,1,0:T(8,128)(2,1)S(1)}, u32[]{:S(2)}, u32[]{:S(2)}) async-start(bf16[8,2,128,768]{3,2,1,0:T(8,128)(2,1)} %bitcast.10), calls=%async_computation | async-start | bytes 6291456 | tf_op jit(solution)/shard_map/all_to_all | solution.py:1255
  15.0 1.3 collective-permute-start
  17.2 7.3 %collective-permute-done.w1_ref.a1_ref = bf16[208,768]{1,0:T(8,128)(2,1)} collective-permute-done((bf16[208,768]{1,0:T(8,128)(2,1)}, bf16[208,768]{1,0:T(8,128)(2,1)}, u32[]{:S(2)}, u32[]{:S(2)}) %collective-permute-start) | collective-permute-done | bytes 319520 | tf_op jit(solution)/shard_map/ppermute | solution.py:1203
  24.5 1.4 collective-permute-start.1
  26.2 6.5 %collective-permute-done.2.w3_ref.a3_ref = bf16[208,768]{1,0:T(8,128)(2,1)} collective-permute-done((bf16[208,768]{1,0:T(8,128)(2,1)}, bf16[208,768]{1,0:T(8,128)(2,1)}, u32[]{:S(2)}, u32[]{:S(2)}) %collective-permute-start.2) | collective-permute-done | bytes 319520 | tf_op jit(solution)/shard_map/ppermute | solution.py:1203
  34.1 2.8 collective-permute-start.3
  36.9 1.2 collective-permute-done.1.w2_ref.a2_ref
  39.0 5.9 %collective-permute-start.4 = (bf16[208,768]{1,0:T(8,128)(2,1)}, bf16[208,768]{1,0:T(8,128)(2,1)}, u32[]{:S(2)}, u32[]{:S(2)}) collective-permute-start(bf16[208,768]{1,0:T(8,128)(2,1)} %copy-done.16), channel_id=1, source_target_pairs={{0,4},{4,0},{8,12},{12,8},{16,20},{20,16},{24,28},{28,24},{1,5},{5... | collective-permute-start | bytes 958472 | tf_op jit(solution)/shard_map/ppermute | solution.py:1198
  45.7 1.0 fusion.off_ref
  46.8 3.5 collective-permute-start.9
  50.3 1.6 copy-done.1
  51.9 14.7 %attn_forward.2 = (bf16[8,1,192,128]{3,2,1,0:T(8,128)(2,1)}, f32[2,1024,256]{2,1,0:T(8,128)}, bf16[2,1024,192]{2,1,0:T(8,128)(2,1)}, bf16[2,1024,192]{2,1,0:T(8,...) custom-call(s32[4]{0:T(128)} %get-tuple-element.119.lens_ref, s32[3]{0:T(128)} %pad_add_fusion.where_ref, ...), custom_call_target="tpu_custom_call" | custom-call | flops 2063597568 | bytes 2359296 | tf_op jit(solution)/shard_map/attn_forward/pallas_call | solution.py:347
  66.7 1.7 collective-permute-start.15
  68.4 3.4 collective-permute-start.10
  71.8 12.6 %all-to-all-start.1 = ((bf16[8,1,192,128]{3,2,1,0:T(8,128)(2,1)}), bf16[8,1,192,128]{3,2,1,0:T(8,128)(2,1)S(1)}, u32[]{:S(2)}, u32[]{:S(2)}) async-start(bf16[8,1,192,128]{3,2,1,0:T(8,128)(2,1)} %get-tuple-element.134), calls=%async_computation.1 | async-start | bytes 786432 | tf_op jit(solution)/shard_map/all_to_all | solution.py:1284
  84.4 7.8 %attn_forward.3 = (bf16[8,1,192,128]{3,2,1,0:T(8,128)(2,1)}, f32[2,1024,256]{2,1,0:T(8,128)}, bf16[2,1024,192]{2,1,0:T(8,128)(2,1)}, bf16[2,1024,192]{2,1,0:T(8,128)(2,1)}, bf16[2,1024,192]{2,1,0:T(8,128)(2,1)}) custom-call(s32[4]{0:T(128)} %get-tuple-element.119.lens_ref, ...), custom_call_target="tpu_custom_call", output_to_operand_aliasing={{1}: (6, {}), {2}: (7, {}), {3}: (8, {}), {4}: (9, {})} | custom-call | flops 2063597568 | bytes 2359296 | tf_op jit(solution)/shard_map/attn_forward/pallas_call | solution.py:347
  92.2 1.4 collective-permute-start.14
  93.6 1.3 collective-permute-start.13
  95.1 0.9 collective-permute-start.12
  96.0 1.2 collective-permute-start.16
  97.2 5.1 %all-to-all-start.2 = ((bf16[8,1,192,128]{3,2,1,0:T(8,128)(2,1)}), bf16[8,1,192,128]{3,2,1,0:T(8,128)(2,1)S(1)}, u32[]{:S(2)}, u32[]{:S(2)}) async-start(bf16[8,1,192,128]{3,2,1,0:T(8,128)(2,1)} %get-tuple-element.138), calls=%async_computation.2 | async-start | bytes 786432 | tf_op jit(solution)/shard_map/all_to_all | solution.py:1288
  102.3 4.3 %sort_rows.1 = (bf16[512,768]{1,0:T(8,128)(2,1)}, bf16[512,768]{1,0:T(8,128)(2,1)}) custom-call(s32[4]{0:T(128)} %get-tuple-element.118.order_ref, s32[4]{0:T(128)} %get-tuple-element.119.lens_ref, s32[1]{0:T(128)} %bitcast.3.start_ref, bf16[4,128,768]{2,1,0:T(8,128)(2,1)} %tok_ref.2, bf16[4,128,768]{2,1,0:T(8,128)(2,1)} %cot_ref.1), custom_call_target="tpu_custom_call" | custom-call | bytes 1500000 | tf_op jit(solution)/shard_map/sort_rows/pallas_call | solution.py:168
  107.4 18.9 %all-to-all-done.2.attn1_ref = bf16[8,1,192,128]{3,2,1,0:T(8,128)(2,1)S(1)} async-done(((bf16[8,1,192,128]{3,2,1,0:T(8,128)(2,1)}), bf16[8,1,192,128]{3,2,1,0:T(8,128)(2,1)S(1)}, u32[]{:S(2)}, u32[]{:S(2)}) %all-to-all-start.2) | async-done | bytes 393248 | tf_op jit(solution)/shard_map/all_to_all | solution.py:1288
  127.0 5.1 %out_project.1 = (f32[512,768]{1,0:T(8,128)}, bf16[512,768]{1,0:T(8,128)(2,1)}, bf16[768,768]{1,0:T(8,128)(2,1)}) custom-call(s32[3]{0:T(128)} %pad_add_fusion.where_ref, bf16[512,768]{1,0:T(8,128)(2,1)} %get-tuple-element.120.tok_ref, bf16[8,1,192,128]{3,2,1,0:T(8,128)(2,1)} %copy-done.2, bf16[8,1,192,128]{3,2,1,0:T(8,128)(2,1)} %copy-done.3, ...), custom_call_target="tpu_custom_call" | custom-call | flops 603979776 | bytes 2359296 | tf_op jit(solution)/shard_map/out_project/pallas_call | solution.py:597
  132.7 1.8 collective-permute-done.19.dy_other_ref
  134.5 1.3 collective-permute-done.18.nf_other_ref
  135.8 0.9 copy-done.26
  136.7 25.7 %ffn_first.1 = (bf16[1024,1536]{1,0:T(8,128)(2,1)}, bf16[1024,1536]{1,0:T(8,128)(2,1)}, f32[512,768]{1,0:T(8,128)}, bf16[512,768]{1,0:T(8,128)(2,1)}, bf16[1536,...) custom-call(s32[3]{0:T(128)} %pad_add_fusion.where_ref, ...), custom_call_target="tpu_custom_call" | custom-call | flops 14495514624 | bytes 12189696 | tf_op jit(solution)/shard_map/ffn_first/pallas_call | solution.py:803
  162.7 1.5 collective-permute-start.22
  165.0 0.9 copy-done.8
  165.9 6.5 %out_back.1 = (bf16[8,2,192,128]{3,2,1,0:T(8,128)(2,1)}, f32[512,768]{1,0:T(8,128)}, f32[1,768]{1,0:T(1,128)}, bf16[4,96,768]{2,1,0:T(8,128)(2,1)}, bf16[4,96,768]{2,1,0:T(8,128)(2,1)}) custom-call(s32[3]{0:T(128)} %pad_add_fusion.where_ref, f32[512,768]{1,0:T(8,128)} %get-tuple-element.157.own_ref, bf16[512,768]{1,0:T(8,128)(2,1)} %copy-done.8, ...), custom_call_target="tpu_custom_call" | custom-call | flops 1207959552 | bytes 3932160 | tf_op jit(solution)/shard_map/out_back/pallas_call | solution.py:646
  172.5 4.3 %all-to-all-start.3 = ((bf16[8,2,192,128]{3,2,1,0:T(8,128)(2,1)}), bf16[8,2,192,128]{3,2,1,0:T(8,128)(2,1)S(1)}, u32[]{:S(2)}, u32[]{:S(2)}) async-start(bf16[8,2,192,128]{3,2,1,0:T(8,128)(2,1)} %get-tuple-element.160), calls=%async_computation.3 | async-start | bytes 1572864 | tf_op jit(solution)/shard_map/all_to_all | solution.py:1307
  176.7 15.8 %ffn_second.1 = (f32[512,768]{1,0:T(8,128)}, bf16[512,768]{1,0:T(8,128)(2,1)}, bf16[4,2,96,768]{3,2,1,0:T(8,128)(2,1)}, bf16[4,2,96,768]{3,2,1,0:T(8,128)(2,1)},...) custom-call(s32[3]{0:T(128)} %pad_add_fusion.where_ref, bf16[512,768]{1,0:T(8,128)(2,1)} %get-tuple-element.143.nf_own_ref, ...), custom_call_target="tpu_custom_call" | custom-call | flops 7247757312 | bytes 13369344 | tf_op jit(solution)/shard_map/ffn_second/pallas_call | solution.py:889
  193.8 1.7 collective-permute-start.24
  195.5 1.2 collective-permute-start.25
  196.7 35.5 %attn_backward.1 = (bf16[8,2,128,768]{3,2,1,0:T(8,128)(2,1)}, bf16[4,96,768]{2,1,0:T(8,128)(2,1)}, bf16[4,96,768]{2,1,0:T(8,128)(2,1)}, f32[1,768]{1,0:T(1,128)}, f32[3,2048]{1,0:T(4,128)}) custom-call(s32[4]{0:T(128)} %get-tuple-element.119.lens_ref, s32[3]{0:T(128)} %pad_add_fusion.where_ref, bf16[8,2,128,768]{3,2,1,0:T(8,128)(2,1)} %copy-done.1, ...), custom_call_target="tpu_custom_call" | custom-call | flops 19730006016 | bytes 7864320 | tf_op jit(solution)/shard_map/attn_backward/pallas_call | solution.py:514
  232.2 1.3 fusion.2
  234.1 4.1 %by_chip.1 = (bf16[192,768]{1,0:T(8,128)(2,1)}, bf16[192,768]{1,0:T(8,128)(2,1)}, bf16[192,768]{1,0:T(8,128)(2,1)}, bf16[192,768]{1,0:T(8,128)(2,1)}) custom-call(s32[3]{0:T(128)} %pad_add_fusion.where_ref, bf16[2,192,768]{2,1,0:T(8,128)(2,1)} %get-tuple-element.189.refs_0_, bf16[2,192,768]{2,1,0:T(8,128)(2,1)} %copy-done.13, ...), custom_call_target="tpu_custom_call" | custom-call | bytes 1500000 | tf_op jit(solution)/shard_map/by_chip/pallas_call | solution.py:986
  238.7 4.3 %second_halves.1 = (bf16[4,2,48,768]{3,2,1,0:T(8,128)(2,1)}, bf16[4,2,48,768]{3,2,1,0:T(8,128)(2,1)}, bf16[4,96,768]{2,1,0:T(8,128)(2,1)}, bf16[4,96,768]{2,1,0:T(8,128)(2,1)}) custom-call(s32[3]{0:T(128)} %pad_add_fusion.where_ref, bf16[4,2,96,768]{3,2,1,0:T(8,128)(2,1)} %get-tuple-element.176.u_keep_ref, bf16[4,2,96,768]{3,2,1,0:T(8,128)(2,1)} %copy-done.4, ...), custom_call_target="tpu_custom_call" | custom-call | bytes 3500000 | tf_op jit(solution)/shard_map/second_halves/pallas_call | solution.py:941
  243.0 1.4 collective-permute-start.28
  245.8 0.9 collective-permute-done.30.refs_7_
  246.8 1.0 collective-permute-start.33
  248.0 21.3 %collective-permute-done.33.refs_10_ = bf16[192,768]{1,0:T(8,128)(2,1)S(1)} collective-permute-done((bf16[192,768]{1,0:T(8,128)(2,1)}, bf16[192,768]{1,0:T(8,128)(2,1)S(1)}, u32[]{:S(2)}, u32[]{:S(2)}) %collective-permute-start.33) | collective-permute-done | bytes 294944 | tf_op jit(solution)/shard_map/ppermute | solution.py:1198
  270.8 3.9 %by_plane.1 = (bf16[304,768]{1,0:T(8,128)(2,1)}, bf16[304,768]{1,0:T(8,128)(2,1)}, bf16[304,768]{1,0:T(8,128)(2,1)}, bf16[304,768]{1,0:T(8,128)(2,1)}, bf16[96,768]{1,0:T(8,128)(2,1)}) custom-call(s32[3]{0:T(128)} %pad_add_fusion.where_ref, bf16[4,2,48,768]{3,2,1,0:T(8,128)(2,1)} %get-tuple-element.180.refs_0_, bf16[4,2,48,768]{3,2,1,0:T(8,128)(2,1)} %copy-done.10, ...), custom_call_target="tpu_custom_call" | custom-call | bytes 3000000 | tf_op jit(solution)/shard_map/by_plane/pallas_call | solution.py:1040
  274.7 3.6 all-to-all-start.4
  278.4 2.6 collective-permute-start.36
  281.0 1.4 collective-permute-start.37
  282.4 0.9 copy-done.9
  283.3 4.7 %finish_out.1 = bf16[4,128,768]{2,1,0:T(8,128)(2,1)} custom-call(s32[4]{0:T(128)} %get-tuple-element.118.order_ref, s32[4]{0:T(128)} %get-tuple-element.119.lens_ref, s32[1]{0:T(128)} %bitcast.3.start_ref, f32[512,768]{1,0:T(8,128)} %get-tuple-element.142.res_ref, f32[512,768]{1,0:T(8,128)} %get-tuple-element.151.own_ref, bf16[512,768]{1,0:T(8,128)(2,1)} %copy-done.9), custom_call_target="tpu_custom_call" | custom-call | bytes 3000000 | tf_op jit(solution)/shard_map/finish_out/pallas_call | solution.py:1142
  288.0 2.5 collective-permute-done.35
  290.5 28.2 %collective-permute-done.36 = bf16[304,768]{1,0:T(8,128)(2,1)S(1)} collective-permute-done((bf16[304,768]{1,0:T(8,128)(2,1)}, bf16[304,768]{1,0:T(8,128)(2,1)S(1)}, u32[]{:S(2)}, u32[]{:S(2)}) %collective-permute-start.36) | collective-permute-done | bytes 466976 | tf_op jit(solution)/shard_map/ppermute | solution.py:1203
  318.7 3.7 collective-permute-done.37
  322.6 0.9 pad_maximum_fusion.refs_0_
  323.6 1.8 collective-permute-start.40
  326.2 13.5 %collective-permute-done.40.refs_3_ = bf16[400,768]{1,0:T(8,128)(2,1)} collective-permute-done((bf16[400,768]{1,0:T(8,128)(2,1)}, bf16[400,768]{1,0:T(8,128)(2,1)}, u32[]{:S(2)}, u32[]{:S(2)}) %collective-permute-start.40) | collective-permute-done | bytes 614432 | tf_op jit(solution)/shard_map/ppermute | solution.py:1198
  339.7 2.3 collective-permute-start.44
  342.0 10.6 %collective-permute-done.38.refs_1_ = bf16[400,768]{1,0:T(8,128)(2,1)} collective-permute-done((bf16[400,768]{1,0:T(8,128)(2,1)}, bf16[400,768]{1,0:T(8,128)(2,1)}, u32[]{:S(2)}, u32[]{:S(2)}) %collective-permute-start.38) | collective-permute-done | bytes 614432 | tf_op jit(solution)/shard_map/ppermute | solution.py:1198
  352.6 1.3 collective-permute-start.42
  354.2 1.6 copy-done
  355.8 5.4 %finish_tokens.1 = f32[4,128,768]{2,1,0:T(8,128)} custom-call(s32[4]{0:T(128)} %get-tuple-element.118.order_ref, bf16[4,4,128,768]{3,2,1,0:T(8,128)(2,1)} %bitcast.9, bf16[512,768]{1,0:T(8,128)(2,1)} %get-tuple-element.120.tok_ref, f32[512,768]{1,0:T(8,128)} %get-tuple-element.204.dres_ref, f32[1,768]{1,0:T(1,128)} %reshape.122.gain_ref), custom_call_target="tpu_custom_call" | custom-call | bytes 5000000 | tf_op jit(solution)/shard_map/finish_tokens/pallas_call | solution.py:1173
  361.3 7.4 %unpack.1 = (f32[192,3072]{1,0:T(8,128)}, f32[192,3072]{1,0:T(8,128)}, f32[768,768]{1,0:T(8,128)}, f32[192,768]{1,0:T(8,128)}, f32[192,768]{1,0:T(8,128)}, /*ind...) custom-call(s32[3]{0:T(128)} %pad_add_fusion.where_ref, bf16[400,768]{1,0:T(8,128)(2,1)} %pad_maximum_fusion.refs_0_, ...), custom_call_target="tpu_custom_call" | custom-call | bytes 12000000 | tf_op jit(solution)/shard_map/unpack/pallas_call | solution.py:1112
  369.3 1.4 fusion.16
  (154 shorter events, 18.9 us)
Async XLA Ops:
  10.6 15.3 %copy-start.22 = (s32[2047]{0:T(1024)S(1)}, s32[2047]{0:T(1024)}, u32[]{:S(2)}) copy-start(s32[2047]{0:T(1024)} %param.17) | copy-start | bytes 24568
  10.6 39.7 %all-to-all-start = ((bf16[8,2,128,768]{3,2,1,0:T(8,128)(2,1)}), bf16[8,2,128,768]{3,2,1,0:T(8,128)(2,1)S(1)}, u32[]{:S(2)}, u32[]{:S(2)}) async-start(bf16[8,2,128,768]{3,2,1,0:T(8,128)(2,1)} %bitcast.10), calls=%async_computation | async-start | bytes 6291456 | tf_op jit(solution)/shard_map/all_to_all | solution.py:1255
  15.0 9.5 %collective-permute-start = (bf16[208,768]{1,0:T(8,128)(2,1)}, bf16[208,768]{1,0:T(8,128)(2,1)}, u32[]{:S(2)}, u32[]{:S(2)}) collective-permute-start(bf16[208,768]{1,0:T(8,128)(2,1)} %get-tuple-element.116), channel_id=1, source_target_pairs={{0,1},{1,2},{2,3},{3,0},{4,5},{5,6},{6,7},{7,4},{8,9},{9,10},{10,1... | collective-permute-start | bytes 958472 | tf_op jit(solution)/shard_map/ppermute | solution.py:1203
  16.3 16.4 %collective-permute-start.2 = (bf16[208,768]{1,0:T(8,128)(2,1)}, bf16[208,768]{1,0:T(8,128)(2,1)}, u32[]{:S(2)}, u32[]{:S(2)}) collective-permute-start(bf16[208,768]{1,0:T(8,128)(2,1)} %get-tuple-element.116), channel_id=1, source_target_pairs={{0,3},{1,0},{2,1},{3,2},{4,7},{5,4},{6,5},{7,6},{8,11},{9,8},{10,9... | collective-permute-start | bytes 958472 | tf_op jit(solution)/shard_map/ppermute | solution.py:1203
  24.5 13.6 %collective-permute-start.1 = (bf16[208,768]{1,0:T(8,128)(2,1)}, bf16[208,768]{1,0:T(8,128)(2,1)S(1)}, u32[]{:S(2)}, u32[]{:S(2)}) collective-permute-start(bf16[208,768]{1,0:T(8,128)(2,1)} %collective-permute-done.w1_ref.a1_ref), channel_id=1, source_target_pairs={{0,1},{1,2},{2,3},{3,0},{4,5},{5,6},{6,7},{7,4},{8,9},{9,10},{10,1... | collective-permute-start | bytes 958472 | tf_op jit(solution)/shard_map/ppermute | solution.py:1203
  32.7 33.9 %collective-permute-start.6 = (bf16[288,768]{1,0:T(8,128)(2,1)}, bf16[288,768]{1,0:T(8,128)(2,1)}, u32[]{:S(2)}, u32[]{:S(2)}) collective-permute-start(bf16[288,768]{1,0:T(8,128)(2,1)} %get-tuple-element.130), channel_id=1, source_target_pairs={{0,1},{1,2},{2,3},{3,0},{4,5},{5,6},{6,7},{7,4},{8,9},{9,10},{10,1... | collective-permute-start | bytes 1327112 | tf_op jit(solution)/shard_map/ppermute | solution.py:1203
  34.1 12.5 %collective-permute-start.3 = (bf16[208,768]{1,0:T(8,128)(2,1)}, bf16[208,768]{1,0:T(8,128)(2,1)}, u32[]{:S(2)}, u32[]{:S(2)}) collective-permute-start(bf16[208,768]{1,0:T(8,128)(2,1)} %collective-permute-done.w1_ref.a1_ref), channel_id=1, source_target_pairs={{0,4},{4,0},{8,12},{12,8},{16,20},{20,16},{24,28},{28,24},{1,5},{5... | collective-permute-start | bytes 958472 | tf_op jit(solution)/shard_map/ppermute | solution.py:1198
  36.9 9.9 %collective-permute-start.5 = (bf16[208,768]{1,0:T(8,128)(2,1)}, bf16[208,768]{1,0:T(8,128)(2,1)}, u32[]{:S(2)}, u32[]{:S(2)}) collective-permute-start(bf16[208,768]{1,0:T(8,128)(2,1)} %collective-permute-done.2.w3_ref.a3_ref), channel_id=1, source_target_pairs={{0,4},{4,0},{8,12},{12,8},{16,20},{20,16},{24,28},{28,24},{1,5},{5... | collective-permute-start | bytes 958472 | tf_op jit(solution)/shard_map/ppermute | solution.py:1198
  39.0 27.6 %collective-permute-start.7 = (bf16[288,768]{1,0:T(8,128)(2,1)}, bf16[288,768]{1,0:T(8,128)(2,1)}, u32[]{:S(2)}, u32[]{:S(2)}) collective-permute-start(bf16[288,768]{1,0:T(8,128)(2,1)} %get-tuple-element.132), channel_id=1, source_target_pairs={{0,1},{1,2},{2,3},{3,0},{4,5},{5,6},{6,7},{7,4},{8,9},{9,10},{10,1... | collective-permute-start | bytes 1327112 | tf_op jit(solution)/shard_map/ppermute | solution.py:1203
  39.0 11.3 %collective-permute-start.4 = (bf16[208,768]{1,0:T(8,128)(2,1)}, bf16[208,768]{1,0:T(8,128)(2,1)}, u32[]{:S(2)}, u32[]{:S(2)}) collective-permute-start(bf16[208,768]{1,0:T(8,128)(2,1)} %copy-done.16), channel_id=1, source_target_pairs={{0,4},{4,0},{8,12},{12,8},{16,20},{20,16},{24,28},{28,24},{1,5},{5... | collective-permute-start | bytes 958472 | tf_op jit(solution)/shard_map/ppermute | solution.py:1198
  46.6 45.6 %collective-permute-start.8 = (bf16[288,768]{1,0:T(8,128)(2,1)}, bf16[288,768]{1,0:T(8,128)(2,1)}, u32[]{:S(2)}, u32[]{:S(2)}) collective-permute-start(bf16[288,768]{1,0:T(8,128)(2,1)} %get-tuple-element.130), channel_id=1, source_target_pairs={{0,3},{1,0},{2,1},{3,2},{4,7},{5,4},{6,5},{7,6},{8,11},{9,8},{10,9... | collective-permute-start | bytes 1327112 | tf_op jit(solution)/shard_map/ppermute | solution.py:1203
  46.8 46.8 %collective-permute-start.9 = (bf16[288,768]{1,0:T(8,128)(2,1)}, bf16[288,768]{1,0:T(8,128)(2,1)}, u32[]{:S(2)}, u32[]{:S(2)}) collective-permute-start(bf16[288,768]{1,0:T(8,128)(2,1)} %get-tuple-element.132), channel_id=1, source_target_pairs={{0,3},{1,0},{2,1},{3,2},{4,7},{5,4},{6,5},{7,6},{8,11},{9,8},{10,9... | collective-permute-start | bytes 1327112 | tf_op jit(solution)/shard_map/ppermute | solution.py:1203
  66.7 28.2 %collective-permute-start.11 = (bf16[288,768]{1,0:T(8,128)(2,1)}, bf16[288,768]{1,0:T(8,128)(2,1)S(1)}, u32[]{:S(2)}, u32[]{:S(2)}) collective-permute-start(bf16[288,768]{1,0:T(8,128)(2,1)} %collective-permute-done.6.x1), channel_id=1, source_target_pairs={{0,1},{1,2},{2,3},{3,0},{4,5},{5,6},{6,7},{7,4},{8,9},{9,10},{10,1... | collective-permute-start | bytes 1327112 | tf_op jit(solution)/shard_map/ppermute | solution.py:1203
  66.7 28.4 %collective-permute-start.15 = (bf16[288,768]{1,0:T(8,128)(2,1)}, bf16[288,768]{1,0:T(8,128)(2,1)S(1)}, u32[]{:S(2)}, u32[]{:S(2)}) collective-permute-start(bf16[288,768]{1,0:T(8,128)(2,1)} %collective-permute-done.7.y1), channel_id=1, source_target_pairs={{0,1},{1,2},{2,3},{3,0},{4,5},{5,6},{6,7},{7,4},{8,9},{9,10},{10,1... | collective-permute-start | bytes 1327112 | tf_op jit(solution)/shard_map/ppermute | solution.py:1203
  68.4 27.6 %collective-permute-start.10 = (bf16[288,768]{1,0:T(8,128)(2,1)}, bf16[288,768]{1,0:T(8,128)(2,1)S(1)}, u32[]{:S(2)}, u32[]{:S(2)}) collective-permute-start(bf16[288,768]{1,0:T(8,128)(2,1)} %collective-permute-done.6.x1), channel_id=1, source_target_pairs={{0,8},{4,12},{8,0},{12,4},{16,24},{20,28},{24,16},{28,20},{1,9},{5... | collective-permute-start | bytes 1327112 | tf_op jit(solution)/shard_map/ppermute | solution.py:1198
  71.8 21.8 %all-to-all-start.1 = ((bf16[8,1,192,128]{3,2,1,0:T(8,128)(2,1)}), bf16[8,1,192,128]{3,2,1,0:T(8,128)(2,1)S(1)}, u32[]{:S(2)}, u32[]{:S(2)}) async-start(bf16[8,1,192,128]{3,2,1,0:T(8,128)(2,1)} %get-tuple-element.134), calls=%async_computation.1 | async-start | bytes 786432 | tf_op jit(solution)/shard_map/all_to_all | solution.py:1284
  92.2 15.2 %collective-permute-start.14 = (bf16[288,768]{1,0:T(8,128)(2,1)}, bf16[288,768]{1,0:T(8,128)(2,1)S(1)}, u32[]{:S(2)}, u32[]{:S(2)}) collective-permute-start(bf16[288,768]{1,0:T(8,128)(2,1)} %collective-permute-done.7.y1), channel_id=1, source_target_pairs={{0,16},{4,20},{8,24},{12,28},{16,0},{20,4},{24,8},{28,12},{1,17},{... | collective-permute-start | bytes 1327112 | tf_op jit(solution)/shard_map/ppermute | solution.py:1198
  93.6 32.7 %copy-start.2 = (bf16[8,1,192,128]{3,2,1,0:T(8,128)(2,1)}, bf16[8,1,192,128]{3,2,1,0:T(8,128)(2,1)S(1)}, u32[]{:S(2)}) copy-start(bf16[8,1,192,128]{3,2,1,0:T(8,128)(2,1)S(1)} %all-to-all-done.1.attn0_ref) | copy-start | bytes 1179652
  93.6 32.7 %collective-permute-start.13 = (bf16[288,768]{1,0:T(8,128)(2,1)}, bf16[288,768]{1,0:T(8,128)(2,1)S(1)}, u32[]{:S(2)}, u32[]{:S(2)}) collective-permute-start(bf16[288,768]{1,0:T(8,128)(2,1)} %collective-permute-done.8.x3), channel_id=1, source_target_pairs={{0,8},{4,12},{8,0},{12,4},{16,24},{20,28},{24,16},{28,20},{1,9},{5... | collective-permute-start | bytes 1327112 | tf_op jit(solution)/shard_map/ppermute | solution.py:1198
  94.9 37.2 %copy-start.28 = (bf16[288,768]{1,0:T(8,128)(2,1)}, bf16[288,768]{1,0:T(8,128)(2,1)S(1)}, u32[]{:S(2)}) copy-start(bf16[288,768]{1,0:T(8,128)(2,1)S(1)} %collective-permute-done.11.x2) | copy-start | bytes 1327108
  94.9 31.4 %collective-permute-start.17 = (bf16[288,768]{1,0:T(8,128)(2,1)}, bf16[288,768]{1,0:T(8,128)(2,1)}, u32[]{:S(2)}, u32[]{:S(2)}) collective-permute-start(bf16[288,768]{1,0:T(8,128)(2,1)} %collective-permute-done.9.y3), channel_id=1, source_target_pairs={{0,16},{4,20},{8,24},{12,28},{16,0},{20,4},{24,8},{28,12},{1,17},{... | collective-permute-start | bytes 1327112 | tf_op jit(solution)/shard_map/ppermute | solution.py:1198
  95.1 37.0 %copy-start.29 = (bf16[288,768]{1,0:T(8,128)(2,1)}, bf16[288,768]{1,0:T(8,128)(2,1)S(1)}, u32[]{:S(2)}) copy-start(bf16[288,768]{1,0:T(8,128)(2,1)S(1)} %collective-permute-done.15.y2) | copy-start | bytes 1327108
  95.1 31.2 %collective-permute-start.12 = (bf16[288,768]{1,0:T(8,128)(2,1)S(1)}, bf16[288,768]{1,0:T(8,128)(2,1)}, u32[]{:S(2)}, u32[]{:S(2)}) collective-permute-start(bf16[288,768]{1,0:T(8,128)(2,1)S(1)} %collective-permute-done.11.x2), channel_id=1, source_target_pairs={{0,8},{4,12},{8,0},{12,4},{16,24},{20,28},{24,16},{28,20},{1,9},{5... | collective-permute-start | bytes 1327112 | tf_op jit(solution)/shard_map/ppermute | solution.py:1198
  96.0 36.1 %copy-start.30 = (bf16[288,768]{1,0:T(8,128)(2,1)}, bf16[288,768]{1,0:T(8,128)(2,1)S(1)}, u32[]{:S(2)}) copy-start(bf16[288,768]{1,0:T(8,128)(2,1)S(1)} %collective-permute-done.10.sx1) | copy-start | bytes 1327108
  96.0 30.3 %collective-permute-start.16 = (bf16[288,768]{1,0:T(8,128)(2,1)S(1)}, bf16[288,768]{1,0:T(8,128)(2,1)}, u32[]{:S(2)}, u32[]{:S(2)}) collective-permute-start(bf16[288,768]{1,0:T(8,128)(2,1)S(1)} %collective-permute-done.15.y2), channel_id=1, source_target_pairs={{0,16},{4,20},{8,24},{12,28},{16,0},{20,4},{24,8},{28,12},{1,17},{... | collective-permute-start | bytes 1327112 | tf_op jit(solution)/shard_map/ppermute | solution.py:1198
  97.2 29.1 %all-to-all-start.2 = ((bf16[8,1,192,128]{3,2,1,0:T(8,128)(2,1)}), bf16[8,1,192,128]{3,2,1,0:T(8,128)(2,1)S(1)}, u32[]{:S(2)}, u32[]{:S(2)}) async-start(bf16[8,1,192,128]{3,2,1,0:T(8,128)(2,1)} %get-tuple-element.138), calls=%async_computation.2 | async-start | bytes 786432 | tf_op jit(solution)/shard_map/all_to_all | solution.py:1288
  107.4 28.5 %copy-start.31 = (bf16[288,768]{1,0:T(8,128)(2,1)}, bf16[288,768]{1,0:T(8,128)(2,1)S(1)}, u32[]{:S(2)}) copy-start(bf16[288,768]{1,0:T(8,128)(2,1)S(1)} %collective-permute-done.14.sy1) | copy-start | bytes 1327108
  126.3 5.8 %copy-start.32 = (bf16[288,768]{1,0:T(8,128)(2,1)}, bf16[288,768]{1,0:T(8,128)(2,1)S(1)}, u32[]{:S(2)}) copy-start(bf16[288,768]{1,0:T(8,128)(2,1)S(1)} %collective-permute-done.13.sx3) | copy-start | bytes 1327108
  132.2 2.4 collective-permute-start.19
  132.4 3.5 collective-permute-start.18
  162.5 2.6 collective-permute-start.23
  162.7 30.0 %collective-permute-start.21 = (bf16[2,192,768]{2,1,0:T(8,128)(2,1)}, bf16[2,192,768]{2,1,0:T(8,128)(2,1)S(1)}, u32[]{:S(2)}, u32[]{:S(2)}) collective-permute-start(bf16[2,192,768]{2,1,0:T(8,128)(2,1)} %get-tuple-element.153), channel_id=1, source_target_pairs={{0,1},{1,2},{2,3},{3,0},{4,5},{5,6},{6,7},{7,4},{8,9},{9,10},{10,1... | collective-permute-start | bytes 1769480 | tf_op jit(solution)/shard_map/ppermute | solution.py:1203
  162.7 30.0 %collective-permute-start.22 = (bf16[2,192,768]{2,1,0:T(8,128)(2,1)}, bf16[2,192,768]{2,1,0:T(8,128)(2,1)S(1)}, u32[]{:S(2)}, u32[]{:S(2)}) collective-permute-start(bf16[2,192,768]{2,1,0:T(8,128)(2,1)} %get-tuple-element.154), channel_id=1, source_target_pairs={{0,3},{1,0},{2,1},{3,2},{4,7},{5,4},{6,5},{7,6},{8,11},{9,8},{10,9... | collective-permute-start | bytes 1769480 | tf_op jit(solution)/shard_map/ppermute | solution.py:1203
  164.2 69.9 %collective-permute-start.26 = (bf16[2,192,768]{2,1,0:T(8,128)(2,1)}, bf16[2,192,768]{2,1,0:T(8,128)(2,1)}, u32[]{:S(2)}, u32[]{:S(2)}) collective-permute-start(bf16[2,192,768]{2,1,0:T(8,128)(2,1)} %get-tuple-element.173), channel_id=1, source_target_pairs={{0,2},{1,3},{2,0},{3,1},{4,6},{5,7},{6,4},{7,5},{8,10},{9,11},{10,... | collective-permute-start | bytes 1769480 | tf_op jit(solution)/shard_map/ppermute | solution.py:1203
  172.5 20.3 %all-to-all-start.3 = ((bf16[8,2,192,128]{3,2,1,0:T(8,128)(2,1)}), bf16[8,2,192,128]{3,2,1,0:T(8,128)(2,1)S(1)}, u32[]{:S(2)}, u32[]{:S(2)}) async-start(bf16[8,2,192,128]{3,2,1,0:T(8,128)(2,1)} %get-tuple-element.160), calls=%async_computation.3 | async-start | bytes 1572864 | tf_op jit(solution)/shard_map/all_to_all | solution.py:1307
  176.7 15.9 %copy-start.24 = (f32[1,768]{1,0:T(1,128)S(1)}, f32[1,768]{1,0:T(1,128)}, u32[]{:S(2)}) copy-start(f32[1,768]{1,0:T(1,128)} %get-tuple-element.187) | copy-start | bytes 9220
  192.5 41.6 %collective-permute-start.31 = (bf16[4,96,768]{2,1,0:T(8,128)(2,1)}, bf16[4,96,768]{2,1,0:T(8,128)(2,1)}, u32[]{:S(2)}, u32[]{:S(2)}) collective-permute-start(bf16[4,96,768]{2,1,0:T(8,128)(2,1)} %get-tuple-element.194), channel_id=1, source_target_pairs={{0,4},{4,0},{8,12},{12,8},{16,20},{20,16},{24,28},{28,24},{1,5},{5... | collective-permute-start | bytes 1769480 | tf_op jit(solution)/shard_map/ppermute | solution.py:1198
  193.8 40.2 %collective-permute-start.24 = (bf16[4,2,96,768]{3,2,1,0:T(8,128)(2,1)}, bf16[4,2,96,768]{3,2,1,0:T(8,128)(2,1)S(1)}, u32[]{:S(2)}, u32[]{:S(2)}) collective-permute-start(bf16[4,2,96,768]{3,2,1,0:T(8,128)(2,1)} %get-tuple-element.161), channel_id=1, source_target_pairs={{0,8},{4,12},{8,0},{12,4},{16,24},{20,28},{24,16},{28,20},{1,9},{5... | collective-permute-start | bytes 3538952 | tf_op jit(solution)/shard_map/ppermute | solution.py:1198
  195.5 38.5 %collective-permute-start.25 = (bf16[4,192,768]{2,1,0:T(8,128)(2,1)}, bf16[4,192,768]{2,1,0:T(8,128)(2,1)S(1)}, u32[]{:S(2)}, u32[]{:S(2)}) collective-permute-start(bf16[4,192,768]{2,1,0:T(8,128)(2,1)} %get-tuple-element.162), channel_id=1, source_target_pairs={{0,16},{4,20},{8,24},{12,28},{16,0},{20,4},{24,8},{28,12},{1,17},{... | collective-permute-start | bytes 3538952 | tf_op jit(solution)/shard_map/ppermute | solution.py:1198
  238.2 9.6 %collective-permute-start.32 = (bf16[192,768]{1,0:T(8,128)(2,1)}, bf16[192,768]{1,0:T(8,128)(2,1)S(1)}, u32[]{:S(2)}, u32[]{:S(2)}) collective-permute-start(bf16[192,768]{1,0:T(8,128)(2,1)} %get-tuple-element.196), channel_id=1, source_target_pairs={{0,8},{4,12},{8,0},{12,4},{16,24},{20,28},{24,16},{28,20},{1,9},{5... | collective-permute-start | bytes 884744 | tf_op jit(solution)/shard_map/ppermute | solution.py:1198
  238.7 5.8 %copy-start.23 = (f32[1,768]{1,0:T(1,128)S(1)}, f32[1,768]{1,0:T(1,128)}, u32[]{:S(2)}) copy-start(f32[1,768]{1,0:T(1,128)} %get-tuple-element.186) | copy-start | bytes 9220
  238.7 9.1 %copy-start.33 = (bf16[192,768]{1,0:T(8,128)(2,1)S(1)}, bf16[192,768]{1,0:T(8,128)(2,1)}, u32[]{:S(2)}) copy-start(bf16[192,768]{1,0:T(8,128)(2,1)} %get-tuple-element.198) | copy-start | bytes 884740
  243.0 26.4 %collective-permute-start.27 = (bf16[4,2,48,768]{3,2,1,0:T(8,128)(2,1)}, bf16[4,2,48,768]{3,2,1,0:T(8,128)(2,1)S(1)}, u32[]{:S(2)}, u32[]{:S(2)}) collective-permute-start(bf16[4,2,48,768]{3,2,1,0:T(8,128)(2,1)} %get-tuple-element.181), channel_id=1, source_target_pairs={{0,16},{4,20},{8,24},{12,28},{16,0},{20,4},{24,8},{28,12},{1,17},{... | collective-permute-start | bytes 1769480 | tf_op jit(solution)/shard_map/ppermute | solution.py:1198
  243.0 26.4 %collective-permute-start.28 = (bf16[4,96,768]{2,1,0:T(8,128)(2,1)}, bf16[4,96,768]{2,1,0:T(8,128)(2,1)S(1)}, u32[]{:S(2)}, u32[]{:S(2)}) collective-permute-start(bf16[4,96,768]{2,1,0:T(8,128)(2,1)} %get-tuple-element.183), channel_id=1, source_target_pairs={{0,8},{4,12},{8,0},{12,4},{16,24},{20,28},{24,16},{28,20},{1,9},{5... | collective-permute-start | bytes 1769480 | tf_op jit(solution)/shard_map/ppermute | solution.py:1198
  244.5 24.9 %collective-permute-start.29 = (bf16[4,96,768]{2,1,0:T(8,128)(2,1)S(1)}, bf16[4,96,768]{2,1,0:T(8,128)(2,1)S(1)}, u32[]{:S(2)}, u32[]{:S(2)}) collective-permute-start(bf16[4,96,768]{2,1,0:T(8,128)(2,1)S(1)} %copy-done.27), channel_id=1, source_target_pairs={{0,4},{4,0},{8,12},{12,8},{16,20},{20,16},{24,28},{28,24},{1,5},{5... | collective-permute-start | bytes 1769480 | tf_op jit(solution)/shard_map/ppermute | solution.py:1198
  245.3 1.4 collective-permute-start.30
  246.8 22.7 %copy-start.21 = (bf16[4,16,768]{2,1,0:T(8,128)(2,1)}, bf16[4,16,768]{2,1,0:T(8,128)(2,1)S(1)}, u32[]{:S(2)}) copy-start(bf16[4,16,768]{2,1,0:T(8,128)(2,1)S(1)} %collective-permute-done.30.refs_7_) | copy-start | bytes 294916
  246.8 22.6 %collective-permute-start.33 = (bf16[192,768]{1,0:T(8,128)(2,1)}, bf16[192,768]{1,0:T(8,128)(2,1)S(1)}, u32[]{:S(2)}, u32[]{:S(2)}) collective-permute-start(bf16[192,768]{1,0:T(8,128)(2,1)} %get-tuple-element.197), channel_id=1, source_target_pairs={{0,16},{4,20},{8,24},{12,28},{16,0},{20,4},{24,8},{28,12},{1,17},{... | collective-permute-start | bytes 884744 | tf_op jit(solution)/shard_map/ppermute | solution.py:1198
  247.8 21.7 %copy-start.17 = (bf16[192,768]{1,0:T(8,128)(2,1)}, bf16[192,768]{1,0:T(8,128)(2,1)S(1)}, u32[]{:S(2)}) copy-start(bf16[192,768]{1,0:T(8,128)(2,1)S(1)} %collective-permute-done.32.refs_9_) | copy-start | bytes 884740
  247.8 21.6 %collective-permute-start.34 = (bf16[192,768]{1,0:T(8,128)(2,1)S(1)}, bf16[192,768]{1,0:T(8,128)(2,1)S(1)}, u32[]{:S(2)}, u32[]{:S(2)}) collective-permute-start(bf16[192,768]{1,0:T(8,128)(2,1)S(1)} %copy-done.33), channel_id=1, source_target_pairs={{0,24},{4,28},{8,16},{12,20},{16,8},{20,12},{24,0},{28,4},{1,25},{... | collective-permute-start | bytes 884744 | tf_op jit(solution)/shard_map/ppermute | solution.py:1198
  274.7 79.5 %all-to-all-start.4 = ((bf16[8,2,128,768]{3,2,1,0:T(8,128)(2,1)}), bf16[8,2,128,768]{3,2,1,0:T(8,128)(2,1)S(1)}, u32[]{:S(2)}, u32[]{:S(2)}) async-start(bf16[8,2,128,768]{3,2,1,0:T(8,128)(2,1)} %get-tuple-element.203), calls=%async_computation.4 | async-start | bytes 6291456 | tf_op jit(solution)/shard_map/all_to_all | solution.py:1353
  278.3 4.1 %collective-permute-start.20 = (bf16[512,768]{1,0:T(8,128)(2,1)}, bf16[512,768]{1,0:T(8,128)(2,1)S(1)}, u32[]{:S(2)}, u32[]{:S(2)}) collective-permute-start(bf16[512,768]{1,0:T(8,128)(2,1)} %get-tuple-element.152), channel_id=1, source_target_pairs={{0,4},{4,0},{8,12},{12,8},{16,20},{20,16},{24,28},{28,24},{1,5},{5... | collective-permute-start | bytes 2359304 | tf_op jit(solution)/shard_map/ppermute | solution.py:1198
  278.4 12.1 %collective-permute-start.35 = (bf16[304,768]{1,0:T(8,128)(2,1)}, bf16[304,768]{1,0:T(8,128)(2,1)S(1)}, u32[]{:S(2)}, u32[]{:S(2)}) collective-permute-start(bf16[304,768]{1,0:T(8,128)(2,1)} %get-tuple-element.207), channel_id=1, source_target_pairs={{0,1},{1,2},{2,3},{3,0},{4,5},{5,6},{6,7},{7,4},{8,9},{9,10},{10,1... | collective-permute-start | bytes 1400840 | tf_op jit(solution)/shard_map/ppermute | solution.py:1203
  278.4 40.3 %collective-permute-start.36 = (bf16[304,768]{1,0:T(8,128)(2,1)}, bf16[304,768]{1,0:T(8,128)(2,1)S(1)}, u32[]{:S(2)}, u32[]{:S(2)}) collective-permute-start(bf16[304,768]{1,0:T(8,128)(2,1)} %get-tuple-element.208), channel_id=1, source_target_pairs={{0,2},{1,3},{2,0},{3,1},{4,6},{5,7},{6,4},{7,5},{8,10},{9,11},{10,... | collective-permute-start | bytes 1400840 | tf_op jit(solution)/shard_map/ppermute | solution.py:1203
  281.0 41.4 %collective-permute-start.37 = (bf16[304,768]{1,0:T(8,128)(2,1)}, bf16[304,768]{1,0:T(8,128)(2,1)S(1)}, u32[]{:S(2)}, u32[]{:S(2)}) collective-permute-start(bf16[304,768]{1,0:T(8,128)(2,1)} %get-tuple-element.209), channel_id=1, source_target_pairs={{0,3},{1,0},{2,1},{3,2},{4,7},{5,4},{6,5},{7,6},{8,11},{9,8},{10,9... | collective-permute-start | bytes 1400840 | tf_op jit(solution)/shard_map/ppermute | solution.py:1203
  283.3 39.1 %copy-start.15 = (bf16[304,768]{1,0:T(8,128)(2,1)S(1)}, bf16[304,768]{1,0:T(8,128)(2,1)}, u32[]{:S(2)}) copy-start(bf16[304,768]{1,0:T(8,128)(2,1)} %get-tuple-element.206) | copy-start | bytes 1400836
  288.0 34.6 %copy-start.20 = (bf16[96,768]{1,0:T(8,128)(2,1)S(1)}, bf16[96,768]{1,0:T(8,128)(2,1)}, u32[]{:S(2)}) copy-start(bf16[96,768]{1,0:T(8,128)(2,1)} %get-tuple-element.205) | copy-start | bytes 442372
  323.6 16.2 %collective-permute-start.40 = (bf16[400,768]{1,0:T(8,128)(2,1)}, bf16[400,768]{1,0:T(8,128)(2,1)}, u32[]{:S(2)}, u32[]{:S(2)}) collective-permute-start(bf16[400,768]{1,0:T(8,128)(2,1)} %pad_maximum_fusion.refs_0_), channel_id=1, source_target_pairs={{0,24},{4,28},{8,16},{12,20},{16,8},{20,12},{24,0},{28,4},{1,25},{... | collective-permute-start | bytes 1843208 | tf_op jit(solution)/shard_map/ppermute | solution.py:1198
  325.3 27.3 %collective-permute-start.38 = (bf16[400,768]{1,0:T(8,128)(2,1)}, bf16[400,768]{1,0:T(8,128)(2,1)}, u32[]{:S(2)}, u32[]{:S(2)}) collective-permute-start(bf16[400,768]{1,0:T(8,128)(2,1)} %pad_maximum_fusion.refs_0_), channel_id=1, source_target_pairs={{0,8},{4,12},{8,0},{12,4},{16,24},{20,28},{24,16},{28,20},{1,9},{5... | collective-permute-start | bytes 1843208 | tf_op jit(solution)/shard_map/ppermute | solution.py:1198
  325.6 28.3 %collective-permute-start.39 = (bf16[400,768]{1,0:T(8,128)(2,1)}, bf16[400,768]{1,0:T(8,128)(2,1)}, u32[]{:S(2)}, u32[]{:S(2)}) collective-permute-start(bf16[400,768]{1,0:T(8,128)(2,1)} %pad_maximum_fusion.refs_0_), channel_id=1, source_target_pairs={{0,16},{4,20},{8,24},{12,28},{16,0},{20,4},{24,8},{28,12},{1,17},{... | collective-permute-start | bytes 1843208 | tf_op jit(solution)/shard_map/ppermute | solution.py:1198
  339.7 21.5 %collective-permute-start.44 = (bf16[400,768]{1,0:T(8,128)(2,1)}, bf16[400,768]{1,0:T(8,128)(2,1)}, u32[]{:S(2)}, u32[]{:S(2)}) collective-permute-start(bf16[400,768]{1,0:T(8,128)(2,1)} %collective-permute-done.40.refs_3_), channel_id=1, source_target_pairs={{0,4},{4,0},{8,12},{12,8},{16,20},{20,16},{24,28},{28,24},{1,5},{5... | collective-permute-start | bytes 1843208 | tf_op jit(solution)/shard_map/ppermute | solution.py:1198
  342.0 19.2 %collective-permute-start.41 = (bf16[400,768]{1,0:T(8,128)(2,1)}, bf16[400,768]{1,0:T(8,128)(2,1)}, u32[]{:S(2)}, u32[]{:S(2)}) collective-permute-start(bf16[400,768]{1,0:T(8,128)(2,1)} %pad_maximum_fusion.refs_0_), channel_id=1, source_target_pairs={{0,4},{4,0},{8,12},{12,8},{16,20},{20,16},{24,28},{28,24},{1,5},{5... | collective-permute-start | bytes 1843208 | tf_op jit(solution)/shard_map/ppermute | solution.py:1198
  352.6 8.6 %collective-permute-start.42 = (bf16[400,768]{1,0:T(8,128)(2,1)}, bf16[400,768]{1,0:T(8,128)(2,1)}, u32[]{:S(2)}, u32[]{:S(2)}) collective-permute-start(bf16[400,768]{1,0:T(8,128)(2,1)} %collective-permute-done.38.refs_1_), channel_id=1, source_target_pairs={{0,4},{4,0},{8,12},{12,8},{16,20},{20,16},{24,28},{28,24},{1,5},{5... | collective-permute-start | bytes 1843208 | tf_op jit(solution)/shard_map/ppermute | solution.py:1198
  354.0 7.3 %collective-permute-start.43 = (bf16[400,768]{1,0:T(8,128)(2,1)}, bf16[400,768]{1,0:T(8,128)(2,1)}, u32[]{:S(2)}, u32[]{:S(2)}) collective-permute-start(bf16[400,768]{1,0:T(8,128)(2,1)} %collective-permute-done.39.refs_2_), channel_id=1, source_target_pairs={{0,4},{4,0},{8,12},{12,8},{16,20},{20,16},{24,28},{28,24},{1,5},{5... | collective-permute-start | bytes 1843208 | tf_op jit(solution)/shard_map/ppermute | solution.py:1198
  (20 other events, 38.8 us)

commit v2 on v1

--- a/solution.py
+++ b/solution.py
@@ -13,7 +13,7 @@
 BLOCK = 256
 TILE = 256
 VMEM_BYTES = 56 * 1024 * 1024
-COST = 0.5
+COST = 4
 
 norm_eps = 1e-06
 F32 = jnp.float32
@@ -188,11 +188,17 @@
     span = offsets_ref.shape[1]
     for head in range(heads):
         line = jnp.broadcast_to(offsets_ref[head : head + 1, :], (8, span))
-        for group in range(BLOCK // 8):
+        for group in range(128 // 8):
             turned = pltpu.roll(
                 line, (group * 8 - (BLOCK - 1)) % span, 1, stride=1, stride_axis=0
             )
-            bias_ref[head, group * 8 : group * 8 + 8, :] = turned[:, :width]
+            for first in range(0, BLOCK, 128):
+                rows = slice(first + group * 8, first + group * 8 + 8)
+                if first == 0:
+                    bias_ref[head, rows, :] = turned[:, :width]
+                else:
+                    bias_ref[head, rows, :first] = turned[:, span - first :]
+                    bias_ref[head, rows, first:] = turned[:, : width - first]
 
 
 def fold_diagonals(bias_grad_ref, offsets_grad_ref):
@@ -200,10 +206,15 @@
     span = offsets_grad_ref.shape[1]
     for head in range(heads):
         total = jnp.zeros((8, span), F32)
-        for group in range(BLOCK // 8):
-            rows = bias_grad_ref[head, group * 8 : group * 8 + 8, :]
-            wide = jnp.concatenate([rows, jnp.zeros((8, span - width), F32)], axis=1)
-            total = total + pltpu.roll(wide, (BLOCK - 8 - group * 8) % span, 1)
+        for group in range(128 // 8):
+            part = jnp.zeros((8, span), F32)
+            for first in range(0, BLOCK, 128):
+                rows = bias_grad_ref[head, first + group * 8 : first + group * 8 + 8, :]
+                turned = [rows[:, first:], jnp.zeros((8, span - width), F32)]
+                if first > 0:
+                    turned.append(rows[:, :first])
+                part = part + jnp.concatenate(turned, axis=1)
+            total = total + pltpu.roll(part, (BLOCK - 8 - group * 8) % span, 1)
         line = jnp.zeros((1, span), F32)
         for row in range(8):
             line = line + pltpu.roll(total, (7 - row) % span, 1)[row : row + 1, :]
@@ -1053,80 +1064,97 @@
 def unpack_kernel(where_ref, *refs):
     piece_refs = refs[:8]
     gate_ref, up_ref, down_ref, q_ref, k_ref, v_ref, out_ref, small_ref = refs[8:]
+    step = pl.program_id(0)
     chip, core = where_ref[0], where_ref[1]
-    depth, units = gate_ref.shape
-    model = down_ref.shape[1]
-    part = down_ref.shape[0] // 2
-    quarter, slab = depth // 4, depth // 2
+    rows_here, units = gate_ref.shape
+    _, _, rows, model = down_ref.shape
+    quarter, slab = rows_here // 2, rows_here
+    part = rows * 4
     wide = units // 2 // model
     planes = units // 2 // part
     width, lanes, half = model // 4, model // 2, slab // 2
-    small = jnp.zeros(small_ref.shape, F32)
+    used = 3 * width
+    low = 2 * wide * quarter
+    last = low + rows
     for far in range(8):
         away, other = far % 4, far // 4
         from_core = core if other == 0 else 1 - core
         from_chip = jnp.bitwise_xor(chip, away)
         from_x, from_y = lax.rem(from_chip, 2), from_chip // 2
         piece_ref = piece_refs[far]
-        gate_rows = block_rows(from_x * 2 + from_y, quarter)
-        for plane in range(planes):
-            index, at = divmod(plane * part, model)
-            columns = pl.ds(pl.multiple_of(plane * 2 * part + from_core * part, 128), part)
-            rows = slice(index * quarter, (index + 1) * quarter)
-            gate_ref[gate_rows, columns] = piece_ref[rows, at : at + part].astype(F32)
-            rows = slice((wide + index) * quarter, (wide + index + 1) * quarter)
-            up_ref[gate_rows, columns] = piece_ref[rows, at : at + part].astype(F32)
-        low = 2 * wide * quarter
-        rows = part // 4
-        down_ref[block_rows(from_core * 4 + from_y * 2 + from_x, rows), :] = piece_ref[
-            low : low + rows, :
-        ].astype(F32)
-        low = low + rows
-        used = 3 * width
-        out_ref[block_rows(from_core * 2 + from_x, half), block_rows(from_y, lanes)] = (
-            jnp.concatenate(
-                [piece_ref[low : low + half, used:], piece_ref[low + half : low + slab, used:]],
+
+        @pl.when(from_x == step)
+        def _(piece_ref=piece_ref, from_core=from_core, from_y=from_y):
+            to_rows = block_rows(from_y, quarter)
+            for plane in range(planes):
+                index, at = divmod(plane * part, model)
+                columns = pl.ds(pl.multiple_of(plane * 2 * part + from_core * part, 128), part)
+                own = slice(index * quarter, (index + 1) * quarter)
+                gate_ref[to_rows, columns] = piece_ref[own, at : at + part].astype(F32)
+                own = slice((wide + index) * quarter, (wide + index + 1) * quarter)
+                up_ref[to_rows, columns] = piece_ref[own, at : at + part].astype(F32)
+            down_ref[from_core * 2 + from_y, 0] = piece_ref[low:last, :].astype(F32)
+            out_ref[from_core, 0, :, block_rows(from_y, lanes)] = jnp.concatenate(
+                [piece_ref[last : last + half, used:], piece_ref[last + half : last + slab, used:]],
                 axis=1,
             ).astype(F32)
-        )
+
         for home in range(4):
 
-            @pl.when(from_chip == home)
-            def _(home=home, piece_ref=piece_ref, from_core=from_core, low=low):
+            @pl.when((from_chip == home) & (from_x == step))
+            def _(home=home, piece_ref=piece_ref, from_core=from_core):
                 to_lanes = slice(home * width, (home + 1) * width)
                 for kind, target_ref in enumerate((q_ref, k_ref, v_ref)):
                     target_ref[block_rows(from_core, slab), to_lanes] = piece_ref[
-                        low : low + slab, kind * width : (kind + 1) * width
+                        last : last + slab, kind * width : (kind + 1) * width
                     ].astype(F32)
 
-        small = small + piece_ref[low + slab :, :].astype(F32)
-    small_ref[...] = small
+    @pl.when(step == 0)
+    def _():
+        small = piece_refs[0][last + slab :, :].astype(F32)
+        for piece_ref in piece_refs[1:]:
+            small = small + piece_ref[last + slab :, :].astype(F32)
+        small_ref[...] = small
 
 
 def unpack(where, pieces, depth, units):
     rows, model = pieces[0].shape
     planes = model // depth
     part = units // planes
-    taken = units // 2 // model * depth // 2 + part // 8 + depth // 2
-    vmem = pl.BlockSpec(memory_space=pltpu.VMEM)
-    return pl.pallas_call(
+    wide, slab = units // 2 // model, depth // 2
+    taken = wide * slab + part // 8 + slab
+    whole = lambda dims: pl.BlockSpec(dims, lambda s: (0,) * len(dims))
+    by_rows = pl.BlockSpec((slab, units), lambda s: (s, 0))
+    square = (depth, model)
+    gate, up, down, query, key, value, out, small = pl.pallas_call(
         unpack_kernel,
-        in_specs=[SMEM] + [vmem] * 8,
-        out_specs=[vmem] * 8,
+        grid=(2,),
+        in_specs=[SMEM] + [whole((rows, model))] * 8,
+        out_specs=[
+            by_rows,
+            by_rows,
+            pl.BlockSpec((4, 1, part // 8, model), lambda s: (0, s, 0, 0)),
+            whole(square),
+            whole(square),
+            whole(square),
+            pl.BlockSpec((2, 1, slab // 2, model), lambda s: (0, s, 0, 0)),
+            whole((rows - taken, model)),
+        ],
         out_shape=[
             shape_of((depth, units), F32),
             shape_of((depth, units), F32),
-            shape_of((part, model), F32),
-            shape_of((depth, model), F32),
-            shape_of((depth, model), F32),
-            shape_of((depth, model), F32),
-            shape_of((depth, model), F32),
+            shape_of((4, 2, part // 8, model), F32),
+            shape_of(square, F32),
+            shape_of(square, F32),
+            shape_of(square, F32),
+            shape_of((2, 2, slab // 2, model), F32),
             shape_of((rows - taken, model), F32),
         ],
         compiler_params=params(),
         cost_estimate=cost(0, 24e6),
         name="unpack",
     )(where, *pieces)
+    return gate, up, down.reshape(part, model), query, key, value, out.reshape(square), small
 
 
 def finish_out_kernel(order_ref, lens_ref, start_ref, res_ref, own_ref, recv_ref, out_ref):

time: 378 us -> 375 us (level)
  waiting for transfers between devices: 119 us -> 113 us
  Pallas kernels: 152 us -> 157 us
    ppermute x15, starting transfers between devices: 13.8 us -> 28 us  [shift(): lax.ppermute(values, 'fsdp', [(i, (i + places) % count) for i in range(co...]
    all_to_all x1, starting transfers between devices: 12.6 us -> 4.32 us  [per_device_plane(): attn_first = lax.all_to_all(first_out, 'ctx', 0, 0)]
    pallas_call x2, Pallas kernels: 22.5 us -> 28.8 us  [attn_forward(): pl.pallas_call(attn_forward_first_kernel if slot == 0 else attn_forward_s...]
    ppermute x30, starting transfers between devices: 31.2 us -> 25.8 us  [swap(): return lax.ppermute(values, 'ctx', [(i, i ^ bits) for i in range(count)])]
    all_to_all x1, waiting for transfers between devices: 18.9 us -> 14.2 us  [per_device_plane(): attn = [attn_first, lax.all_to_all(second_out, 'ctx', 0, 0)]]
    ppermute x30, waiting for transfers between devices: 50.4 us -> 46.5 us  [swap(): return lax.ppermute(values, 'ctx', [(i, i ^ bits) for i in range(count)])]
    unnamed x68 -> x72, local copies, waits for them, and re-layouts: 9.81 us -> 8.82 us
  transfers between devices with their start and end apart: 50 -> 50, of which waited for: 14 -> 16; matrix products, arithmetic and copies ran while one was open for 2% -> 3% of each run, Pallas kernels for 27% -> 28%
where the time goes in v2:
time: 375 us; the launch traced here: 371 us
  Pallas kernels  157 us (42%)
  waiting for transfers between devices  113 us (30%)
  starting transfers between devices  75.3 us (20%)
  local copies, waits for them, and re-layouts  17.8 us (5%)
  other arithmetic  3.77 us (1%)
    ppermute x15, waiting for transfers between devices, shift(): lax.ppermute(values, 'fsdp', [(i, (i + places) % count) for i in range(co...  49.7 us
    ppermute x30, waiting for transfers between devices, swap(): return lax.ppermute(values, 'ctx', [(i, i ^ bits) for i in range(count)])  46.5 us
    pallas_call x1, Pallas kernels, attn_backward(): pl.pallas_call(attn_backward_kernel, grid=(slots,), in_specs=[SMEM, SMEM,...  35.9 us
    pallas_call x2, Pallas kernels, attn_forward(): pl.pallas_call(attn_forward_first_kernel if slot == 0 else attn_forward_s...  28.8 us
    ppermute x15, starting transfers between devices, shift(): lax.ppermute(values, 'fsdp', [(i, (i + places) % count) for i in range(co...  28 us
    ppermute x30, starting transfers between devices, swap(): return lax.ppermute(values, 'ctx', [(i, i ^ bits) for i in range(count)])  25.8 us
    pallas_call x1, Pallas kernels, ffn_first(): pl.pallas_call(ffn_first_kernel, grid=(units // tile,), in_specs=[SMEM, w...  25.7 us
    pallas_call x1, Pallas kernels, ffn_second(): pl.pallas_call(ffn_second_kernel, grid=(units // tile,), in_specs=[SMEM,...  15.8 us
  transfers between devices with their start and end apart: 50, of which 16 were waited for; matrix products, arithmetic and copies ran while one was open for 3% of the time, Pallas kernels for 28%

profile of v2, /device:TPU:9, one launch (start us, length us, event | category | flops | bytes accessed | tf_op | source)
XLA Modules:
  0.0 371.0 jit_solution(14527802271835044845)
XLA Ops:
  3.4 4.1 %pack_weights.1 = (bf16[2,192,768]{2,1,0:T(8,128)(2,1)}, bf16[2,192,768]{2,1,0:T(8,128)(2,1)}, bf16[288,768]{1,0:T(8,128)(2,1)}, bf16[288,768]{1,0:T(8,128)(2,1)...) custom-call(s32[3]{0:T(128)} %pad_add_fusion.where_ref, bf16[192,3072]{1,0:T(8,128)(2,1)} %gate_ref.1, ...), custom_call_target="tpu_custom_call" | custom-call | bytes 64000000 | tf_op jit(solution)/shard_map/pack_weights/pallas_call | solution.py:102
  7.5 3.0 prepare.1
  10.6 4.4 %all-to-all-start = ((bf16[8,2,128,768]{3,2,1,0:T(8,128)(2,1)}), bf16[8,2,128,768]{3,2,1,0:T(8,128)(2,1)S(1)}, u32[]{:S(2)}, u32[]{:S(2)}) async-start(bf16[8,2,128,768]{3,2,1,0:T(8,128)(2,1)} %bitcast.12), calls=%async_computation | async-start | bytes 6291456 | tf_op jit(solution)/shard_map/all_to_all | solution.py:1283
  15.0 1.3 collective-permute-start
  17.2 7.3 %collective-permute-done.w1_ref.a1_ref = bf16[208,768]{1,0:T(8,128)(2,1)} collective-permute-done((bf16[208,768]{1,0:T(8,128)(2,1)}, bf16[208,768]{1,0:T(8,128)(2,1)}, u32[]{:S(2)}, u32[]{:S(2)}) %collective-permute-start) | collective-permute-done | bytes 319520 | tf_op jit(solution)/shard_map/ppermute | solution.py:1231
  24.5 1.4 collective-permute-start.1
  26.2 6.4 %collective-permute-done.2.w3_ref.a3_ref = bf16[208,768]{1,0:T(8,128)(2,1)} collective-permute-done((bf16[208,768]{1,0:T(8,128)(2,1)}, bf16[208,768]{1,0:T(8,128)(2,1)}, u32[]{:S(2)}, u32[]{:S(2)}) %collective-permute-start.2) | collective-permute-done | bytes 319520 | tf_op jit(solution)/shard_map/ppermute | solution.py:1231
  32.7 1.5 collective-permute-start.8
  35.6 1.6 collective-permute-start.3
  37.2 0.9 collective-permute-done.1.w2_ref.a2_ref
  38.9 3.6 collective-permute-start.4
  43.2 1.0 fusion.off_ref
  44.2 2.1 collective-permute-start.7
  46.9 2.5 all-to-all-done.tok_ref
  49.4 1.6 copy-done.1
  51.1 14.7 %attn_forward.2 = (bf16[8,1,192,128]{3,2,1,0:T(8,128)(2,1)}, f32[2,1024,256]{2,1,0:T(8,128)}, bf16[2,1024,192]{2,1,0:T(8,128)(2,1)}, bf16[2,1024,192]{2,1,0:T(8,...) custom-call(s32[4]{0:T(128)} %get-tuple-element.119.lens_ref, s32[3]{0:T(128)} %pad_add_fusion.where_ref, ...), custom_call_target="tpu_custom_call" | custom-call | flops 16508780544 | bytes 18874368 | tf_op jit(solution)/shard_map/attn_forward/pallas_call | solution.py:358
  65.8 0.9 collective-permute-done.7.y1
  66.7 1.6 collective-permute-start.11
  68.3 2.1 collective-permute-start.10
  70.5 4.3 %all-to-all-start.1 = ((bf16[8,1,192,128]{3,2,1,0:T(8,128)(2,1)}), bf16[8,1,192,128]{3,2,1,0:T(8,128)(2,1)S(1)}, u32[]{:S(2)}, u32[]{:S(2)}) async-start(bf16[8,1,192,128]{3,2,1,0:T(8,128)(2,1)} %get-tuple-element.134), calls=%async_computation.1 | async-start | bytes 786432 | tf_op jit(solution)/shard_map/all_to_all | solution.py:1312
  74.8 4.6 %collective-permute-start.15 = (bf16[288,768]{1,0:T(8,128)(2,1)}, bf16[288,768]{1,0:T(8,128)(2,1)S(1)}, u32[]{:S(2)}, u32[]{:S(2)}) collective-permute-start(bf16[288,768]{1,0:T(8,128)(2,1)} %collective-permute-done.7.y1), channel_id=1, source_target_pairs={{0,1},{1,2},{2,3},{3,0},{4,5},{5,6},{6,7},{7,4},{8,9},{9,10},{10,1... | collective-permute-start | bytes 1327112 | tf_op jit(solution)/shard_map/ppermute | solution.py:1231
  79.4 14.1 %attn_forward.3 = (bf16[8,1,192,128]{3,2,1,0:T(8,128)(2,1)}, f32[2,1024,256]{2,1,0:T(8,128)}, bf16[2,1024,192]{2,1,0:T(8,128)(2,1)}, bf16[2,1024,192]{2,1,0:T(8,128)(2,1)}, bf16[2,1024,192]{2,1,0:T(8,128)(2,1)}) custom-call(s32[4]{0:T(128)} %get-tuple-element.119.lens_ref, ...), custom_call_target="tpu_custom_call", output_to_operand_aliasing={{1}: (6, {}), {2}: (7, {}), {3}: (8, {}), {4}: (9, {})} | custom-call | flops 16508780544 | bytes 18874368 | tf_op jit(solution)/shard_map/attn_forward/pallas_call | solution.py:358
  93.5 1.4 collective-permute-start.14
  94.9 1.3 collective-permute-start.13
  96.6 1.4 collective-permute-start.16
  98.0 4.4 %all-to-all-start.2 = ((bf16[8,1,192,128]{3,2,1,0:T(8,128)(2,1)}), bf16[8,1,192,128]{3,2,1,0:T(8,128)(2,1)S(1)}, u32[]{:S(2)}, u32[]{:S(2)}) async-start(bf16[8,1,192,128]{3,2,1,0:T(8,128)(2,1)} %get-tuple-element.138), calls=%async_computation.2 | async-start | bytes 786432 | tf_op jit(solution)/shard_map/all_to_all | solution.py:1316
  102.4 4.3 %sort_rows.1 = (bf16[512,768]{1,0:T(8,128)(2,1)}, bf16[512,768]{1,0:T(8,128)(2,1)}) custom-call(s32[4]{0:T(128)} %get-tuple-element.118.order_ref, s32[4]{0:T(128)} %get-tuple-element.119.lens_ref, s32[1]{0:T(128)} %bitcast.3.start_ref, bf16[4,128,768]{2,1,0:T(8,128)(2,1)} %tok_ref.2, bf16[4,128,768]{2,1,0:T(8,128)(2,1)} %cot_ref.1), custom_call_target="tpu_custom_call" | custom-call | bytes 12000000 | tf_op jit(solution)/shard_map/sort_rows/pallas_call | solution.py:168
  107.4 14.2 %all-to-all-done.2.attn1_ref = bf16[8,1,192,128]{3,2,1,0:T(8,128)(2,1)S(1)} async-done(((bf16[8,1,192,128]{3,2,1,0:T(8,128)(2,1)}), bf16[8,1,192,128]{3,2,1,0:T(8,128)(2,1)S(1)}, u32[]{:S(2)}, u32[]{:S(2)}) %all-to-all-start.2) | async-done | bytes 393248 | tf_op jit(solution)/shard_map/all_to_all | solution.py:1316
  122.5 5.1 %out_project.1 = (f32[512,768]{1,0:T(8,128)}, bf16[512,768]{1,0:T(8,128)(2,1)}, bf16[768,768]{1,0:T(8,128)(2,1)}) custom-call(s32[3]{0:T(128)} %pad_add_fusion.where_ref, bf16[512,768]{1,0:T(8,128)(2,1)} %get-tuple-element.120.tok_ref, bf16[8,1,192,128]{3,2,1,0:T(8,128)(2,1)} %copy-done.12, bf16[8,1,192,128]{3,2,1,0:T(8,128)(2,1)} %copy-done.13, ...), custom_call_target="tpu_custom_call" | custom-call | flops 4831838208 | bytes 18874368 | tf_op jit(solution)/shard_map/out_project/pallas_call | solution.py:608
  128.2 1.8 collective-permute-done.19.dy_other_ref
  129.9 1.3 collective-permute-done.18.nf_other_ref
  132.2 25.7 %ffn_first.1 = (bf16[1024,1536]{1,0:T(8,128)(2,1)}, bf16[1024,1536]{1,0:T(8,128)(2,1)}, f32[512,768]{1,0:T(8,128)}, bf16[512,768]{1,0:T(8,128)(2,1)}, bf16[1536,...) custom-call(s32[3]{0:T(128)} %pad_add_fusion.where_ref, ...), custom_call_target="tpu_custom_call" | custom-call | flops 115964116992 | bytes 97517568 | tf_op jit(solution)/shard_map/ffn_first/pallas_call | solution.py:814
  158.9 11.6 %collective-permute-start.22 = (bf16[2,192,768]{2,1,0:T(8,128)(2,1)}, bf16[2,192,768]{2,1,0:T(8,128)(2,1)S(1)}, u32[]{:S(2)}, u32[]{:S(2)}) collective-permute-start(bf16[2,192,768]{2,1,0:T(8,128)(2,1)} %get-tuple-element.154), channel_id=1, source_target_pairs={{0,3},{1,0},{2,1},{3,2},{4,7},{5,4},{6,5},{7,6},{8,11},{9,8},{10,9... | collective-permute-start | bytes 1769480 | tf_op jit(solution)/shard_map/ppermute | solution.py:1231
  171.2 0.9 copy-done.27
  172.1 6.5 %out_back.1 = (bf16[8,2,192,128]{3,2,1,0:T(8,128)(2,1)}, f32[512,768]{1,0:T(8,128)}, f32[1,768]{1,0:T(1,128)}, bf16[4,96,768]{2,1,0:T(8,128)(2,1)}, bf16[4,96,768]{2,1,0:T(8,128)(2,1)}) custom-call(s32[3]{0:T(128)} %pad_add_fusion.where_ref, f32[512,768]{1,0:T(8,128)} %get-tuple-element.157.own_ref, bf16[512,768]{1,0:T(8,128)(2,1)} %copy-done.27, ...), custom_call_target="tpu_custom_call" | custom-call | flops 9663676416 | bytes 31457280 | tf_op jit(solution)/shard_map/out_back/pallas_call | solution.py:657
  178.7 4.8 %all-to-all-start.3 = ((bf16[8,2,192,128]{3,2,1,0:T(8,128)(2,1)}), bf16[8,2,192,128]{3,2,1,0:T(8,128)(2,1)S(1)}, u32[]{:S(2)}, u32[]{:S(2)}) async-start(bf16[8,2,192,128]{3,2,1,0:T(8,128)(2,1)} %get-tuple-element.160), calls=%async_computation.3 | async-start | bytes 1572864 | tf_op jit(solution)/shard_map/all_to_all | solution.py:1335
  183.5 15.8 %ffn_second.1 = (f32[512,768]{1,0:T(8,128)}, bf16[512,768]{1,0:T(8,128)(2,1)}, bf16[4,2,96,768]{3,2,1,0:T(8,128)(2,1)}, bf16[4,2,96,768]{3,2,1,0:T(8,128)(2,1)},...) custom-call(s32[3]{0:T(128)} %pad_add_fusion.where_ref, bf16[512,768]{1,0:T(8,128)(2,1)} %get-tuple-element.143.nf_own_ref, ...), custom_call_target="tpu_custom_call" | custom-call | flops 57982058496 | bytes 106954752 | tf_op jit(solution)/shard_map/ffn_second/pallas_call | solution.py:900
  200.1 1.8 collective-permute-start.24
  201.9 1.2 collective-permute-start.25
  203.0 35.9 %attn_backward.1 = (bf16[8,2,128,768]{3,2,1,0:T(8,128)(2,1)}, bf16[4,96,768]{2,1,0:T(8,128)(2,1)}, bf16[4,96,768]{2,1,0:T(8,128)(2,1)}, f32[1,768]{1,0:T(1,128)}, f32[3,2048]{1,0:T(4,128)}) custom-call(s32[4]{0:T(128)} %get-tuple-element.119.lens_ref, s32[3]{0:T(128)} %pad_add_fusion.where_ref, bf16[8,2,128,768]{3,2,1,0:T(8,128)(2,1)} %copy-done.1, ...), custom_call_target="tpu_custom_call" | custom-call | flops 157840048128 | bytes 62914560 | tf_op jit(solution)/shard_map/attn_backward/pallas_call | solution.py:525
  238.9 1.3 fusion.2
  240.8 3.2 by_chip.1
  244.4 4.3 %second_halves.1 = (bf16[4,2,48,768]{3,2,1,0:T(8,128)(2,1)}, bf16[4,2,48,768]{3,2,1,0:T(8,128)(2,1)}, bf16[4,96,768]{2,1,0:T(8,128)(2,1)}, bf16[4,96,768]{2,1,0:T(8,128)(2,1)}) custom-call(s32[3]{0:T(128)} %pad_add_fusion.where_ref, bf16[4,2,96,768]{3,2,1,0:T(8,128)(2,1)} %get-tuple-element.176.u_keep_ref, ...), custom_call_target="tpu_custom_call" | custom-call | bytes 28000000 | tf_op jit(solution)/shard_map/second_halves/pallas_call | solution.py:952
  249.3 0.9 collective-permute-start.28
  251.6 0.9 collective-permute-done.30.refs_7_
  252.5 1.0 collective-permute-start.33
  254.3 16.0 %collective-permute-done.33.refs_10_ = bf16[192,768]{1,0:T(8,128)(2,1)S(1)} collective-permute-done((bf16[192,768]{1,0:T(8,128)(2,1)S(1)}, bf16[192,768]{1,0:T(8,128)(2,1)S(1)}, u32[]{:S(2)}, u32[]{:S(2)}) %collective-permute-start.33) | collective-permute-done | bytes 294944 | tf_op jit(solution)/shard_map/ppermute | solution.py:1226
  271.7 3.9 %by_plane.1 = (bf16[304,768]{1,0:T(8,128)(2,1)}, bf16[304,768]{1,0:T(8,128)(2,1)}, bf16[304,768]{1,0:T(8,128)(2,1)}, bf16[304,768]{1,0:T(8,128)(2,1)}, bf16[96,768]{1,0:T(8,128)(2,1)}) custom-call(s32[3]{0:T(128)} %pad_add_fusion.where_ref, bf16[4,2,48,768]{3,2,1,0:T(8,128)(2,1)} %get-tuple-element.180.refs_0_, bf16[4,2,48,768]{3,2,1,0:T(8,128)(2,1)} %copy-done.6, ...), custom_call_target="tpu_custom_call" | custom-call | bytes 24000000 | tf_op jit(solution)/shard_map/by_plane/pallas_call | solution.py:1051
  275.6 3.6 all-to-all-start.4
  280.8 1.0 collective-permute-done.20.recv_ref
  282.7 4.7 %finish_out.1 = bf16[4,128,768]{2,1,0:T(8,128)(2,1)} custom-call(s32[4]{0:T(128)} %get-tuple-element.118.order_ref, s32[4]{0:T(128)} %get-tuple-element.119.lens_ref, s32[1]{0:T(128)} %bitcast.3.start_ref, f32[512,768]{1,0:T(8,128)} %get-tuple-element.142.res_ref, f32[512,768]{1,0:T(8,128)} %get-tuple-element.151.own_ref, bf16[512,768]{1,0:T(8,128)(2,1)} %copy-done.5), custom_call_target="tpu_custom_call" | custom-call | bytes 24000000 | tf_op jit(solution)/shard_map/finish_out/pallas_call | solution.py:1170
  287.4 4.0 %collective-permute-done.35 = bf16[304,768]{1,0:T(8,128)(2,1)S(1)} collective-permute-done((bf16[304,768]{1,0:T(8,128)(2,1)}, bf16[304,768]{1,0:T(8,128)(2,1)S(1)}, u32[]{:S(2)}, u32[]{:S(2)}) %collective-permute-start.35) | collective-permute-done | bytes 466976 | tf_op jit(solution)/shard_map/ppermute | solution.py:1231
  291.4 28.2 %collective-permute-done.36 = bf16[304,768]{1,0:T(8,128)(2,1)S(1)} collective-permute-done((bf16[304,768]{1,0:T(8,128)(2,1)}, bf16[304,768]{1,0:T(8,128)(2,1)S(1)}, u32[]{:S(2)}, u32[]{:S(2)}) %collective-permute-start.36) | collective-permute-done | bytes 466976 | tf_op jit(solution)/shard_map/ppermute | solution.py:1231
  319.6 2.0 collective-permute-done.37
  321.9 0.9 pad_maximum_fusion.refs_0_
  322.8 2.7 collective-permute-start.40
  325.7 13.9 %collective-permute-done.40.refs_3_ = bf16[400,768]{1,0:T(8,128)(2,1)} collective-permute-done((bf16[400,768]{1,0:T(8,128)(2,1)}, bf16[400,768]{1,0:T(8,128)(2,1)}, u32[]{:S(2)}, u32[]{:S(2)}) %collective-permute-start.40) | collective-permute-done | bytes 614432 | tf_op jit(solution)/shard_map/ppermute | solution.py:1226
  339.6 1.6 collective-permute-start.44
  341.2 11.5 %collective-permute-done.38.refs_1_ = bf16[400,768]{1,0:T(8,128)(2,1)} collective-permute-done((bf16[400,768]{1,0:T(8,128)(2,1)}, bf16[400,768]{1,0:T(8,128)(2,1)}, u32[]{:S(2)}, u32[]{:S(2)}) %collective-permute-start.38) | collective-permute-done | bytes 614432 | tf_op jit(solution)/shard_map/ppermute | solution.py:1226
  352.7 1.3 collective-permute-start.42
  354.1 1.6 copy-done
  355.7 5.4 %finish_tokens.1 = f32[4,128,768]{2,1,0:T(8,128)} custom-call(s32[4]{0:T(128)} %get-tuple-element.118.order_ref, bf16[4,4,128,768]{3,2,1,0:T(8,128)(2,1)} %bitcast.11, bf16[512,768]{1,0:T(8,128)(2,1)} %get-tuple-element.120.tok_ref, f32[512,768]{1,0:T(8,128)} %get-tuple-element.204.dres_ref, f32[1,768]{1,0:T(1,128)} %reshape.130.gain_ref), custom_call_target="tpu_custom_call" | custom-call | bytes 40000000 | tf_op jit(solution)/shard_map/finish_tokens/pallas_call | solution.py:1201
  361.1 6.8 %unpack.1 = (f32[192,3072]{1,0:T(8,128)}, f32[192,3072]{1,0:T(8,128)}, f32[4,2,96,768]{3,2,1,0:T(8,128)}, f32[192,768]{1,0:T(8,128)}, f32[192,768]{1,0:T(8,128)}...) custom-call(s32[3]{0:T(128)} %pad_add_fusion.where_ref, ...), custom_call_target="tpu_custom_call" | custom-call | bytes 96000000 | tf_op jit(solution)/shard_map/unpack/pallas_call | solution.py:1129
  368.7 1.4 fusion.16
  (158 shorter events, 23.0 us)
Async XLA Ops:
  10.5 15.3 %copy-start.20 = (s32[2047]{0:T(1024)S(1)}, s32[2047]{0:T(1024)}, u32[]{:S(2)}) copy-start(s32[2047]{0:T(1024)} %param.17) | copy-start | bytes 24568
  10.6 38.9 %all-to-all-start = ((bf16[8,2,128,768]{3,2,1,0:T(8,128)(2,1)}), bf16[8,2,128,768]{3,2,1,0:T(8,128)(2,1)S(1)}, u32[]{:S(2)}, u32[]{:S(2)}) async-start(bf16[8,2,128,768]{3,2,1,0:T(8,128)(2,1)} %bitcast.12), calls=%async_computation | async-start | bytes 6291456 | tf_op jit(solution)/shard_map/all_to_all | solution.py:1283
  15.0 9.5 %collective-permute-start = (bf16[208,768]{1,0:T(8,128)(2,1)}, bf16[208,768]{1,0:T(8,128)(2,1)}, u32[]{:S(2)}, u32[]{:S(2)}) collective-permute-start(bf16[208,768]{1,0:T(8,128)(2,1)} %get-tuple-element.116), channel_id=1, source_target_pairs={{0,1},{1,2},{2,3},{3,0},{4,5},{5,6},{6,7},{7,4},{8,9},{9,10},{10,1... | collective-permute-start | bytes 958472 | tf_op jit(solution)/shard_map/ppermute | solution.py:1231
  16.3 16.4 %collective-permute-start.2 = (bf16[208,768]{1,0:T(8,128)(2,1)}, bf16[208,768]{1,0:T(8,128)(2,1)}, u32[]{:S(2)}, u32[]{:S(2)}) collective-permute-start(bf16[208,768]{1,0:T(8,128)(2,1)} %get-tuple-element.116), channel_id=1, source_target_pairs={{0,3},{1,0},{2,1},{3,2},{4,7},{5,4},{6,5},{7,6},{8,11},{9,8},{10,9... | collective-permute-start | bytes 958472 | tf_op jit(solution)/shard_map/ppermute | solution.py:1231
  24.5 13.6 %collective-permute-start.1 = (bf16[208,768]{1,0:T(8,128)(2,1)}, bf16[208,768]{1,0:T(8,128)(2,1)S(1)}, u32[]{:S(2)}, u32[]{:S(2)}) collective-permute-start(bf16[208,768]{1,0:T(8,128)(2,1)} %collective-permute-done.w1_ref.a1_ref), channel_id=1, source_target_pairs={{0,1},{1,2},{2,3},{3,0},{4,5},{5,6},{6,7},{7,4},{8,9},{9,10},{10,1... | collective-permute-start | bytes 958472 | tf_op jit(solution)/shard_map/ppermute | solution.py:1231
  26.2 39.5 %copy-start.2 = (pred[2047,32]{1,0:T(8,128)(4,1)}, pred[2047,32]{1,0:T(8,128)(4,1)S(1)}, u32[]{:S(2)}) copy-start(pred[2047,32]{1,0:T(8,128)(4,1)S(1)} %iota_compare_fusion) | copy-start | bytes 196516
  32.7 33.1 %collective-permute-start.6 = (bf16[288,768]{1,0:T(8,128)(2,1)}, bf16[288,768]{1,0:T(8,128)(2,1)}, u32[]{:S(2)}, u32[]{:S(2)}) collective-permute-start(bf16[288,768]{1,0:T(8,128)(2,1)} %get-tuple-element.130), channel_id=1, source_target_pairs={{0,1},{1,2},{2,3},{3,0},{4,5},{5,6},{6,7},{7,4},{8,9},{9,10},{10,1... | collective-permute-start | bytes 1327112 | tf_op jit(solution)/shard_map/ppermute | solution.py:1231
  32.7 60.8 %collective-permute-start.8 = (bf16[288,768]{1,0:T(8,128)(2,1)}, bf16[288,768]{1,0:T(8,128)(2,1)}, u32[]{:S(2)}, u32[]{:S(2)}) collective-permute-start(bf16[288,768]{1,0:T(8,128)(2,1)} %get-tuple-element.130), channel_id=1, source_target_pairs={{0,3},{1,0},{2,1},{3,2},{4,7},{5,4},{6,5},{7,6},{8,11},{9,8},{10,9... | collective-permute-start | bytes 1327112 | tf_op jit(solution)/shard_map/ppermute | solution.py:1231
  35.6 8.6 %collective-permute-start.3 = (bf16[208,768]{1,0:T(8,128)(2,1)}, bf16[208,768]{1,0:T(8,128)(2,1)}, u32[]{:S(2)}, u32[]{:S(2)}) collective-permute-start(bf16[208,768]{1,0:T(8,128)(2,1)} %collective-permute-done.w1_ref.a1_ref), channel_id=1, source_target_pairs={{0,4},{4,0},{8,12},{12,8},{16,20},{20,16},{24,28},{28,24},{1,5},{5... | collective-permute-start | bytes 958472 | tf_op jit(solution)/shard_map/ppermute | solution.py:1226
  37.2 9.0 %collective-permute-start.5 = (bf16[208,768]{1,0:T(8,128)(2,1)}, bf16[208,768]{1,0:T(8,128)(2,1)}, u32[]{:S(2)}, u32[]{:S(2)}) collective-permute-start(bf16[208,768]{1,0:T(8,128)(2,1)} %collective-permute-done.2.w3_ref.a3_ref), channel_id=1, source_target_pairs={{0,4},{4,0},{8,12},{12,8},{16,20},{20,16},{24,28},{28,24},{1,5},{5... | collective-permute-start | bytes 958472 | tf_op jit(solution)/shard_map/ppermute | solution.py:1226
  38.9 8.0 %collective-permute-start.4 = (bf16[208,768]{1,0:T(8,128)(2,1)}, bf16[208,768]{1,0:T(8,128)(2,1)}, u32[]{:S(2)}, u32[]{:S(2)}) collective-permute-start(bf16[208,768]{1,0:T(8,128)(2,1)} %copy-done.23), channel_id=1, source_target_pairs={{0,4},{4,0},{8,12},{12,8},{16,20},{20,16},{24,28},{28,24},{1,5},{5... | collective-permute-start | bytes 958472 | tf_op jit(solution)/shard_map/ppermute | solution.py:1226
  44.2 22.5 %collective-permute-start.7 = (bf16[288,768]{1,0:T(8,128)(2,1)}, bf16[288,768]{1,0:T(8,128)(2,1)}, u32[]{:S(2)}, u32[]{:S(2)}) collective-permute-start(bf16[288,768]{1,0:T(8,128)(2,1)} %get-tuple-element.132), channel_id=1, source_target_pairs={{0,1},{1,2},{2,3},{3,0},{4,5},{5,6},{6,7},{7,4},{8,9},{9,10},{10,1... | collective-permute-start | bytes 1327112 | tf_op jit(solution)/shard_map/ppermute | solution.py:1231
  46.3 48.7 %collective-permute-start.9 = (bf16[288,768]{1,0:T(8,128)(2,1)}, bf16[288,768]{1,0:T(8,128)(2,1)}, u32[]{:S(2)}, u32[]{:S(2)}) collective-permute-start(bf16[288,768]{1,0:T(8,128)(2,1)} %get-tuple-element.132), channel_id=1, source_target_pairs={{0,3},{1,0},{2,1},{3,2},{4,7},{5,4},{6,5},{7,6},{8,11},{9,8},{10,9... | collective-permute-start | bytes 1327112 | tf_op jit(solution)/shard_map/ppermute | solution.py:1231
  66.7 29.5 %collective-permute-start.11 = (bf16[288,768]{1,0:T(8,128)(2,1)}, bf16[288,768]{1,0:T(8,128)(2,1)S(1)}, u32[]{:S(2)}, u32[]{:S(2)}) collective-permute-start(bf16[288,768]{1,0:T(8,128)(2,1)} %collective-permute-done.6.x1), channel_id=1, source_target_pairs={{0,1},{1,2},{2,3},{3,0},{4,5},{5,6},{6,7},{7,4},{8,9},{9,10},{10,1... | collective-permute-start | bytes 1327112 | tf_op jit(solution)/shard_map/ppermute | solution.py:1231
  68.3 28.3 %collective-permute-start.10 = (bf16[288,768]{1,0:T(8,128)(2,1)}, bf16[288,768]{1,0:T(8,128)(2,1)S(1)}, u32[]{:S(2)}, u32[]{:S(2)}) collective-permute-start(bf16[288,768]{1,0:T(8,128)(2,1)} %collective-permute-done.6.x1), channel_id=1, source_target_pairs={{0,8},{4,12},{8,0},{12,4},{16,24},{20,28},{24,16},{28,20},{1,9},{5... | collective-permute-start | bytes 1327112 | tf_op jit(solution)/shard_map/ppermute | solution.py:1226
  70.5 24.5 %all-to-all-start.1 = ((bf16[8,1,192,128]{3,2,1,0:T(8,128)(2,1)}), bf16[8,1,192,128]{3,2,1,0:T(8,128)(2,1)S(1)}, u32[]{:S(2)}, u32[]{:S(2)}) async-start(bf16[8,1,192,128]{3,2,1,0:T(8,128)(2,1)} %get-tuple-element.134), calls=%async_computation.1 | async-start | bytes 786432 | tf_op jit(solution)/shard_map/all_to_all | solution.py:1312
  74.8 21.7 %collective-permute-start.15 = (bf16[288,768]{1,0:T(8,128)(2,1)}, bf16[288,768]{1,0:T(8,128)(2,1)S(1)}, u32[]{:S(2)}, u32[]{:S(2)}) collective-permute-start(bf16[288,768]{1,0:T(8,128)(2,1)} %collective-permute-done.7.y1), channel_id=1, source_target_pairs={{0,1},{1,2},{2,3},{3,0},{4,5},{5,6},{6,7},{7,4},{8,9},{9,10},{10,1... | collective-permute-start | bytes 1327112 | tf_op jit(solution)/shard_map/ppermute | solution.py:1231
  93.5 13.9 %collective-permute-start.14 = (bf16[288,768]{1,0:T(8,128)(2,1)}, bf16[288,768]{1,0:T(8,128)(2,1)S(1)}, u32[]{:S(2)}, u32[]{:S(2)}) collective-permute-start(bf16[288,768]{1,0:T(8,128)(2,1)} %collective-permute-done.7.y1), channel_id=1, source_target_pairs={{0,16},{4,20},{8,24},{12,28},{16,0},{20,4},{24,8},{28,12},{1,17},{... | collective-permute-start | bytes 1327112 | tf_op jit(solution)/shard_map/ppermute | solution.py:1226
  94.9 27.5 %copy-start.12 = (bf16[8,1,192,128]{3,2,1,0:T(8,128)(2,1)}, bf16[8,1,192,128]{3,2,1,0:T(8,128)(2,1)S(1)}, u32[]{:S(2)}) copy-start(bf16[8,1,192,128]{3,2,1,0:T(8,128)(2,1)S(1)} %all-to-all-done.1.attn0_ref) | copy-start | bytes 1179652
  94.9 26.7 %collective-permute-start.13 = (bf16[288,768]{1,0:T(8,128)(2,1)}, bf16[288,768]{1,0:T(8,128)(2,1)S(1)}, u32[]{:S(2)}, u32[]{:S(2)}) collective-permute-start(bf16[288,768]{1,0:T(8,128)(2,1)} %collective-permute-done.8.x3), channel_id=1, source_target_pairs={{0,8},{4,12},{8,0},{12,4},{16,24},{20,28},{24,16},{28,20},{1,9},{5... | collective-permute-start | bytes 1327112 | tf_op jit(solution)/shard_map/ppermute | solution.py:1226
  96.2 31.4 %copy-start.29 = (bf16[288,768]{1,0:T(8,128)(2,1)}, bf16[288,768]{1,0:T(8,128)(2,1)S(1)}, u32[]{:S(2)}) copy-start(bf16[288,768]{1,0:T(8,128)(2,1)S(1)} %collective-permute-done.11.x2) | copy-start | bytes 1327108
  96.2 25.4 %collective-permute-start.17 = (bf16[288,768]{1,0:T(8,128)(2,1)}, bf16[288,768]{1,0:T(8,128)(2,1)}, u32[]{:S(2)}, u32[]{:S(2)}) collective-permute-start(bf16[288,768]{1,0:T(8,128)(2,1)} %collective-permute-done.9.y3), channel_id=1, source_target_pairs={{0,16},{4,20},{8,24},{12,28},{16,0},{20,4},{24,8},{28,12},{1,17},{... | collective-permute-start | bytes 1327112 | tf_op jit(solution)/shard_map/ppermute | solution.py:1226
  96.5 25.2 %copy-start.31 = (bf16[288,768]{1,0:T(8,128)(2,1)}, bf16[288,768]{1,0:T(8,128)(2,1)S(1)}, u32[]{:S(2)}) copy-start(bf16[288,768]{1,0:T(8,128)(2,1)S(1)} %collective-permute-done.15.y2) | copy-start | bytes 1327108
  96.5 25.1 %collective-permute-start.12 = (bf16[288,768]{1,0:T(8,128)(2,1)S(1)}, bf16[288,768]{1,0:T(8,128)(2,1)}, u32[]{:S(2)}, u32[]{:S(2)}) collective-permute-start(bf16[288,768]{1,0:T(8,128)(2,1)S(1)} %collective-permute-done.11.x2), channel_id=1, source_target_pairs={{0,8},{4,12},{8,0},{12,4},{16,24},{20,28},{24,16},{28,20},{1,9},{5... | collective-permute-start | bytes 1327112 | tf_op jit(solution)/shard_map/ppermute | solution.py:1226
  96.6 31.0 %copy-start.30 = (bf16[288,768]{1,0:T(8,128)(2,1)}, bf16[288,768]{1,0:T(8,128)(2,1)S(1)}, u32[]{:S(2)}) copy-start(bf16[288,768]{1,0:T(8,128)(2,1)S(1)} %collective-permute-done.10.sx1) | copy-start | bytes 1327108
  96.6 25.0 %collective-permute-start.16 = (bf16[288,768]{1,0:T(8,128)(2,1)S(1)}, bf16[288,768]{1,0:T(8,128)(2,1)}, u32[]{:S(2)}, u32[]{:S(2)}) collective-permute-start(bf16[288,768]{1,0:T(8,128)(2,1)S(1)} %collective-permute-done.15.y2), channel_id=1, source_target_pairs={{0,16},{4,20},{8,24},{12,28},{16,0},{20,4},{24,8},{28,12},{1,17},{... | collective-permute-start | bytes 1327112 | tf_op jit(solution)/shard_map/ppermute | solution.py:1226
  98.0 23.6 %all-to-all-start.2 = ((bf16[8,1,192,128]{3,2,1,0:T(8,128)(2,1)}), bf16[8,1,192,128]{3,2,1,0:T(8,128)(2,1)S(1)}, u32[]{:S(2)}, u32[]{:S(2)}) async-start(bf16[8,1,192,128]{3,2,1,0:T(8,128)(2,1)} %get-tuple-element.138), calls=%async_computation.2 | async-start | bytes 786432 | tf_op jit(solution)/shard_map/all_to_all | solution.py:1316
  127.6 2.4 collective-permute-start.19
  127.8 3.5 collective-permute-start.18
  157.9 13.4 %collective-permute-start.23 = (bf16[512,768]{1,0:T(8,128)(2,1)}, bf16[512,768]{1,0:T(8,128)(2,1)S(1)}, u32[]{:S(2)}, u32[]{:S(2)}) collective-permute-start(bf16[512,768]{1,0:T(8,128)(2,1)} %get-tuple-element.158), channel_id=1, source_target_pairs={{0,4},{4,0},{8,12},{12,8},{16,20},{20,16},{24,28},{28,24},{1,5},{5... | collective-permute-start | bytes 2359304 | tf_op jit(solution)/shard_map/ppermute | solution.py:1226
  158.1 41.9 %collective-permute-start.21 = (bf16[2,192,768]{2,1,0:T(8,128)(2,1)}, bf16[2,192,768]{2,1,0:T(8,128)(2,1)S(1)}, u32[]{:S(2)}, u32[]{:S(2)}) collective-permute-start(bf16[2,192,768]{2,1,0:T(8,128)(2,1)} %get-tuple-element.153), channel_id=1, source_target_pairs={{0,1},{1,2},{2,3},{3,0},{4,5},{5,6},{6,7},{7,4},{8,9},{9,10},{10,1... | collective-permute-start | bytes 1769480 | tf_op jit(solution)/shard_map/ppermute | solution.py:1231
  158.9 41.1 %collective-permute-start.22 = (bf16[2,192,768]{2,1,0:T(8,128)(2,1)}, bf16[2,192,768]{2,1,0:T(8,128)(2,1)S(1)}, u32[]{:S(2)}, u32[]{:S(2)}) collective-permute-start(bf16[2,192,768]{2,1,0:T(8,128)(2,1)} %get-tuple-element.154), channel_id=1, source_target_pairs={{0,3},{1,0},{2,1},{3,2},{4,7},{5,4},{6,5},{7,6},{8,11},{9,8},{10,9... | collective-permute-start | bytes 1769480 | tf_op jit(solution)/shard_map/ppermute | solution.py:1231
  170.5 70.3 %collective-permute-start.26 = (bf16[2,192,768]{2,1,0:T(8,128)(2,1)}, bf16[2,192,768]{2,1,0:T(8,128)(2,1)}, u32[]{:S(2)}, u32[]{:S(2)}) collective-permute-start(bf16[2,192,768]{2,1,0:T(8,128)(2,1)} %get-tuple-element.173), channel_id=1, source_target_pairs={{0,2},{1,3},{2,0},{3,1},{4,6},{5,7},{6,4},{7,5},{8,10},{9,11},{10,... | collective-permute-start | bytes 1769480 | tf_op jit(solution)/shard_map/ppermute | solution.py:1231
  178.7 21.4 %all-to-all-start.3 = ((bf16[8,2,192,128]{3,2,1,0:T(8,128)(2,1)}), bf16[8,2,192,128]{3,2,1,0:T(8,128)(2,1)S(1)}, u32[]{:S(2)}, u32[]{:S(2)}) async-start(bf16[8,2,192,128]{3,2,1,0:T(8,128)(2,1)} %get-tuple-element.160), calls=%async_computation.3 | async-start | bytes 1572864 | tf_op jit(solution)/shard_map/all_to_all | solution.py:1335
  183.5 15.9 %copy-start.22 = (f32[1,768]{1,0:T(1,128)S(1)}, f32[1,768]{1,0:T(1,128)}, u32[]{:S(2)}) copy-start(f32[1,768]{1,0:T(1,128)} %get-tuple-element.187) | copy-start | bytes 9220
  199.2 41.5 %collective-permute-start.31 = (bf16[4,96,768]{2,1,0:T(8,128)(2,1)}, bf16[4,96,768]{2,1,0:T(8,128)(2,1)}, u32[]{:S(2)}, u32[]{:S(2)}) collective-permute-start(bf16[4,96,768]{2,1,0:T(8,128)(2,1)} %get-tuple-element.194), channel_id=1, source_target_pairs={{0,4},{4,0},{8,12},{12,8},{16,20},{20,16},{24,28},{28,24},{1,5},{5... | collective-permute-start | bytes 1769480 | tf_op jit(solution)/shard_map/ppermute | solution.py:1226
  200.0 38.9 %copy-start.9 = (bf16[2,192,768]{2,1,0:T(8,128)(2,1)}, bf16[2,192,768]{2,1,0:T(8,128)(2,1)S(1)}, u32[]{:S(2)}) copy-start(bf16[2,192,768]{2,1,0:T(8,128)(2,1)S(1)} %collective-permute-done.21.refs_1_) | copy-start | bytes 1769476
  200.0 38.9 %copy-start.10 = (bf16[2,192,768]{2,1,0:T(8,128)(2,1)}, bf16[2,192,768]{2,1,0:T(8,128)(2,1)S(1)}, u32[]{:S(2)}) copy-start(bf16[2,192,768]{2,1,0:T(8,128)(2,1)S(1)} %collective-permute-done.22.refs_3_) | copy-start | bytes 1769476
  200.1 40.7 %collective-permute-start.24 = (bf16[4,2,96,768]{3,2,1,0:T(8,128)(2,1)}, bf16[4,2,96,768]{3,2,1,0:T(8,128)(2,1)}, u32[]{:S(2)}, u32[]{:S(2)}) collective-permute-start(bf16[4,2,96,768]{3,2,1,0:T(8,128)(2,1)} %get-tuple-element.161), channel_id=1, source_target_pairs={{0,8},{4,12},{8,0},{12,4},{16,24},{20,28},{24,16},{28,20},{1,9},{5... | collective-permute-start | bytes 3538952 | tf_op jit(solution)/shard_map/ppermute | solution.py:1226
  201.9 38.9 %collective-permute-start.25 = (bf16[4,192,768]{2,1,0:T(8,128)(2,1)}, bf16[4,192,768]{2,1,0:T(8,128)(2,1)}, u32[]{:S(2)}, u32[]{:S(2)}) collective-permute-start(bf16[4,192,768]{2,1,0:T(8,128)(2,1)} %get-tuple-element.162), channel_id=1, source_target_pairs={{0,16},{4,20},{8,24},{12,28},{16,0},{20,4},{24,8},{28,12},{1,17},{... | collective-permute-start | bytes 3538952 | tf_op jit(solution)/shard_map/ppermute | solution.py:1226
  203.0 35.9 %copy-start.3 = (pred[2047,32]{1,0:T(8,128)(4,1)S(1)}, pred[2047,32]{1,0:T(8,128)(4,1)}, u32[]{:S(2)}) copy-start(pred[2047,32]{1,0:T(8,128)(4,1)} %copy-done.2) | copy-start | bytes 196516
  244.0 9.6 %collective-permute-start.32 = (bf16[192,768]{1,0:T(8,128)(2,1)}, bf16[192,768]{1,0:T(8,128)(2,1)S(1)}, u32[]{:S(2)}, u32[]{:S(2)}) collective-permute-start(bf16[192,768]{1,0:T(8,128)(2,1)} %get-tuple-element.196), channel_id=1, source_target_pairs={{0,8},{4,12},{8,0},{12,4},{16,24},{20,28},{24,16},{28,20},{1,9},{5... | collective-permute-start | bytes 884744 | tf_op jit(solution)/shard_map/ppermute | solution.py:1226
  248.7 21.6 %collective-permute-start.27 = (bf16[4,2,48,768]{3,2,1,0:T(8,128)(2,1)}, bf16[4,2,48,768]{3,2,1,0:T(8,128)(2,1)S(1)}, u32[]{:S(2)}, u32[]{:S(2)}) collective-permute-start(bf16[4,2,48,768]{3,2,1,0:T(8,128)(2,1)} %get-tuple-element.181), channel_id=1, source_target_pairs={{0,16},{4,20},{8,24},{12,28},{16,0},{20,4},{24,8},{28,12},{1,17},{... | collective-permute-start | bytes 1769480 | tf_op jit(solution)/shard_map/ppermute | solution.py:1226
  249.3 21.0 %collective-permute-start.28 = (bf16[4,96,768]{2,1,0:T(8,128)(2,1)}, bf16[4,96,768]{2,1,0:T(8,128)(2,1)S(1)}, u32[]{:S(2)}, u32[]{:S(2)}) collective-permute-start(bf16[4,96,768]{2,1,0:T(8,128)(2,1)} %get-tuple-element.183), channel_id=1, source_target_pairs={{0,8},{4,12},{8,0},{12,4},{16,24},{20,28},{24,16},{28,20},{1,9},{5... | collective-permute-start | bytes 1769480 | tf_op jit(solution)/shard_map/ppermute | solution.py:1226
  250.2 20.1 %collective-permute-start.29 = (bf16[4,96,768]{2,1,0:T(8,128)(2,1)S(1)}, bf16[4,96,768]{2,1,0:T(8,128)(2,1)S(1)}, u32[]{:S(2)}, u32[]{:S(2)}) collective-permute-start(bf16[4,96,768]{2,1,0:T(8,128)(2,1)S(1)} %copy-done.28), channel_id=1, source_target_pairs={{0,4},{4,0},{8,12},{12,8},{16,20},{20,16},{24,28},{28,24},{1,5},{5... | collective-permute-start | bytes 1769480 | tf_op jit(solution)/shard_map/ppermute | solution.py:1226
  251.1 1.4 collective-permute-start.30
  252.5 17.9 %copy-start.18 = (bf16[4,16,768]{2,1,0:T(8,128)(2,1)}, bf16[4,16,768]{2,1,0:T(8,128)(2,1)S(1)}, u32[]{:S(2)}) copy-start(bf16[4,16,768]{2,1,0:T(8,128)(2,1)S(1)} %collective-permute-done.30.refs_7_) | copy-start | bytes 294916
  252.5 17.8 %collective-permute-start.33 = (bf16[192,768]{1,0:T(8,128)(2,1)S(1)}, bf16[192,768]{1,0:T(8,128)(2,1)S(1)}, u32[]{:S(2)}, u32[]{:S(2)}) collective-permute-start(bf16[192,768]{1,0:T(8,128)(2,1)S(1)} %copy-done.35), channel_id=1, source_target_pairs={{0,16},{4,20},{8,24},{12,28},{16,0},{20,4},{24,8},{28,12},{1,17},{... | collective-permute-start | bytes 884744 | tf_op jit(solution)/shard_map/ppermute | solution.py:1226
  253.5 16.8 %copy-start.14 = (bf16[192,768]{1,0:T(8,128)(2,1)}, bf16[192,768]{1,0:T(8,128)(2,1)S(1)}, u32[]{:S(2)}) copy-start(bf16[192,768]{1,0:T(8,128)(2,1)S(1)} %collective-permute-done.32.refs_9_) | copy-start | bytes 884740
  253.6 16.8 %collective-permute-start.34 = (bf16[192,768]{1,0:T(8,128)(2,1)S(1)}, bf16[192,768]{1,0:T(8,128)(2,1)S(1)}, u32[]{:S(2)}, u32[]{:S(2)}) collective-permute-start(bf16[192,768]{1,0:T(8,128)(2,1)S(1)} %copy-done.34), channel_id=1, source_target_pairs={{0,24},{4,28},{8,16},{12,20},{16,8},{20,12},{24,0},{28,4},{1,25},{... | collective-permute-start | bytes 884744 | tf_op jit(solution)/shard_map/ppermute | solution.py:1226
  275.6 78.4 %all-to-all-start.4 = ((bf16[8,2,128,768]{3,2,1,0:T(8,128)(2,1)}), bf16[8,2,128,768]{3,2,1,0:T(8,128)(2,1)S(1)}, u32[]{:S(2)}, u32[]{:S(2)}) async-start(bf16[8,2,128,768]{3,2,1,0:T(8,128)(2,1)} %get-tuple-element.203), calls=%async_computation.4 | async-start | bytes 6291456 | tf_op jit(solution)/shard_map/all_to_all | solution.py:1381
  279.2 2.6 collective-permute-start.20
  279.3 12.1 %collective-permute-start.35 = (bf16[304,768]{1,0:T(8,128)(2,1)}, bf16[304,768]{1,0:T(8,128)(2,1)S(1)}, u32[]{:S(2)}, u32[]{:S(2)}) collective-permute-start(bf16[304,768]{1,0:T(8,128)(2,1)} %get-tuple-element.207), channel_id=1, source_target_pairs={{0,1},{1,2},{2,3},{3,0},{4,5},{5,6},{6,7},{7,4},{8,9},{9,10},{10,1... | collective-permute-start | bytes 1400840 | tf_op jit(solution)/shard_map/ppermute | solution.py:1231
  279.4 40.3 %collective-permute-start.36 = (bf16[304,768]{1,0:T(8,128)(2,1)}, bf16[304,768]{1,0:T(8,128)(2,1)S(1)}, u32[]{:S(2)}, u32[]{:S(2)}) collective-permute-start(bf16[304,768]{1,0:T(8,128)(2,1)} %get-tuple-element.208), channel_id=1, source_target_pairs={{0,2},{1,3},{2,0},{3,1},{4,6},{5,7},{6,4},{7,5},{8,10},{9,11},{10,... | collective-permute-start | bytes 1400840 | tf_op jit(solution)/shard_map/ppermute | solution.py:1231
  280.2 41.4 %collective-permute-start.37 = (bf16[304,768]{1,0:T(8,128)(2,1)}, bf16[304,768]{1,0:T(8,128)(2,1)S(1)}, u32[]{:S(2)}, u32[]{:S(2)}) collective-permute-start(bf16[304,768]{1,0:T(8,128)(2,1)} %get-tuple-element.209), channel_id=1, source_target_pairs={{0,3},{1,0},{2,1},{3,2},{4,7},{5,4},{6,5},{7,6},{8,11},{9,8},{10,9... | collective-permute-start | bytes 1400840 | tf_op jit(solution)/shard_map/ppermute | solution.py:1231
  282.7 38.9 %copy-start.11 = (bf16[304,768]{1,0:T(8,128)(2,1)S(1)}, bf16[304,768]{1,0:T(8,128)(2,1)}, u32[]{:S(2)}) copy-start(bf16[304,768]{1,0:T(8,128)(2,1)} %get-tuple-element.206) | copy-start | bytes 1400836
  287.4 34.4 %copy-start.17 = (bf16[96,768]{1,0:T(8,128)(2,1)S(1)}, bf16[96,768]{1,0:T(8,128)(2,1)}, u32[]{:S(2)}) copy-start(bf16[96,768]{1,0:T(8,128)(2,1)} %get-tuple-element.205) | copy-start | bytes 442372
  322.8 16.8 %collective-permute-start.40 = (bf16[400,768]{1,0:T(8,128)(2,1)}, bf16[400,768]{1,0:T(8,128)(2,1)}, u32[]{:S(2)}, u32[]{:S(2)}) collective-permute-start(bf16[400,768]{1,0:T(8,128)(2,1)} %pad_maximum_fusion.refs_0_), channel_id=1, source_target_pairs={{0,24},{4,28},{8,16},{12,20},{16,8},{20,12},{24,0},{28,4},{1,25},{... | collective-permute-start | bytes 1843208 | tf_op jit(solution)/shard_map/ppermute | solution.py:1226
  325.4 27.3 %collective-permute-start.38 = (bf16[400,768]{1,0:T(8,128)(2,1)}, bf16[400,768]{1,0:T(8,128)(2,1)}, u32[]{:S(2)}, u32[]{:S(2)}) collective-permute-start(bf16[400,768]{1,0:T(8,128)(2,1)} %pad_maximum_fusion.refs_0_), channel_id=1, source_target_pairs={{0,8},{4,12},{8,0},{12,4},{16,24},{20,28},{24,16},{28,20},{1,9},{5... | collective-permute-start | bytes 1843208 | tf_op jit(solution)/shard_map/ppermute | solution.py:1226
  325.7 28.3 %collective-permute-start.39 = (bf16[400,768]{1,0:T(8,128)(2,1)}, bf16[400,768]{1,0:T(8,128)(2,1)}, u32[]{:S(2)}, u32[]{:S(2)}) collective-permute-start(bf16[400,768]{1,0:T(8,128)(2,1)} %pad_maximum_fusion.refs_0_), channel_id=1, source_target_pairs={{0,16},{4,20},{8,24},{12,28},{16,0},{20,4},{24,8},{28,12},{1,17},{... | collective-permute-start | bytes 1843208 | tf_op jit(solution)/shard_map/ppermute | solution.py:1226
  339.6 21.5 %collective-permute-start.44 = (bf16[400,768]{1,0:T(8,128)(2,1)}, bf16[400,768]{1,0:T(8,128)(2,1)}, u32[]{:S(2)}, u32[]{:S(2)}) collective-permute-start(bf16[400,768]{1,0:T(8,128)(2,1)} %collective-permute-done.40.refs_3_), channel_id=1, source_target_pairs={{0,4},{4,0},{8,12},{12,8},{16,20},{20,16},{24,28},{28,24},{1,5},{5... | collective-permute-start | bytes 1843208 | tf_op jit(solution)/shard_map/ppermute | solution.py:1226
  341.2 19.9 %collective-permute-start.41 = (bf16[400,768]{1,0:T(8,128)(2,1)}, bf16[400,768]{1,0:T(8,128)(2,1)}, u32[]{:S(2)}, u32[]{:S(2)}) collective-permute-start(bf16[400,768]{1,0:T(8,128)(2,1)} %pad_maximum_fusion.refs_0_), channel_id=1, source_target_pairs={{0,4},{4,0},{8,12},{12,8},{16,20},{20,16},{24,28},{28,24},{1,5},{5... | collective-permute-start | bytes 1843208 | tf_op jit(solution)/shard_map/ppermute | solution.py:1226
  352.7 8.4 %collective-permute-start.42 = (bf16[400,768]{1,0:T(8,128)(2,1)}, bf16[400,768]{1,0:T(8,128)(2,1)}, u32[]{:S(2)}, u32[]{:S(2)}) collective-permute-start(bf16[400,768]{1,0:T(8,128)(2,1)} %collective-permute-done.38.refs_1_), channel_id=1, source_target_pairs={{0,4},{4,0},{8,12},{12,8},{16,20},{20,16},{24,28},{28,24},{1,5},{5... | collective-permute-start | bytes 1843208 | tf_op jit(solution)/shard_map/ppermute | solution.py:1226
  354.1 7.1 %collective-permute-start.43 = (bf16[400,768]{1,0:T(8,128)(2,1)}, bf16[400,768]{1,0:T(8,128)(2,1)}, u32[]{:S(2)}, u32[]{:S(2)}) collective-permute-start(bf16[400,768]{1,0:T(8,128)(2,1)} %collective-permute-done.39.refs_2_), channel_id=1, source_target_pairs={{0,4},{4,0},{8,12},{12,8},{16,20},{20,16},{24,28},{28,24},{1,5},{5... | collective-permute-start | bytes 1843208 | tf_op jit(solution)/shard_map/ppermute | solution.py:1226
  (22 other events, 71.9 us)

commit v3 on v2

--- a/solution.py
+++ b/solution.py
@@ -13,7 +13,7 @@
 BLOCK = 256
 TILE = 256
 VMEM_BYTES = 56 * 1024 * 1024
-COST = 4
+COST = 12
 
 norm_eps = 1e-06
 F32 = jnp.float32

time: 375 us -> 375 us (level)
  Pallas kernels: 157 us -> 149 us
  starting transfers between devices: 75.3 us -> 80.9 us
    pallas_call x1, Pallas kernels: 35.9 us -> 30.7 us  [attn_backward(): pl.pallas_call(attn_backward_kernel, grid=(slots,), in_specs=[SMEM, SMEM,...]
    unnamed x72 -> x66, local copies, waits for them, and re-layouts: 8.82 us -> 8.63 us
  transfers between devices with their start and end apart: 50 -> 50, of which waited for: 16 -> 16; matrix products, arithmetic and copies ran while one was open for 3% -> 3% of each run, Pallas kernels for 28% -> 26%
where the time goes in v3:
time: 375 us; the launch traced here: 369 us
  Pallas kernels  149 us (40%)
  waiting for transfers between devices  114 us (30%)
  starting transfers between devices  80.9 us (22%)
  local copies, waits for them, and re-layouts  17.6 us (5%)
  other arithmetic  3.77 us (1%)
    ppermute x15, waiting for transfers between devices, shift(): lax.ppermute(values, 'fsdp', [(i, (i + places) % count) for i in range(co...  53.2 us
    ppermute x30, waiting for transfers between devices, swap(): return lax.ppermute(values, 'ctx', [(i, i ^ bits) for i in range(count)])  45.6 us
    pallas_call x1, Pallas kernels, attn_backward(): pl.pallas_call(attn_backward_kernel, grid=(slots,), in_specs=[SMEM, SMEM,...  30.7 us
    ppermute x15, starting transfers between devices, shift(): lax.ppermute(values, 'fsdp', [(i, (i + places) % count) for i in range(co...  30.2 us
    ppermute x30, starting transfers between devices, swap(): return lax.ppermute(values, 'ctx', [(i, i ^ bits) for i in range(count)])  27 us
    pallas_call x1, Pallas kernels, ffn_first(): pl.pallas_call(ffn_first_kernel, grid=(units // tile,), in_specs=[SMEM, w...  25.7 us
    pallas_call x2, Pallas kernels, attn_forward(): pl.pallas_call(attn_forward_first_kernel if slot == 0 else attn_forward_s...  25.2 us
    pallas_call x1, Pallas kernels, ffn_second(): pl.pallas_call(ffn_second_kernel, grid=(units // tile,), in_specs=[SMEM,...  15.8 us
  transfers between devices with their start and end apart: 50, of which 16 were waited for; matrix products, arithmetic and copies ran while one was open for 3% of the time, Pallas kernels for 26%

profile of v3, /device:TPU:9, one launch (start us, length us, event | category | flops | bytes accessed | tf_op | source)
XLA Modules:
  0.0 369.2 jit_solution(1452807162458884034)
XLA Ops:
  3.4 4.1 %pack_weights.1 = (bf16[2,192,768]{2,1,0:T(8,128)(2,1)}, bf16[2,192,768]{2,1,0:T(8,128)(2,1)}, bf16[288,768]{1,0:T(8,128)(2,1)}, bf16[288,768]{1,0:T(8,128)(2,1)...) custom-call(s32[3]{0:T(128)} %pad_add_fusion.where_ref, bf16[192,3072]{1,0:T(8,128)(2,1)} %gate_ref.1, ...), custom_call_target="tpu_custom_call" | custom-call | bytes 192000000 | tf_op jit(solution)/shard_map/pack_weights/pallas_call | solution.py:102
  7.5 3.0 prepare.1
  10.5 4.4 %all-to-all-start = ((bf16[8,2,128,768]{3,2,1,0:T(8,128)(2,1)}), bf16[8,2,128,768]{3,2,1,0:T(8,128)(2,1)S(1)}, u32[]{:S(2)}, u32[]{:S(2)}) async-start(bf16[8,2,128,768]{3,2,1,0:T(8,128)(2,1)} %bitcast.12), calls=%async_computation | async-start | bytes 6291456 | tf_op jit(solution)/shard_map/all_to_all | solution.py:1283
  15.0 1.3 collective-permute-start
  17.2 7.3 %collective-permute-done.w1_ref.a1_ref = bf16[208,768]{1,0:T(8,128)(2,1)} collective-permute-done((bf16[208,768]{1,0:T(8,128)(2,1)}, bf16[208,768]{1,0:T(8,128)(2,1)}, u32[]{:S(2)}, u32[]{:S(2)}) %collective-permute-start) | collective-permute-done | bytes 319520 | tf_op jit(solution)/shard_map/ppermute | solution.py:1231
  24.4 1.4 collective-permute-start.1
  26.2 6.4 %collective-permute-done.2.w3_ref.a3_ref = bf16[208,768]{1,0:T(8,128)(2,1)} collective-permute-done((bf16[208,768]{1,0:T(8,128)(2,1)}, bf16[208,768]{1,0:T(8,128)(2,1)}, u32[]{:S(2)}, u32[]{:S(2)}) %collective-permute-start.2) | collective-permute-done | bytes 319520 | tf_op jit(solution)/shard_map/ppermute | solution.py:1231
  32.7 1.5 collective-permute-start.8
  35.5 1.6 collective-permute-start.3
  38.9 3.6 collective-permute-start.4
  43.1 1.0 fusion.off_ref
  44.1 2.1 collective-permute-start.7
  46.9 2.5 all-to-all-done.tok_ref
  49.4 1.6 copy-done.1
  51.0 14.6 %attn_forward.2 = (bf16[8,1,192,128]{3,2,1,0:T(8,128)(2,1)}, f32[2,1024,256]{2,1,0:T(8,128)}, bf16[2,1024,192]{2,1,0:T(8,128)(2,1)}, bf16[2,1024,192]{2,1,0:T(8,...) custom-call(s32[4]{0:T(128)} %get-tuple-element.119.lens_ref, s32[3]{0:T(128)} %pad_add_fusion.where_ref, ...), custom_call_target="tpu_custom_call" | custom-call | flops 49526341632 | bytes 56623104 | tf_op jit(solution)/shard_map/attn_forward/pallas_call | solution.py:358
  65.7 1.0 collective-permute-done.7.y1
  66.7 1.6 collective-permute-start.11
  68.3 1.0 collective-permute-start.10
  69.3 5.5 %all-to-all-start.1 = ((bf16[8,1,192,128]{3,2,1,0:T(8,128)(2,1)}), bf16[8,1,192,128]{3,2,1,0:T(8,128)(2,1)S(1)}, u32[]{:S(2)}, u32[]{:S(2)}) async-start(bf16[8,1,192,128]{3,2,1,0:T(8,128)(2,1)} %get-tuple-element.134), calls=%async_computation.1 | async-start | bytes 786432 | tf_op jit(solution)/shard_map/all_to_all | solution.py:1312
  74.8 3.4 collective-permute-start.15
  78.2 10.6 %attn_forward.3 = (bf16[8,1,192,128]{3,2,1,0:T(8,128)(2,1)}, f32[2,1024,256]{2,1,0:T(8,128)}, bf16[2,1024,192]{2,1,0:T(8,128)(2,1)}, bf16[2,1024,192]{2,1,0:T(8,128)(2,1)}, bf16[2,1024,192]{2,1,0:T(8,128)(2,1)}) custom-call(s32[4]{0:T(128)} %get-tuple-element.119.lens_ref, ...), custom_call_target="tpu_custom_call", output_to_operand_aliasing={{1}: (6, {}), {2}: (7, {}), {3}: (8, {}), {4}: (9, {})} | custom-call | flops 49526341632 | bytes 56623104 | tf_op jit(solution)/shard_map/attn_forward/pallas_call | solution.py:358
  88.8 1.4 collective-permute-start.14
  90.2 1.3 collective-permute-start.13
  91.7 3.5 collective-permute-done.15.y2
  95.2 1.0 collective-permute-start.12
  96.2 1.2 collective-permute-start.16
  97.4 5.0 %all-to-all-start.2 = ((bf16[8,1,192,128]{3,2,1,0:T(8,128)(2,1)}), bf16[8,1,192,128]{3,2,1,0:T(8,128)(2,1)S(1)}, u32[]{:S(2)}, u32[]{:S(2)}) async-start(bf16[8,1,192,128]{3,2,1,0:T(8,128)(2,1)} %get-tuple-element.138), calls=%async_computation.2 | async-start | bytes 786432 | tf_op jit(solution)/shard_map/all_to_all | solution.py:1316
  102.4 4.3 %sort_rows.1 = (bf16[512,768]{1,0:T(8,128)(2,1)}, bf16[512,768]{1,0:T(8,128)(2,1)}) custom-call(s32[4]{0:T(128)} %get-tuple-element.118.order_ref, s32[4]{0:T(128)} %get-tuple-element.119.lens_ref, s32[1]{0:T(128)} %bitcast.3.start_ref, bf16[4,128,768]{2,1,0:T(8,128)(2,1)} %tok_ref.2, bf16[4,128,768]{2,1,0:T(8,128)(2,1)} %cot_ref.1), custom_call_target="tpu_custom_call" | custom-call | bytes 36000000 | tf_op jit(solution)/shard_map/sort_rows/pallas_call | solution.py:168
  107.4 13.0 %all-to-all-done.2.attn1_ref = bf16[8,1,192,128]{3,2,1,0:T(8,128)(2,1)S(1)} async-done(((bf16[8,1,192,128]{3,2,1,0:T(8,128)(2,1)}), bf16[8,1,192,128]{3,2,1,0:T(8,128)(2,1)S(1)}, u32[]{:S(2)}, u32[]{:S(2)}) %all-to-all-start.2) | async-done | bytes 393248 | tf_op jit(solution)/shard_map/all_to_all | solution.py:1316
  121.1 5.1 %out_project.1 = (f32[512,768]{1,0:T(8,128)}, bf16[512,768]{1,0:T(8,128)(2,1)}, bf16[768,768]{1,0:T(8,128)(2,1)}) custom-call(s32[3]{0:T(128)} %pad_add_fusion.where_ref, bf16[512,768]{1,0:T(8,128)(2,1)} %get-tuple-element.120.tok_ref, bf16[8,1,192,128]{3,2,1,0:T(8,128)(2,1)} %copy-done.9, bf16[8,1,192,128]{3,2,1,0:T(8,128)(2,1)} %copy-done.10, ...), custom_call_target="tpu_custom_call" | custom-call | flops 14495514624 | bytes 56623104 | tf_op jit(solution)/shard_map/out_project/pallas_call | solution.py:608
  126.8 1.8 collective-permute-done.19.dy_other_ref
  128.6 1.3 collective-permute-done.18.nf_other_ref
  130.8 25.7 %ffn_first.1 = (bf16[1024,1536]{1,0:T(8,128)(2,1)}, bf16[1024,1536]{1,0:T(8,128)(2,1)}, f32[512,768]{1,0:T(8,128)}, bf16[512,768]{1,0:T(8,128)(2,1)}, bf16[1536,...) custom-call(s32[3]{0:T(128)} %pad_add_fusion.where_ref, ...), custom_call_target="tpu_custom_call" | custom-call | flops 347892350976 | bytes 292552704 | tf_op jit(solution)/shard_map/ffn_first/pallas_call | solution.py:814
  156.8 2.0 collective-permute-start.21
  158.8 10.9 %collective-permute-start.22 = (bf16[2,192,768]{2,1,0:T(8,128)(2,1)}, bf16[2,192,768]{2,1,0:T(8,128)(2,1)}, u32[]{:S(2)}, u32[]{:S(2)}) collective-permute-start(bf16[2,192,768]{2,1,0:T(8,128)(2,1)} %get-tuple-element.154), channel_id=1, source_target_pairs={{0,3},{1,0},{2,1},{3,2},{4,7},{5,4},{6,5},{7,6},{8,11},{9,8},{10,9... | collective-permute-start | bytes 1769480 | tf_op jit(solution)/shard_map/ppermute | solution.py:1231
  169.7 1.4 collective-permute-start.26
  172.0 6.6 %out_back.1 = (bf16[8,2,192,128]{3,2,1,0:T(8,128)(2,1)}, f32[512,768]{1,0:T(8,128)}, f32[1,768]{1,0:T(1,128)}, bf16[4,96,768]{2,1,0:T(8,128)(2,1)}, bf16[4,96,768]{2,1,0:T(8,128)(2,1)}) custom-call(s32[3]{0:T(128)} %pad_add_fusion.where_ref, f32[512,768]{1,0:T(8,128)} %get-tuple-element.157.own_ref, bf16[512,768]{1,0:T(8,128)(2,1)} %copy-done.24, ...), custom_call_target="tpu_custom_call" | custom-call | flops 28991029248 | bytes 94371840 | tf_op jit(solution)/shard_map/out_back/pallas_call | solution.py:657
  178.6 4.8 %all-to-all-start.3 = ((bf16[8,2,192,128]{3,2,1,0:T(8,128)(2,1)}), bf16[8,2,192,128]{3,2,1,0:T(8,128)(2,1)}, u32[]{:S(2)}, u32[]{:S(2)}) async-start(bf16[8,2,192,128]{3,2,1,0:T(8,128)(2,1)} %get-tuple-element.160), calls=%async_computation.3 | async-start | bytes 1572864 | tf_op jit(solution)/shard_map/all_to_all | solution.py:1335
  183.4 15.8 %ffn_second.1 = (f32[512,768]{1,0:T(8,128)}, bf16[512,768]{1,0:T(8,128)(2,1)}, bf16[4,2,96,768]{3,2,1,0:T(8,128)(2,1)}, bf16[4,2,96,768]{3,2,1,0:T(8,128)(2,1)},...) custom-call(s32[3]{0:T(128)} %pad_add_fusion.where_ref, bf16[512,768]{1,0:T(8,128)(2,1)} %get-tuple-element.143.nf_own_ref, ...), custom_call_target="tpu_custom_call" | custom-call | flops 173946175488 | bytes 320864256 | tf_op jit(solution)/shard_map/ffn_second/pallas_call | solution.py:900
  200.1 1.7 collective-permute-start.24
  201.8 1.2 collective-permute-start.25
  203.0 30.7 %attn_backward.1 = (bf16[8,2,128,768]{3,2,1,0:T(8,128)(2,1)}, bf16[4,96,768]{2,1,0:T(8,128)(2,1)}, bf16[4,96,768]{2,1,0:T(8,128)(2,1)}, f32[1,768]{1,0:T(1,128)}, f32[3,2048]{1,0:T(4,128)}) custom-call(s32[4]{0:T(128)} %get-tuple-element.119.lens_ref, s32[3]{0:T(128)} %pad_add_fusion.where_ref, bf16[8,2,128,768]{3,2,1,0:T(8,128)(2,1)} %copy-done.1, ...), custom_call_target="tpu_custom_call" | custom-call | flops 473520144384 | bytes 188743680 | tf_op jit(solution)/shard_map/attn_backward/pallas_call | solution.py:525
  233.7 1.3 fusion.2
  235.6 3.2 by_chip.1
  239.2 4.3 %second_halves.1 = (bf16[4,2,48,768]{3,2,1,0:T(8,128)(2,1)}, bf16[4,2,48,768]{3,2,1,0:T(8,128)(2,1)}, bf16[4,96,768]{2,1,0:T(8,128)(2,1)}, bf16[4,96,768]{2,1,0:T(8,128)(2,1)}) custom-call(s32[3]{0:T(128)} %pad_add_fusion.where_ref, bf16[4,2,96,768]{3,2,1,0:T(8,128)(2,1)} %get-tuple-element.176.u_keep_ref, ...), custom_call_target="tpu_custom_call" | custom-call | bytes 84000000 | tf_op jit(solution)/shard_map/second_halves/pallas_call | solution.py:952
  243.6 1.4 collective-permute-start.28
  247.3 1.1 collective-permute-start.33
  248.6 18.1 %collective-permute-done.33.refs_10_ = bf16[192,768]{1,0:T(8,128)(2,1)S(1)} collective-permute-done((bf16[192,768]{1,0:T(8,128)(2,1)S(1)}, bf16[192,768]{1,0:T(8,128)(2,1)S(1)}, u32[]{:S(2)}, u32[]{:S(2)}) %collective-permute-start.33) | collective-permute-done | bytes 294944 | tf_op jit(solution)/shard_map/ppermute | solution.py:1226
  268.1 3.9 %by_plane.1 = (bf16[304,768]{1,0:T(8,128)(2,1)}, bf16[304,768]{1,0:T(8,128)(2,1)}, bf16[304,768]{1,0:T(8,128)(2,1)}, bf16[304,768]{1,0:T(8,128)(2,1)}, bf16[96,768]{1,0:T(8,128)(2,1)}) custom-call(s32[3]{0:T(128)} %pad_add_fusion.where_ref, bf16[4,2,48,768]{3,2,1,0:T(8,128)(2,1)} %get-tuple-element.180.refs_0_, bf16[4,2,48,768]{3,2,1,0:T(8,128)(2,1)} %copy-done.5, ...), custom_call_target="tpu_custom_call" | custom-call | bytes 72000000 | tf_op jit(solution)/shard_map/by_plane/pallas_call | solution.py:1051
  272.1 4.0 %all-to-all-start.4 = ((bf16[8,2,128,768]{3,2,1,0:T(8,128)(2,1)}), bf16[8,2,128,768]{3,2,1,0:T(8,128)(2,1)S(1)}, u32[]{:S(2)}, u32[]{:S(2)}) async-start(bf16[8,2,128,768]{3,2,1,0:T(8,128)(2,1)} %get-tuple-element.203), calls=%async_computation.4 | async-start | bytes 6291456 | tf_op jit(solution)/shard_map/all_to_all | solution.py:1381
  276.1 3.8 %collective-permute-start.36 = (bf16[304,768]{1,0:T(8,128)(2,1)}, bf16[304,768]{1,0:T(8,128)(2,1)S(1)}, u32[]{:S(2)}, u32[]{:S(2)}) collective-permute-start(bf16[304,768]{1,0:T(8,128)(2,1)} %get-tuple-element.208), channel_id=1, source_target_pairs={{0,2},{1,3},{2,0},{3,1},{4,6},{5,7},{6,4},{7,5},{8,10},{9,11},{10,... | collective-permute-start | bytes 1400840 | tf_op jit(solution)/shard_map/ppermute | solution.py:1231
  280.7 4.7 %finish_out.1 = bf16[4,128,768]{2,1,0:T(8,128)(2,1)} custom-call(s32[4]{0:T(128)} %get-tuple-element.118.order_ref, s32[4]{0:T(128)} %get-tuple-element.119.lens_ref, s32[1]{0:T(128)} %bitcast.3.start_ref, f32[512,768]{1,0:T(8,128)} %get-tuple-element.142.res_ref, f32[512,768]{1,0:T(8,128)} %get-tuple-element.151.own_ref, bf16[512,768]{1,0:T(8,128)(2,1)} %copy-done.4), custom_call_target="tpu_custom_call" | custom-call | bytes 72000000 | tf_op jit(solution)/shard_map/finish_out/pallas_call | solution.py:1170
  285.4 3.1 collective-permute-done.35
  288.5 27.7 %collective-permute-done.36 = bf16[304,768]{1,0:T(8,128)(2,1)S(1)} collective-permute-done((bf16[304,768]{1,0:T(8,128)(2,1)}, bf16[304,768]{1,0:T(8,128)(2,1)S(1)}, u32[]{:S(2)}, u32[]{:S(2)}) %collective-permute-start.36) | collective-permute-done | bytes 466976 | tf_op jit(solution)/shard_map/ppermute | solution.py:1231
  316.3 3.3 collective-permute-done.37
  320.8 2.9 collective-permute-start.40
  324.0 13.2 %collective-permute-done.40.refs_3_ = bf16[400,768]{1,0:T(8,128)(2,1)} collective-permute-done((bf16[400,768]{1,0:T(8,128)(2,1)}, bf16[400,768]{1,0:T(8,128)(2,1)}, u32[]{:S(2)}, u32[]{:S(2)}) %collective-permute-start.40) | collective-permute-done | bytes 614432 | tf_op jit(solution)/shard_map/ppermute | solution.py:1226
  337.1 3.0 collective-permute-start.44
  340.1 10.2 %collective-permute-done.38.refs_1_ = bf16[400,768]{1,0:T(8,128)(2,1)} collective-permute-done((bf16[400,768]{1,0:T(8,128)(2,1)}, bf16[400,768]{1,0:T(8,128)(2,1)}, u32[]{:S(2)}, u32[]{:S(2)}) %collective-permute-start.38) | collective-permute-done | bytes 614432 | tf_op jit(solution)/shard_map/ppermute | solution.py:1226
  350.3 1.9 collective-permute-start.42
  352.3 1.6 copy-done
  353.9 5.4 %finish_tokens.1 = f32[4,128,768]{2,1,0:T(8,128)} custom-call(s32[4]{0:T(128)} %get-tuple-element.118.order_ref, bf16[4,4,128,768]{3,2,1,0:T(8,128)(2,1)} %bitcast.11, bf16[512,768]{1,0:T(8,128)(2,1)} %get-tuple-element.120.tok_ref, f32[512,768]{1,0:T(8,128)} %get-tuple-element.204.dres_ref, f32[1,768]{1,0:T(1,128)} %reshape.130.gain_ref), custom_call_target="tpu_custom_call" | custom-call | bytes 120000000 | tf_op jit(solution)/shard_map/finish_tokens/pallas_call | solution.py:1201
  359.4 6.8 %unpack.1 = (f32[192,3072]{1,0:T(8,128)}, f32[192,3072]{1,0:T(8,128)}, f32[4,2,96,768]{3,2,1,0:T(8,128)}, f32[192,768]{1,0:T(8,128)}, f32[192,768]{1,0:T(8,128)}...) custom-call(s32[3]{0:T(128)} %pad_add_fusion.where_ref, ...), custom_call_target="tpu_custom_call" | custom-call | bytes 288000000 | tf_op jit(solution)/shard_map/unpack/pallas_call | solution.py:1129
  366.9 1.4 fusion.16
  (152 shorter events, 22.3 us)
Async XLA Ops:
  10.5 15.3 %copy-start.17 = (s32[2047]{0:T(1024)S(1)}, s32[2047]{0:T(1024)}, u32[]{:S(2)}) copy-start(s32[2047]{0:T(1024)} %param.17) | copy-start | bytes 24568
  10.5 38.9 %all-to-all-start = ((bf16[8,2,128,768]{3,2,1,0:T(8,128)(2,1)}), bf16[8,2,128,768]{3,2,1,0:T(8,128)(2,1)S(1)}, u32[]{:S(2)}, u32[]{:S(2)}) async-start(bf16[8,2,128,768]{3,2,1,0:T(8,128)(2,1)} %bitcast.12), calls=%async_computation | async-start | bytes 6291456 | tf_op jit(solution)/shard_map/all_to_all | solution.py:1283
  15.0 9.5 %collective-permute-start = (bf16[208,768]{1,0:T(8,128)(2,1)}, bf16[208,768]{1,0:T(8,128)(2,1)}, u32[]{:S(2)}, u32[]{:S(2)}) collective-permute-start(bf16[208,768]{1,0:T(8,128)(2,1)} %get-tuple-element.116), channel_id=1, source_target_pairs={{0,1},{1,2},{2,3},{3,0},{4,5},{5,6},{6,7},{7,4},{8,9},{9,10},{10,1... | collective-permute-start | bytes 958472 | tf_op jit(solution)/shard_map/ppermute | solution.py:1231
  16.3 16.4 %collective-permute-start.2 = (bf16[208,768]{1,0:T(8,128)(2,1)}, bf16[208,768]{1,0:T(8,128)(2,1)}, u32[]{:S(2)}, u32[]{:S(2)}) collective-permute-start(bf16[208,768]{1,0:T(8,128)(2,1)} %get-tuple-element.116), channel_id=1, source_target_pairs={{0,3},{1,0},{2,1},{3,2},{4,7},{5,4},{6,5},{7,6},{8,11},{9,8},{10,9... | collective-permute-start | bytes 958472 | tf_op jit(solution)/shard_map/ppermute | solution.py:1231
  24.4 13.6 %collective-permute-start.1 = (bf16[208,768]{1,0:T(8,128)(2,1)}, bf16[208,768]{1,0:T(8,128)(2,1)S(1)}, u32[]{:S(2)}, u32[]{:S(2)}) collective-permute-start(bf16[208,768]{1,0:T(8,128)(2,1)} %collective-permute-done.w1_ref.a1_ref), channel_id=1, source_target_pairs={{0,1},{1,2},{2,3},{3,0},{4,5},{5,6},{6,7},{7,4},{8,9},{9,10},{10,1... | collective-permute-start | bytes 958472 | tf_op jit(solution)/shard_map/ppermute | solution.py:1231
  26.2 39.5 %copy-start.2 = (pred[2047,32]{1,0:T(8,128)(4,1)}, pred[2047,32]{1,0:T(8,128)(4,1)S(1)}, u32[]{:S(2)}) copy-start(pred[2047,32]{1,0:T(8,128)(4,1)S(1)} %iota_compare_fusion) | copy-start | bytes 196516
  32.7 33.0 %collective-permute-start.6 = (bf16[288,768]{1,0:T(8,128)(2,1)}, bf16[288,768]{1,0:T(8,128)(2,1)}, u32[]{:S(2)}, u32[]{:S(2)}) collective-permute-start(bf16[288,768]{1,0:T(8,128)(2,1)} %get-tuple-element.130), channel_id=1, source_target_pairs={{0,1},{1,2},{2,3},{3,0},{4,5},{5,6},{6,7},{7,4},{8,9},{9,10},{10,1... | collective-permute-start | bytes 1327112 | tf_op jit(solution)/shard_map/ppermute | solution.py:1231
  32.7 56.1 %collective-permute-start.8 = (bf16[288,768]{1,0:T(8,128)(2,1)}, bf16[288,768]{1,0:T(8,128)(2,1)}, u32[]{:S(2)}, u32[]{:S(2)}) collective-permute-start(bf16[288,768]{1,0:T(8,128)(2,1)} %get-tuple-element.130), channel_id=1, source_target_pairs={{0,3},{1,0},{2,1},{3,2},{4,7},{5,4},{6,5},{7,6},{8,11},{9,8},{10,9... | collective-permute-start | bytes 1327112 | tf_op jit(solution)/shard_map/ppermute | solution.py:1231
  35.5 8.6 %collective-permute-start.3 = (bf16[208,768]{1,0:T(8,128)(2,1)}, bf16[208,768]{1,0:T(8,128)(2,1)}, u32[]{:S(2)}, u32[]{:S(2)}) collective-permute-start(bf16[208,768]{1,0:T(8,128)(2,1)} %collective-permute-done.w1_ref.a1_ref), channel_id=1, source_target_pairs={{0,4},{4,0},{8,12},{12,8},{16,20},{20,16},{24,28},{28,24},{1,5},{5... | collective-permute-start | bytes 958472 | tf_op jit(solution)/shard_map/ppermute | solution.py:1226
  37.2 9.0 %collective-permute-start.5 = (bf16[208,768]{1,0:T(8,128)(2,1)}, bf16[208,768]{1,0:T(8,128)(2,1)}, u32[]{:S(2)}, u32[]{:S(2)}) collective-permute-start(bf16[208,768]{1,0:T(8,128)(2,1)} %collective-permute-done.2.w3_ref.a3_ref), channel_id=1, source_target_pairs={{0,4},{4,0},{8,12},{12,8},{16,20},{20,16},{24,28},{28,24},{1,5},{5... | collective-permute-start | bytes 958472 | tf_op jit(solution)/shard_map/ppermute | solution.py:1226
  38.9 7.9 %collective-permute-start.4 = (bf16[208,768]{1,0:T(8,128)(2,1)}, bf16[208,768]{1,0:T(8,128)(2,1)}, u32[]{:S(2)}, u32[]{:S(2)}) collective-permute-start(bf16[208,768]{1,0:T(8,128)(2,1)} %copy-done.20), channel_id=1, source_target_pairs={{0,4},{4,0},{8,12},{12,8},{16,20},{20,16},{24,28},{28,24},{1,5},{5... | collective-permute-start | bytes 958472 | tf_op jit(solution)/shard_map/ppermute | solution.py:1226
  44.1 22.6 %collective-permute-start.7 = (bf16[288,768]{1,0:T(8,128)(2,1)}, bf16[288,768]{1,0:T(8,128)(2,1)}, u32[]{:S(2)}, u32[]{:S(2)}) collective-permute-start(bf16[288,768]{1,0:T(8,128)(2,1)} %get-tuple-element.132), channel_id=1, source_target_pairs={{0,1},{1,2},{2,3},{3,0},{4,5},{5,6},{6,7},{7,4},{8,9},{9,10},{10,1... | collective-permute-start | bytes 1327112 | tf_op jit(solution)/shard_map/ppermute | solution.py:1231
  46.2 44.0 %collective-permute-start.9 = (bf16[288,768]{1,0:T(8,128)(2,1)}, bf16[288,768]{1,0:T(8,128)(2,1)}, u32[]{:S(2)}, u32[]{:S(2)}) collective-permute-start(bf16[288,768]{1,0:T(8,128)(2,1)} %get-tuple-element.132), channel_id=1, source_target_pairs={{0,3},{1,0},{2,1},{3,2},{4,7},{5,4},{6,5},{7,6},{8,11},{9,8},{10,9... | collective-permute-start | bytes 1327112 | tf_op jit(solution)/shard_map/ppermute | solution.py:1231
  66.7 24.8 %collective-permute-start.11 = (bf16[288,768]{1,0:T(8,128)(2,1)}, bf16[288,768]{1,0:T(8,128)(2,1)S(1)}, u32[]{:S(2)}, u32[]{:S(2)}) collective-permute-start(bf16[288,768]{1,0:T(8,128)(2,1)} %collective-permute-done.6.x1), channel_id=1, source_target_pairs={{0,1},{1,2},{2,3},{3,0},{4,5},{5,6},{6,7},{7,4},{8,9},{9,10},{10,1... | collective-permute-start | bytes 1327112 | tf_op jit(solution)/shard_map/ppermute | solution.py:1231
  68.3 27.9 %collective-permute-start.10 = (bf16[288,768]{1,0:T(8,128)(2,1)}, bf16[288,768]{1,0:T(8,128)(2,1)S(1)}, u32[]{:S(2)}, u32[]{:S(2)}) collective-permute-start(bf16[288,768]{1,0:T(8,128)(2,1)} %collective-permute-done.6.x1), channel_id=1, source_target_pairs={{0,8},{4,12},{8,0},{12,4},{16,24},{20,28},{24,16},{28,20},{1,9},{5... | collective-permute-start | bytes 1327112 | tf_op jit(solution)/shard_map/ppermute | solution.py:1226
  69.3 20.9 %all-to-all-start.1 = ((bf16[8,1,192,128]{3,2,1,0:T(8,128)(2,1)}), bf16[8,1,192,128]{3,2,1,0:T(8,128)(2,1)S(1)}, u32[]{:S(2)}, u32[]{:S(2)}) async-start(bf16[8,1,192,128]{3,2,1,0:T(8,128)(2,1)} %get-tuple-element.134), calls=%async_computation.1 | async-start | bytes 786432 | tf_op jit(solution)/shard_map/all_to_all | solution.py:1312
  74.8 20.4 %collective-permute-start.15 = (bf16[288,768]{1,0:T(8,128)(2,1)}, bf16[288,768]{1,0:T(8,128)(2,1)S(1)}, u32[]{:S(2)}, u32[]{:S(2)}) collective-permute-start(bf16[288,768]{1,0:T(8,128)(2,1)} %collective-permute-done.7.y1), channel_id=1, source_target_pairs={{0,1},{1,2},{2,3},{3,0},{4,5},{5,6},{6,7},{7,4},{8,9},{9,10},{10,1... | collective-permute-start | bytes 1327112 | tf_op jit(solution)/shard_map/ppermute | solution.py:1231
  88.8 18.6 %collective-permute-start.14 = (bf16[288,768]{1,0:T(8,128)(2,1)}, bf16[288,768]{1,0:T(8,128)(2,1)S(1)}, u32[]{:S(2)}, u32[]{:S(2)}) collective-permute-start(bf16[288,768]{1,0:T(8,128)(2,1)} %collective-permute-done.7.y1), channel_id=1, source_target_pairs={{0,16},{4,20},{8,24},{12,28},{16,0},{20,4},{24,8},{28,12},{1,17},{... | collective-permute-start | bytes 1327112 | tf_op jit(solution)/shard_map/ppermute | solution.py:1226
  90.2 30.3 %copy-start.9 = (bf16[8,1,192,128]{3,2,1,0:T(8,128)(2,1)}, bf16[8,1,192,128]{3,2,1,0:T(8,128)(2,1)S(1)}, u32[]{:S(2)}) copy-start(bf16[8,1,192,128]{3,2,1,0:T(8,128)(2,1)S(1)} %all-to-all-done.1.attn0_ref) | copy-start | bytes 1179652
  90.2 30.2 %collective-permute-start.13 = (bf16[288,768]{1,0:T(8,128)(2,1)}, bf16[288,768]{1,0:T(8,128)(2,1)S(1)}, u32[]{:S(2)}, u32[]{:S(2)}) collective-permute-start(bf16[288,768]{1,0:T(8,128)(2,1)} %collective-permute-done.8.x3), channel_id=1, source_target_pairs={{0,8},{4,12},{8,0},{12,4},{16,24},{20,28},{24,16},{28,20},{1,9},{5... | collective-permute-start | bytes 1327112 | tf_op jit(solution)/shard_map/ppermute | solution.py:1226
  91.5 34.8 %copy-start.26 = (bf16[288,768]{1,0:T(8,128)(2,1)}, bf16[288,768]{1,0:T(8,128)(2,1)S(1)}, u32[]{:S(2)}) copy-start(bf16[288,768]{1,0:T(8,128)(2,1)S(1)} %collective-permute-done.11.x2) | copy-start | bytes 1327108
  91.5 28.9 %collective-permute-start.17 = (bf16[288,768]{1,0:T(8,128)(2,1)}, bf16[288,768]{1,0:T(8,128)(2,1)}, u32[]{:S(2)}, u32[]{:S(2)}) collective-permute-start(bf16[288,768]{1,0:T(8,128)(2,1)} %collective-permute-done.9.y3), channel_id=1, source_target_pairs={{0,16},{4,20},{8,24},{12,28},{16,0},{20,4},{24,8},{28,12},{1,17},{... | collective-permute-start | bytes 1327112 | tf_op jit(solution)/shard_map/ppermute | solution.py:1226
  95.2 25.3 %copy-start.28 = (bf16[288,768]{1,0:T(8,128)(2,1)}, bf16[288,768]{1,0:T(8,128)(2,1)S(1)}, u32[]{:S(2)}) copy-start(bf16[288,768]{1,0:T(8,128)(2,1)S(1)} %collective-permute-done.15.y2) | copy-start | bytes 1327108
  95.2 25.2 %collective-permute-start.12 = (bf16[288,768]{1,0:T(8,128)(2,1)S(1)}, bf16[288,768]{1,0:T(8,128)(2,1)}, u32[]{:S(2)}, u32[]{:S(2)}) collective-permute-start(bf16[288,768]{1,0:T(8,128)(2,1)S(1)} %collective-permute-done.11.x2), channel_id=1, source_target_pairs={{0,8},{4,12},{8,0},{12,4},{16,24},{20,28},{24,16},{28,20},{1,9},{5... | collective-permute-start | bytes 1327112 | tf_op jit(solution)/shard_map/ppermute | solution.py:1226
  96.2 30.1 %copy-start.27 = (bf16[288,768]{1,0:T(8,128)(2,1)}, bf16[288,768]{1,0:T(8,128)(2,1)S(1)}, u32[]{:S(2)}) copy-start(bf16[288,768]{1,0:T(8,128)(2,1)S(1)} %collective-permute-done.10.sx1) | copy-start | bytes 1327108
  96.2 24.3 %collective-permute-start.16 = (bf16[288,768]{1,0:T(8,128)(2,1)S(1)}, bf16[288,768]{1,0:T(8,128)(2,1)}, u32[]{:S(2)}, u32[]{:S(2)}) collective-permute-start(bf16[288,768]{1,0:T(8,128)(2,1)S(1)} %collective-permute-done.15.y2), channel_id=1, source_target_pairs={{0,16},{4,20},{8,24},{12,28},{16,0},{20,4},{24,8},{28,12},{1,17},{... | collective-permute-start | bytes 1327112 | tf_op jit(solution)/shard_map/ppermute | solution.py:1226
  97.4 23.1 %all-to-all-start.2 = ((bf16[8,1,192,128]{3,2,1,0:T(8,128)(2,1)}), bf16[8,1,192,128]{3,2,1,0:T(8,128)(2,1)S(1)}, u32[]{:S(2)}, u32[]{:S(2)}) async-start(bf16[8,1,192,128]{3,2,1,0:T(8,128)(2,1)} %get-tuple-element.138), calls=%async_computation.2 | async-start | bytes 786432 | tf_op jit(solution)/shard_map/all_to_all | solution.py:1316
  107.4 13.1 %copy-start.29 = (bf16[288,768]{1,0:T(8,128)(2,1)}, bf16[288,768]{1,0:T(8,128)(2,1)S(1)}, u32[]{:S(2)}) copy-start(bf16[288,768]{1,0:T(8,128)(2,1)S(1)} %collective-permute-done.14.sy1) | copy-start | bytes 1327108
  126.2 2.4 collective-permute-start.19
  126.5 3.5 collective-permute-start.18
  156.6 14.6 %collective-permute-start.23 = (bf16[512,768]{1,0:T(8,128)(2,1)}, bf16[512,768]{1,0:T(8,128)(2,1)S(1)}, u32[]{:S(2)}, u32[]{:S(2)}) collective-permute-start(bf16[512,768]{1,0:T(8,128)(2,1)} %get-tuple-element.158), channel_id=1, source_target_pairs={{0,4},{4,0},{8,12},{12,8},{16,20},{20,16},{24,28},{28,24},{1,5},{5... | collective-permute-start | bytes 2359304 | tf_op jit(solution)/shard_map/ppermute | solution.py:1226
  156.8 43.3 %collective-permute-start.21 = (bf16[2,192,768]{2,1,0:T(8,128)(2,1)}, bf16[2,192,768]{2,1,0:T(8,128)(2,1)}, u32[]{:S(2)}, u32[]{:S(2)}) collective-permute-start(bf16[2,192,768]{2,1,0:T(8,128)(2,1)} %get-tuple-element.153), channel_id=1, source_target_pairs={{0,1},{1,2},{2,3},{3,0},{4,5},{5,6},{6,7},{7,4},{8,9},{9,10},{10,1... | collective-permute-start | bytes 1769480 | tf_op jit(solution)/shard_map/ppermute | solution.py:1231
  158.8 41.3 %collective-permute-start.22 = (bf16[2,192,768]{2,1,0:T(8,128)(2,1)}, bf16[2,192,768]{2,1,0:T(8,128)(2,1)}, u32[]{:S(2)}, u32[]{:S(2)}) collective-permute-start(bf16[2,192,768]{2,1,0:T(8,128)(2,1)} %get-tuple-element.154), channel_id=1, source_target_pairs={{0,3},{1,0},{2,1},{3,2},{4,7},{5,4},{6,5},{7,6},{8,11},{9,8},{10,9... | collective-permute-start | bytes 1769480 | tf_op jit(solution)/shard_map/ppermute | solution.py:1231
  169.7 65.9 %collective-permute-start.26 = (bf16[2,192,768]{2,1,0:T(8,128)(2,1)}, bf16[2,192,768]{2,1,0:T(8,128)(2,1)}, u32[]{:S(2)}, u32[]{:S(2)}) collective-permute-start(bf16[2,192,768]{2,1,0:T(8,128)(2,1)} %get-tuple-element.173), channel_id=1, source_target_pairs={{0,2},{1,3},{2,0},{3,1},{4,6},{5,7},{6,4},{7,5},{8,10},{9,11},{10,... | collective-permute-start | bytes 1769480 | tf_op jit(solution)/shard_map/ppermute | solution.py:1231
  178.6 21.5 %all-to-all-start.3 = ((bf16[8,2,192,128]{3,2,1,0:T(8,128)(2,1)}), bf16[8,2,192,128]{3,2,1,0:T(8,128)(2,1)}, u32[]{:S(2)}, u32[]{:S(2)}) async-start(bf16[8,2,192,128]{3,2,1,0:T(8,128)(2,1)} %get-tuple-element.160), calls=%async_computation.3 | async-start | bytes 1572864 | tf_op jit(solution)/shard_map/all_to_all | solution.py:1335
  183.4 16.0 %copy-start.19 = (f32[1,768]{1,0:T(1,128)S(1)}, f32[1,768]{1,0:T(1,128)}, u32[]{:S(2)}) copy-start(f32[1,768]{1,0:T(1,128)} %get-tuple-element.187) | copy-start | bytes 9220
  199.2 36.4 %collective-permute-start.31 = (bf16[4,96,768]{2,1,0:T(8,128)(2,1)}, bf16[4,96,768]{2,1,0:T(8,128)(2,1)}, u32[]{:S(2)}, u32[]{:S(2)}) collective-permute-start(bf16[4,96,768]{2,1,0:T(8,128)(2,1)} %get-tuple-element.194), channel_id=1, source_target_pairs={{0,4},{4,0},{8,12},{12,8},{16,20},{20,16},{24,28},{28,24},{1,5},{5... | collective-permute-start | bytes 1769480 | tf_op jit(solution)/shard_map/ppermute | solution.py:1226
  200.1 35.4 %collective-permute-start.24 = (bf16[4,2,96,768]{3,2,1,0:T(8,128)(2,1)}, bf16[4,2,96,768]{3,2,1,0:T(8,128)(2,1)}, u32[]{:S(2)}, u32[]{:S(2)}) collective-permute-start(bf16[4,2,96,768]{3,2,1,0:T(8,128)(2,1)} %get-tuple-element.161), channel_id=1, source_target_pairs={{0,8},{4,12},{8,0},{12,4},{16,24},{20,28},{24,16},{28,20},{1,9},{5... | collective-permute-start | bytes 3538952 | tf_op jit(solution)/shard_map/ppermute | solution.py:1226
  201.8 33.8 %collective-permute-start.25 = (bf16[4,192,768]{2,1,0:T(8,128)(2,1)}, bf16[4,192,768]{2,1,0:T(8,128)(2,1)}, u32[]{:S(2)}, u32[]{:S(2)}) collective-permute-start(bf16[4,192,768]{2,1,0:T(8,128)(2,1)} %get-tuple-element.162), channel_id=1, source_target_pairs={{0,16},{4,20},{8,24},{12,28},{16,0},{20,4},{24,8},{28,12},{1,17},{... | collective-permute-start | bytes 3538952 | tf_op jit(solution)/shard_map/ppermute | solution.py:1226
  203.0 30.7 %copy-start.3 = (pred[2047,32]{1,0:T(8,128)(4,1)S(1)}, pred[2047,32]{1,0:T(8,128)(4,1)}, u32[]{:S(2)}) copy-start(pred[2047,32]{1,0:T(8,128)(4,1)} %copy-done.2) | copy-start | bytes 196516
  238.8 9.6 %collective-permute-start.32 = (bf16[192,768]{1,0:T(8,128)(2,1)}, bf16[192,768]{1,0:T(8,128)(2,1)S(1)}, u32[]{:S(2)}, u32[]{:S(2)}) collective-permute-start(bf16[192,768]{1,0:T(8,128)(2,1)} %get-tuple-element.196), channel_id=1, source_target_pairs={{0,8},{4,12},{8,0},{12,4},{16,24},{20,28},{24,16},{28,20},{1,9},{5... | collective-permute-start | bytes 884744 | tf_op jit(solution)/shard_map/ppermute | solution.py:1226
  239.2 9.2 %copy-start.31 = (bf16[192,768]{1,0:T(8,128)(2,1)S(1)}, bf16[192,768]{1,0:T(8,128)(2,1)}, u32[]{:S(2)}) copy-start(bf16[192,768]{1,0:T(8,128)(2,1)} %get-tuple-element.198) | copy-start | bytes 884740
  243.5 23.3 %collective-permute-start.27 = (bf16[4,2,48,768]{3,2,1,0:T(8,128)(2,1)}, bf16[4,2,48,768]{3,2,1,0:T(8,128)(2,1)S(1)}, u32[]{:S(2)}, u32[]{:S(2)}) collective-permute-start(bf16[4,2,48,768]{3,2,1,0:T(8,128)(2,1)} %get-tuple-element.181), channel_id=1, source_target_pairs={{0,16},{4,20},{8,24},{12,28},{16,0},{20,4},{24,8},{28,12},{1,17},{... | collective-permute-start | bytes 1769480 | tf_op jit(solution)/shard_map/ppermute | solution.py:1226
  243.6 23.2 %collective-permute-start.28 = (bf16[4,96,768]{2,1,0:T(8,128)(2,1)}, bf16[4,96,768]{2,1,0:T(8,128)(2,1)S(1)}, u32[]{:S(2)}, u32[]{:S(2)}) collective-permute-start(bf16[4,96,768]{2,1,0:T(8,128)(2,1)} %get-tuple-element.183), channel_id=1, source_target_pairs={{0,8},{4,12},{8,0},{12,4},{16,24},{20,28},{24,16},{28,20},{1,9},{5... | collective-permute-start | bytes 1769480 | tf_op jit(solution)/shard_map/ppermute | solution.py:1226
  245.0 21.8 %collective-permute-start.29 = (bf16[4,96,768]{2,1,0:T(8,128)(2,1)S(1)}, bf16[4,96,768]{2,1,0:T(8,128)(2,1)S(1)}, u32[]{:S(2)}, u32[]{:S(2)}) collective-permute-start(bf16[4,96,768]{2,1,0:T(8,128)(2,1)S(1)} %copy-done.25), channel_id=1, source_target_pairs={{0,4},{4,0},{8,12},{12,8},{16,20},{20,16},{24,28},{28,24},{1,5},{5... | collective-permute-start | bytes 1769480 | tf_op jit(solution)/shard_map/ppermute | solution.py:1226
  245.8 1.4 collective-permute-start.30
  247.3 19.5 %copy-start.15 = (bf16[4,16,768]{2,1,0:T(8,128)(2,1)}, bf16[4,16,768]{2,1,0:T(8,128)(2,1)S(1)}, u32[]{:S(2)}) copy-start(bf16[4,16,768]{2,1,0:T(8,128)(2,1)S(1)} %collective-permute-done.30.refs_7_) | copy-start | bytes 294916
  247.3 19.5 %collective-permute-start.33 = (bf16[192,768]{1,0:T(8,128)(2,1)S(1)}, bf16[192,768]{1,0:T(8,128)(2,1)S(1)}, u32[]{:S(2)}, u32[]{:S(2)}) collective-permute-start(bf16[192,768]{1,0:T(8,128)(2,1)S(1)} %copy-done.32), channel_id=1, source_target_pairs={{0,16},{4,20},{8,24},{12,28},{16,0},{20,4},{24,8},{28,12},{1,17},{... | collective-permute-start | bytes 884744 | tf_op jit(solution)/shard_map/ppermute | solution.py:1226
  248.4 18.5 %copy-start.11 = (bf16[192,768]{1,0:T(8,128)(2,1)}, bf16[192,768]{1,0:T(8,128)(2,1)S(1)}, u32[]{:S(2)}) copy-start(bf16[192,768]{1,0:T(8,128)(2,1)S(1)} %collective-permute-done.32.refs_9_) | copy-start | bytes 884740
  248.4 18.4 %collective-permute-start.34 = (bf16[192,768]{1,0:T(8,128)(2,1)S(1)}, bf16[192,768]{1,0:T(8,128)(2,1)S(1)}, u32[]{:S(2)}, u32[]{:S(2)}) collective-permute-start(bf16[192,768]{1,0:T(8,128)(2,1)S(1)} %copy-done.31), channel_id=1, source_target_pairs={{0,24},{4,28},{8,16},{12,20},{16,8},{20,12},{24,0},{28,4},{1,25},{... | collective-permute-start | bytes 884744 | tf_op jit(solution)/shard_map/ppermute | solution.py:1226
  272.1 80.2 %all-to-all-start.4 = ((bf16[8,2,128,768]{3,2,1,0:T(8,128)(2,1)}), bf16[8,2,128,768]{3,2,1,0:T(8,128)(2,1)S(1)}, u32[]{:S(2)}, u32[]{:S(2)}) async-start(bf16[8,2,128,768]{3,2,1,0:T(8,128)(2,1)} %get-tuple-element.203), calls=%async_computation.4 | async-start | bytes 6291456 | tf_op jit(solution)/shard_map/all_to_all | solution.py:1381
  276.0 3.8 %collective-permute-start.20 = (bf16[512,768]{1,0:T(8,128)(2,1)}, bf16[512,768]{1,0:T(8,128)(2,1)S(1)}, u32[]{:S(2)}, u32[]{:S(2)}) collective-permute-start(bf16[512,768]{1,0:T(8,128)(2,1)} %get-tuple-element.152), channel_id=1, source_target_pairs={{0,4},{4,0},{8,12},{12,8},{16,20},{20,16},{24,28},{28,24},{1,5},{5... | collective-permute-start | bytes 2359304 | tf_op jit(solution)/shard_map/ppermute | solution.py:1226
  276.0 12.5 %collective-permute-start.35 = (bf16[304,768]{1,0:T(8,128)(2,1)}, bf16[304,768]{1,0:T(8,128)(2,1)S(1)}, u32[]{:S(2)}, u32[]{:S(2)}) collective-permute-start(bf16[304,768]{1,0:T(8,128)(2,1)} %get-tuple-element.207), channel_id=1, source_target_pairs={{0,1},{1,2},{2,3},{3,0},{4,5},{5,6},{6,7},{7,4},{8,9},{9,10},{10,1... | collective-permute-start | bytes 1400840 | tf_op jit(solution)/shard_map/ppermute | solution.py:1231
  276.1 40.2 %collective-permute-start.36 = (bf16[304,768]{1,0:T(8,128)(2,1)}, bf16[304,768]{1,0:T(8,128)(2,1)S(1)}, u32[]{:S(2)}, u32[]{:S(2)}) collective-permute-start(bf16[304,768]{1,0:T(8,128)(2,1)} %get-tuple-element.208), channel_id=1, source_target_pairs={{0,2},{1,3},{2,0},{3,1},{4,6},{5,7},{6,4},{7,5},{8,10},{9,11},{10,... | collective-permute-start | bytes 1400840 | tf_op jit(solution)/shard_map/ppermute | solution.py:1231
  279.8 39.8 %collective-permute-start.37 = (bf16[304,768]{1,0:T(8,128)(2,1)}, bf16[304,768]{1,0:T(8,128)(2,1)S(1)}, u32[]{:S(2)}, u32[]{:S(2)}) collective-permute-start(bf16[304,768]{1,0:T(8,128)(2,1)} %get-tuple-element.209), channel_id=1, source_target_pairs={{0,3},{1,0},{2,1},{3,2},{4,7},{5,4},{6,5},{7,6},{8,11},{9,8},{10,9... | collective-permute-start | bytes 1400840 | tf_op jit(solution)/shard_map/ppermute | solution.py:1231
  280.7 38.9 %copy-start.8 = (bf16[304,768]{1,0:T(8,128)(2,1)S(1)}, bf16[304,768]{1,0:T(8,128)(2,1)}, u32[]{:S(2)}) copy-start(bf16[304,768]{1,0:T(8,128)(2,1)} %get-tuple-element.206) | copy-start | bytes 1400836
  285.4 34.5 %copy-start.14 = (bf16[96,768]{1,0:T(8,128)(2,1)S(1)}, bf16[96,768]{1,0:T(8,128)(2,1)}, u32[]{:S(2)}) copy-start(bf16[96,768]{1,0:T(8,128)(2,1)} %get-tuple-element.205) | copy-start | bytes 442372
  320.8 16.3 %collective-permute-start.40 = (bf16[400,768]{1,0:T(8,128)(2,1)}, bf16[400,768]{1,0:T(8,128)(2,1)}, u32[]{:S(2)}, u32[]{:S(2)}) collective-permute-start(bf16[400,768]{1,0:T(8,128)(2,1)} %pad_maximum_fusion.refs_0_), channel_id=1, source_target_pairs={{0,24},{4,28},{8,16},{12,20},{16,8},{20,12},{24,0},{28,4},{1,25},{... | collective-permute-start | bytes 1843208 | tf_op jit(solution)/shard_map/ppermute | solution.py:1226
  323.7 26.7 %collective-permute-start.38 = (bf16[400,768]{1,0:T(8,128)(2,1)}, bf16[400,768]{1,0:T(8,128)(2,1)}, u32[]{:S(2)}, u32[]{:S(2)}) collective-permute-start(bf16[400,768]{1,0:T(8,128)(2,1)} %pad_maximum_fusion.refs_0_), channel_id=1, source_target_pairs={{0,8},{4,12},{8,0},{12,4},{16,24},{20,28},{24,16},{28,20},{1,9},{5... | collective-permute-start | bytes 1843208 | tf_op jit(solution)/shard_map/ppermute | solution.py:1226
  324.0 28.3 %collective-permute-start.39 = (bf16[400,768]{1,0:T(8,128)(2,1)}, bf16[400,768]{1,0:T(8,128)(2,1)}, u32[]{:S(2)}, u32[]{:S(2)}) collective-permute-start(bf16[400,768]{1,0:T(8,128)(2,1)} %pad_maximum_fusion.refs_0_), channel_id=1, source_target_pairs={{0,16},{4,20},{8,24},{12,28},{16,0},{20,4},{24,8},{28,12},{1,17},{... | collective-permute-start | bytes 1843208 | tf_op jit(solution)/shard_map/ppermute | solution.py:1226
  337.1 22.2 %collective-permute-start.44 = (bf16[400,768]{1,0:T(8,128)(2,1)}, bf16[400,768]{1,0:T(8,128)(2,1)}, u32[]{:S(2)}, u32[]{:S(2)}) collective-permute-start(bf16[400,768]{1,0:T(8,128)(2,1)} %collective-permute-done.40.refs_3_), channel_id=1, source_target_pairs={{0,4},{4,0},{8,12},{12,8},{16,20},{20,16},{24,28},{28,24},{1,5},{5... | collective-permute-start | bytes 1843208 | tf_op jit(solution)/shard_map/ppermute | solution.py:1226
  340.1 19.2 %collective-permute-start.41 = (bf16[400,768]{1,0:T(8,128)(2,1)}, bf16[400,768]{1,0:T(8,128)(2,1)}, u32[]{:S(2)}, u32[]{:S(2)}) collective-permute-start(bf16[400,768]{1,0:T(8,128)(2,1)} %pad_maximum_fusion.refs_0_), channel_id=1, source_target_pairs={{0,4},{4,0},{8,12},{12,8},{16,20},{20,16},{24,28},{28,24},{1,5},{5... | collective-permute-start | bytes 1843208 | tf_op jit(solution)/shard_map/ppermute | solution.py:1226
  350.3 9.0 %collective-permute-start.42 = (bf16[400,768]{1,0:T(8,128)(2,1)}, bf16[400,768]{1,0:T(8,128)(2,1)}, u32[]{:S(2)}, u32[]{:S(2)}) collective-permute-start(bf16[400,768]{1,0:T(8,128)(2,1)} %collective-permute-done.38.refs_1_), channel_id=1, source_target_pairs={{0,4},{4,0},{8,12},{12,8},{16,20},{20,16},{24,28},{28,24},{1,5},{5... | collective-permute-start | bytes 1843208 | tf_op jit(solution)/shard_map/ppermute | solution.py:1226
  352.3 7.1 %collective-permute-start.43 = (bf16[400,768]{1,0:T(8,128)(2,1)}, bf16[400,768]{1,0:T(8,128)(2,1)}, u32[]{:S(2)}, u32[]{:S(2)}) collective-permute-start(bf16[400,768]{1,0:T(8,128)(2,1)} %collective-permute-done.39.refs_2_), channel_id=1, source_target_pairs={{0,4},{4,0},{8,12},{12,8},{16,20},{20,16},{24,28},{28,24},{1,5},{5... | collective-permute-start | bytes 1843208 | tf_op jit(solution)/shard_map/ppermute | solution.py:1226
  (19 other events, 50.3 us)
